TPU v7x, 512 devices: a whole 4x4x16 slice. The times are simulated.
512 devices in a mesh: section: 4 (over y), dp: 16 (over z), tensor: 8 (over x, core).
Axes of the slice: x: 4, y: 4, z: 16, core: 2. Of those that a mesh axis runs over, the one named last changes fastest.
Arguments:
- hidden: bfloat16 [4, 2048, 14336], P('section', 'dp', 'tensor'), may hold values from -6 to 6
- residual_in: bfloat16 [2048, 4096], P('dp', 'tensor'), may hold values from -6 to 6
- weights: bfloat16 [4, 8, 32, 7, 128, 128], P('section', 'tensor', 'dp'), may hold values from -0.0625 to 0.0625
- kept: int32 [4, 8, 32, 7], P('section', 'tensor'), may hold values from 0 to 13, as said below
- cotangent: bfloat16 [2048, 4096], P('dp', 'tensor'), may hold values from -0.125 to 0.125
- norm_gain: float32 [4096], P('tensor'), may hold values from 0.1 to 1.9
Outputs:
- section_out: bfloat16 [4, 2048, 4096], P('section', 'dp', 'tensor')
- weight_grad: bfloat16 [4, 8, 32, 7, 128, 128], P('section', 'tensor', 'dp')
Inputs may be any that keep to these rules, and one draw needn't show every extreme that they name: `kept`: for every section, tensor shard and column block, the 7 entries are distinct hidden blocks of that shard, in increasing order.
All inputs are finite; a program needn't handle non-finite values.
Results may differ from a plain program's by a relative error of at most 0.02.
Values may be sent and summed in bfloat16 or wider, within the bound.
No kernel may reach another device: no remote copies, remote signals or barrier semaphores. Data moves between devices by JAX's collectives and lax.ppermute only.
A program may use at most 64 MiB of HBM per device.

v0:
```python
import jax
import jax.numpy as jnp
from jax import lax
from jax.sharding import PartitionSpec as P

D = 4096


def shifted(value, axis, steps):
    count = lax.axis_size(axis)
    initial, last = (max(0, -steps), min(count, count - steps))
    return lax.ppermute(value, axis, [(source, source + steps) for source in range(initial, last)])


def body(hidden, residual_in, weights, kept, cotangent, norm_gain):
    section_count = lax.axis_size("section")
    section_index = lax.axis_index("section")
    acts = hidden[0]
    row_count = acts.shape[0]
    block_size = weights.shape[-1]
    kept_table = kept[0, 0]
    local_blocks = weights[0, 0]
    owned_cols = local_blocks.shape[0]
    group_count = lax.axis_size("dp")
    picked = jnp.take(acts.reshape(row_count, -1, block_size), kept_table, axis=1)
    piece = lax.all_gather(local_blocks, "dp", axis=0, tiled=True)
    width_blocks = piece.shape[0]
    result = jnp.einsum("rckb,ckbd->rcd", picked, piece, preferred_element_type=jnp.float32)
    partial_out = result.reshape(row_count, width_blocks * block_size)
    contrib = lax.psum_scatter(
        partial_out.astype(jnp.bfloat16), "tensor", scatter_dimension=1, tiled=True
    ).astype(jnp.float32)
    current = (residual_in.astype(jnp.float32) + contrib).astype(jnp.bfloat16)
    for turn_index in range(1, section_count):
        incoming = shifted(current, "section", 1)
        updated = (incoming.astype(jnp.float32) + contrib).astype(jnp.bfloat16)
        current = jnp.where(section_index == turn_index, updated, current)
    final = current.astype(jnp.float32)
    scaled = cotangent.astype(jnp.float32) * norm_gain[None, :]
    square_sum, mixed_sum = lax.psum(
        (jnp.sum(final * final, axis=1), jnp.sum(scaled * final, axis=1)), "tensor"
    )
    inverse = lax.rsqrt(square_sum / D + 1e-05)
    mixed = mixed_sum / D
    out_grad = (inverse[:, None] * (scaled - final * (inverse * inverse * mixed)[:, None])).astype(
        jnp.bfloat16
    )
    carried = out_grad
    for turn_index in range(1, section_count):
        incoming = shifted(carried, "section", -1)
        carried = jnp.where(section_index == section_count - 1 - turn_index, incoming, carried)
    full_grad = lax.all_gather(carried, "tensor", axis=1, tiled=True)
    grad_full = full_grad.reshape(row_count, -1, block_size)
    block_grads = jnp.einsum(
        "rckb,rcd->ckbd", picked, grad_full, preferred_element_type=jnp.float32
    )
    received = lax.all_to_all(
        block_grads.astype(jnp.bfloat16), "dp", split_axis=0, concat_axis=0, tiled=True
    )
    received = received.reshape((group_count, owned_cols) + received.shape[1:])
    summed = jnp.sum(received.astype(jnp.float32), axis=0).astype(jnp.bfloat16)
    return (current[None], summed[None, None])


def solution(mesh):
    in_specs = (
        P("section", "dp", "tensor"),
        P("dp", "tensor"),
        P("section", "tensor", "dp", None, None, None),
        P("section", "tensor", None, None),
        P("dp", "tensor"),
        P("tensor"),
    )
    out_specs = (P("section", "dp", "tensor"), P("section", "tensor", "dp", None, None, None))
    return jax.shard_map(body, mesh=mesh, in_specs=in_specs, out_specs=out_specs, check_vma=False)
```

profile of v0, /device:TPU:1, one launch (start us, length us, event | category | flops | bytes accessed | tf_op | source)
XLA Modules:
  0.0 596.4 jit_solution(6685144097167939001)
XLA Ops:
  7.2 0.0 all-gather.6.cloned.1.call-start
  7.2 0.7 all-gather.6.cloned.1.call-update
  7.9 0.0 reduce-scatter.2.cloned.1.call-start
  7.9 1.3 copy.26
  9.2 0.3 copy.28
  9.5 0.7 compare_select_fusion
  10.2 0.1 copy.27
  10.3 0.1 reshape.53
  10.4 8.3 %gather_fusion = bf16[224,128,128]{2,1,0:T(8,128)(2,1)} fusion(bf16[128,14,128]{2,0,1:T(8,128)(2,1)S(1)} %copy.28, s32[1024]{0:T(1024)S(1)} %pad_clamp_fusion), kind=kCustom, calls=%fused_computation | custom fusion | bytes 14680960 | tf_op jit(solution)/shard_map/jit(_take)/gather | solution.py:25
  18.7 10.8 %copy.29 = bf16[32,7,128,128]{2,3,1,0:T(8,128)(2,1)} copy(bf16[32,7,128,128]{3,2,1,0:T(8,128)(2,1)} %bitcast.41) | data formatting | bytes 14680064 | tf_op jit(solution)/shard_map/jit(_take)/gather | solution.py:25
  29.5 0.0 copy-done.2
  29.5 0.1 copy.25
  29.6 0.0 copy-start.1
  29.6 0.0 copy-start.3
  29.6 81.2 %all-gather.6.cloned.1.call-done = bf16[1,1,32,7,128,128]{5,4,3,1,0,2:T(8,128)(2,1)} async-done(((bf16[1,1,2,7,128,128]{5,4,3,1,0,2:T(8,128)(2,1)}), bf16[1,1,32,7,128,128]{5,4,3,1,0,2:T(8,128)(2,1)}) %all-gather.6.cloned.1.call-update) | async-done | bytes 7340048 | tf_op jit(solution)/shard_map/all_gather | solution.py:26
  110.8 9.4 %bitcast_convert_fusion = bf16[32,128,128]{1,2,0:T(8,128)(2,1)} fusion(bf16[32,7,128,128]{2,3,1,0:T(8,128)(2,1)} %copy.29, pred[32,7]{1,0:T(8,128)(4,1)S(1)} %copy.25, bf16[1,1,32,7,128,128]{5,4,3,1,0,2:T(8,128)(2,1)} %all-gather.6.cloned.1.call-done), kind=kOutput, calls=%fused_computation.10 | convolution fusion | flops 943718400 | bytes 15728864 | tf_op jit(solution)/shard_map/rckb,ckbd->rcd/dot_general | solution.py:28
  120.3 0.0 reduce-scatter.2.cloned.1.call-update
  120.3 0.0 all-gather.4.cloned.1.call-start
  120.3 0.0 copy-done
  120.4 0.1 copy.24
  120.5 35.8 %reduce-scatter.2.cloned.1.call-done = bf16[128,512]{0,1:T(8,128)(2,1)} async-done(((bf16[128,4096]{0,1:T(8,128)(2,1)}), bf16[128,512]{0,1:T(8,128)(2,1)}) %reduce-scatter.2.cloned.1.call-update) | async-done | bytes 131088 | tf_op jit(solution)/shard_map/reduce_scatter | solution.py:30
  156.2 0.9 fusion.19
  157.2 2.1 collective-permute-start
  159.3 1.9 collective-permute-done
  161.2 1.0 fusion.25
  162.2 3.8 collective-permute-start.1
  166.0 1.9 collective-permute-done.1
  167.9 1.0 fusion.24
  168.9 3.8 collective-permute-start.2
  172.7 0.1 copy.33
  172.8 1.8 collective-permute-done.2
  174.6 1.1 fusion.14
  175.7 18.3 %all-reduce = (f32[128]{0:T(128)S(1)}, f32[128]{0:T(128)S(1)}) all-reduce(f32[128]{0:T(128)S(1)} %get-tuple-element.7, f32[128]{0:T(128)S(1)} %get-tuple-element.6), channel_id=1, replica_groups=mesh['section'=4,'dp'=16,'tensor'=8] {'tensor'}, use_global_device_ids=true, to_apply=%region_4.5 | all-reduce | flops 256 | bytes 2048 | tf_op jit(solution)/shard_map/psum | solution.py:40
  193.9 0.1 fusion.18
  194.1 1.3 collective-permute-start.3
  195.4 6.0 %collective-permute-done.3 = bf16[128,512]{0,1:T(8,128)(2,1)S(1)} collective-permute-done((bf16[128,512]{0,1:T(8,128)(2,1)S(1)}, bf16[128,512]{0,1:T(8,128)(2,1)S(1)}, u32[]{:S(2)}, u32[]{:S(2)}) %collective-permute-start.3) | collective-permute-done | bytes 131104 | tf_op jit(solution)/shard_map/ppermute | solution.py:12
  201.4 1.3 collective-permute-start.4
  202.7 4.4 collective-permute-done.4
  207.1 1.3 collective-permute-start.5
  208.5 4.4 collective-permute-done.5
  212.9 0.7 broadcast_select_fusion.3
  213.5 0.0 all-gather.4.cloned.1.call-update
  213.6 33.7 %all-gather.4.cloned.1.call-done = bf16[128,4096]{0,1:T(8,128)(2,1)} async-done(((bf16[128,512]{0,1:T(8,128)(2,1)}), bf16[128,4096]{0,1:T(8,128)(2,1)}) %all-gather.4.cloned.1.call-update) | async-done | bytes 1048592 | tf_op jit(solution)/shard_map/all_gather | solution.py:52
  247.3 8.5 %fusion.5 = bf16[32,7,128,128]{3,2,1,0:T(8,128)(2,1)} fusion(bf16[128,32,128,1]{0,2,3,1:T(8,128)(2,1)} %bitcast.47, bf16[32,7,128,128]{2,3,1,0:T(8,128)(2,1)} %copy.29, pred[32,7]{1,0:T(8,128)(4,1)S(1)} %copy.25), kind=kOutput, calls=%fused_computation.7 | convolution fusion | flops 946864128 | bytes 15728864 | tf_op jit(solution)/shard_map/rckb,rcd->ckbd/dot_general | solution.py:54
  255.8 11.9 %all-to-all-start = ((bf16[32,7,128,128]{3,2,1,0:T(8,128)(2,1)}), bf16[32,7,128,128]{3,2,1,0:T(8,128)(2,1)}, u32[]{:S(2)}, u32[]{:S(2)}) async-start(bf16[32,7,128,128]{3,2,1,0:T(8,128)(2,1)} %fusion.5), calls=%async_computation.1 | async-start | bytes 14680064 | tf_op jit(solution)/shard_map/all_to_all | solution.py:57
  267.6 0.8 copy.35
  268.4 316.0 %all-to-all-done = bf16[32,7,128,128]{3,2,1,0:T(8,128)(2,1)} async-done(((bf16[32,7,128,128]{3,2,1,0:T(8,128)(2,1)}), bf16[32,7,128,128]{3,2,1,0:T(8,128)(2,1)}, u32[]{:S(2)}, u32[]{:S(2)}) %all-to-all-start) | async-done | bytes 7340064 | tf_op jit(solution)/shard_map/all_to_all | solution.py:57
  584.4 5.5 reduce_sum.32
  (9 shorter events, 0.1 us)
Async XLA Ops:
  7.2 103.7 %all-gather.6.cloned.1.call-start = ((), (), s32[]{:S(2)}) async-start(), calls=%async_computation.4 | async-start | bytes 7798784 | tf_op jit(solution)/shard_map/all_gather | solution.py:26
  7.9 148.3 %reduce-scatter.2.cloned.1.call-start = ((), (), s32[]{:S(2)}) async-start(), calls=%async_computation.2 | async-start | bytes 1179648 | tf_op jit(solution)/shard_map/reduce_scatter | solution.py:30
  18.7 10.8 %copy-start.2 = (s32[1,1,32,7]{2,1,3,0:T(1,128)S(1)}, s32[1,1,32,7]{2,1,3,0:T(1,128)}, u32[]{:S(2)}) copy-start(s32[1,1,32,7]{2,1,3,0:T(1,128)} %param.9) | copy-start | bytes 2692
  29.6 90.8 %copy-start = (bf16[128,512]{1,0:T(8,128)(2,1)S(1)}, bf16[128,512]{1,0:T(8,128)(2,1)}, u32[]{:S(2)}) copy-start(bf16[128,512]{1,0:T(8,128)(2,1)} %param.7) | copy-start | bytes 393220
  29.6 143.1 %copy-start.1 = (bf16[128,512]{1,0:T(8,128)(2,1)S(1)}, bf16[128,512]{1,0:T(8,128)(2,1)}, u32[]{:S(2)}) copy-start(bf16[128,512]{1,0:T(8,128)(2,1)} %param.10) | copy-start | bytes 393220
  29.6 145.0 %copy-start.3 = (f32[512]{0:T(512)S(1)}, f32[512]{0:T(512)}, u32[]{:S(2)}) copy-start(f32[512]{0:T(512)} %param.11) | copy-start | bytes 6148
  120.3 127.0 %all-gather.4.cloned.1.call-start = ((), (), s32[]{:S(2)}) async-start(), calls=%async_computation.3 | async-start | bytes 1179648 | tf_op jit(solution)/shard_map/all_gather | solution.py:52
  157.2 4.1 collective-permute-start
  162.2 5.7 collective-permute-start.1
  168.9 5.7 collective-permute-start.2
  194.1 7.3 %collective-permute-start.3 = (bf16[128,512]{0,1:T(8,128)(2,1)S(1)}, bf16[128,512]{0,1:T(8,128)(2,1)S(1)}, u32[]{:S(2)}, u32[]{:S(2)}) collective-permute-start(bf16[128,512]{0,1:T(8,128)(2,1)S(1)} %fusion.18), channel_id=1, source_target_pairs={{128,0},{256,128},{384,256},{129,1},{257,129},{385,257},{130,2},{2... | collective-permute-start | bytes 393224 | tf_op jit(solution)/shard_map/ppermute | solution.py:12
  201.4 5.7 collective-permute-start.4
  207.1 5.7 collective-permute-start.5
  255.8 328.6 %all-to-all-start = ((bf16[32,7,128,128]{3,2,1,0:T(8,128)(2,1)}), bf16[32,7,128,128]{3,2,1,0:T(8,128)(2,1)}, u32[]{:S(2)}, u32[]{:S(2)}) async-start(bf16[32,7,128,128]{3,2,1,0:T(8,128)(2,1)} %fusion.5), calls=%async_computation.1 | async-start | bytes 14680064 | tf_op jit(solution)/shard_map/all_to_all | solution.py:57
Sparse Core Ops, SparseCore 0:
  10.1 100.7 all-gather.5
  120.4 35.7 reduce-scatter.1
  213.7 33.5 all-gather.3
where the time goes:
time: 598 us; the launch traced here: 596 us
  waiting for transfers between devices  488 us (82%)
  starting transfers between devices  25.6 us (4%)
  local copies, waits for them, and re-layouts  21.9 us (4%)
  blocking collectives  18.3 us (3%)
  matrix products  17.9 us (3%)
  between operations  13.9 us (2%)
  other arithmetic  11 us (2%)
    all_to_all x1, waiting for transfers between devices, body(): lax.all_to_all(block_grads.astype(jnp.bfloat16), 'dp', split_axis=0, conc...  316 us
    all_gather x1, waiting for transfers between devices, body(): piece = lax.all_gather(local_blocks, 'dp', axis=0, tiled=True)  81.2 us
    reduce_scatter x1, waiting for transfers between devices, body(): lax.psum_scatter(partial_out.astype(jnp.bfloat16), 'tensor', scatter_dime...  35.8 us
    all_gather x1, waiting for transfers between devices, body(): full_grad = lax.all_gather(carried, 'tensor', axis=1, tiled=True)  33.7 us
    ppermute x6, waiting for transfers between devices, shifted(): lax.ppermute(value, axis, [(source, source + steps) for source in range(i...  20.5 us
    gather x2, local copies, waits for them, and re-layouts, body(): jnp.take(acts.reshape(row_count, -1, block_size), kept_table, axis=1)  19.1 us
    psum x1, blocking collectives, body(): lax.psum((jnp.sum(final * final, axis=1), jnp.sum(scaled * final, axis=1)...  18.3 us
    ppermute x6, starting transfers between devices, shifted(): lax.ppermute(value, axis, [(source, source + steps) for source in range(i...  13.6 us
  transfers between devices with their start and end apart: 10, of which 10 were waited for; matrix products, arithmetic and copies ran while one was open for 4% of the time, Pallas kernels for 0%

commit v1 on v0

v1 whole, which is shorter than its diff:
```python
import jax
import jax.numpy as jnp
from jax import lax
from jax.sharding import PartitionSpec as P

D = 4096
PLANE = ("section", "tensor")
ALL = ("section", "dp", "tensor")


def to_columns_pairs(ns, nz, nt):
    pairs = []
    for s in range(ns):
        for p in range(nz):
            for t in range(nt):
                piece = 2 * p + s // 2
                plane = 2 * t + s % 2
                pairs.append(
                    ((s * nz + p) * nt + t, ((piece // nt) * nz + plane) * nt + piece % nt)
                )
    return pairs


def to_tokens_pairs(ns, nz, nt, turn):
    pairs = []
    for s in range(ns):
        for z in range(nz):
            for t in range(nt):
                piece = s * nt + t
                quarter = 2 * (piece % 2) + z % 2
                section = (turn + quarter) % ns
                pairs.append(
                    ((s * nz + z) * nt + t, (section * nz + piece // 2) * nt + z // 2)
                )
    return pairs


def body(hidden, residual_in, weights, kept, cotangent, norm_gain):
    ns, nz, nt = (lax.axis_size(a) for a in ALL)
    section, plane, shard = (lax.axis_index(a) for a in ALL)
    acts = hidden[0]
    blocks = weights[0, 0]
    cols, keep, blk, _ = blocks.shape
    width = cols * blk
    hidden_blocks = acts.shape[1] // blk
    every = lax.all_gather(acts, "dp", axis=0, tiled=True)
    tokens = every.shape[0]
    piece = tokens // (ns * nt)

    own_kept = lax.dynamic_slice_in_dim(kept[0, 0], plane * cols, cols, axis=0)
    hit = own_kept[None] == jnp.arange(hidden_blocks, dtype=own_kept.dtype)[:, None, None]
    dense = jnp.sum(
        jnp.where(hit[..., None, None], blocks[None].astype(jnp.float32), 0.0), axis=2
    ).astype(jnp.bfloat16)
    dense = dense.transpose(0, 2, 1, 3).reshape(hidden_blocks * blk, width)

    down, across = section // 2, section % 2
    corner = lambda a: lax.dynamic_slice(a, (down * piece, across * width), (piece, width))
    pairs = to_columns_pairs(ns, nz, nt)
    residual = lax.ppermute(corner(residual_in), ALL, pairs).astype(jnp.float32)
    scaled = corner(cotangent.astype(jnp.float32) * norm_gain[None, :])
    scaled = lax.ppermute(scaled, ALL, pairs)

    partial_out = jnp.dot(every, dense, preferred_element_type=jnp.float32).astype(jnp.bfloat16)
    received = lax.all_to_all(
        partial_out.reshape(ns * nt, piece, width), PLANE, split_axis=0, concat_axis=0, tiled=True
    )
    contrib = jnp.sum(received.reshape(ns, nt, piece, width).astype(jnp.float32), axis=1)
    outs = []
    current = residual
    for turn in range(ns):
        outs.append((current + contrib[turn]).astype(jnp.bfloat16))
        current = outs[-1].astype(jnp.float32)
    stacked = jnp.stack(outs)

    sums = jnp.concatenate([jnp.sum(current * current, axis=1), jnp.sum(scaled * current, axis=1)])
    spread = jnp.broadcast_to(sums[None, None, :], (nz, 1, 2 * piece))
    spread = lax.all_to_all(spread, "dp", split_axis=0, concat_axis=0, tiled=True)
    totals = jnp.sum(spread, axis=(0, 1)) / D
    inverse = lax.rsqrt(totals[:piece] + 1e-05)
    mixed = totals[piece:]
    out_grad = (
        inverse[:, None] * (scaled - current * (inverse * inverse * mixed)[:, None])
    ).astype(jnp.bfloat16)

    full_grad = lax.all_to_all(
        jnp.broadcast_to(out_grad[None], (ns * nt, piece, width)),
        PLANE,
        split_axis=0,
        concat_axis=0,
        tiled=True,
    ).reshape(tokens, width)

    quarter = 2 * (shard % 2) + plane % 2
    back = []
    for turn in range(ns):
        chosen = lax.dynamic_index_in_dim(stacked, (turn + quarter) % ns, 0, keepdims=False)
        back.append(lax.ppermute(chosen, ALL, to_tokens_pairs(ns, nz, nt, turn)))
    back = jnp.stack(back)
    corners = [
        lax.dynamic_index_in_dim(back, (section - q) % ns, 0, keepdims=False) for q in range(ns)
    ]
    section_out = jnp.concatenate(
        [jnp.concatenate(corners[:2], axis=1), jnp.concatenate(corners[2:], axis=1)], axis=0
    )

    grads = lax.dot_general(
        every, full_grad, (((0,), (0,)), ((), ())), preferred_element_type=jnp.float32
    ).astype(jnp.bfloat16)
    grads = grads.reshape(hidden_blocks, blk, cols, blk)
    picked = []
    for c in range(cols):
        picked.append(
            jnp.stack(
                [
                    lax.dynamic_index_in_dim(grads[:, :, c], own_kept[c, k], 0, keepdims=False)
                    for k in range(keep)
                ]
            )
        )
    return (section_out[None], jnp.stack(picked)[None, None])


def solution(mesh):
    in_specs = (
        P("section", "dp", "tensor"),
        P("dp", "tensor"),
        P("section", "tensor", "dp", None, None, None),
        P("section", "tensor", None, None),
        P("dp", "tensor"),
        P("tensor"),
    )
    out_specs = (P("section", "dp", "tensor"), P("section", "tensor", "dp", None, None, None))
    return jax.shard_map(body, mesh=mesh, in_specs=in_specs, out_specs=out_specs, check_vma=False)
```

time: 598 us -> 258 us (0.43)
  the two profiles are of different devices: /device:TPU:1 before, /device:TPU:22 now
where the time goes in v1:
time: 258 us; the launch traced here: 257 us
  waiting for transfers between devices  109 us (42%)
  starting transfers between devices  61.4 us (24%)
  between operations  40.7 us (16%)
  blocking collectives  20.1 us (8%)
  matrix products  10.4 us (4%)
  local copies, waits for them, and re-layouts  9.1 us (4%)
  other arithmetic  5.71 us (2%)
    all_gather x1, waiting for transfers between devices, body(): every = lax.all_gather(acts, 'dp', axis=0, tiled=True)  97.8 us
    ppermute x4, starting transfers between devices, body(): back.append(lax.ppermute(chosen, ALL, to_tokens_pairs(ns, nz, nt, turn)))  33.6 us
    all_to_all x1, blocking collectives, body(): lax.all_to_all(spread, 'dp', split_axis=0, concat_axis=0, tiled=True)  20.1 us
    ppermute x1, waiting for transfers between devices, body(): residual = lax.ppermute(corner(residual_in), ALL, pairs).astype(jnp.float32)  10.7 us
    all_to_all x1, starting transfers between devices, body(): lax.all_to_all(jnp.broadcast_to(out_grad[None], (ns * nt, piece, width)),...  8.5 us
    all_to_all x1, starting transfers between devices, body(): lax.all_to_all(partial_out.reshape(ns * nt, piece, width), PLANE, split_a...  7.39 us
    ppermute x1, starting transfers between devices, body(): scaled = lax.ppermute(scaled, ALL, pairs)  6.42 us
    ppermute x1, starting transfers between devices, body(): residual = lax.ppermute(corner(residual_in), ALL, pairs).astype(jnp.float32)  5.4 us
  transfers between devices with their start and end apart: 9, of which 2 were waited for; matrix products, arithmetic and copies ran while one was open for 3% of the time, Pallas kernels for 0%

profile of v1, /device:TPU:22, one launch (start us, length us, event | category | flops | bytes accessed | tf_op | source)
XLA Modules:
  0.0 256.6 jit_solution(9980051409578166541)
XLA Ops:
  7.2 0.7 all-gather.3.cloned.1.call-update
  7.9 0.1 constant_dynamic-slice_fusion.14
  8.0 0.1 copy.33
  8.1 1.1 bitcast_convert_fusion
  9.2 1.8 select_reduce_fusion
  11.0 0.9 copy.34
  12.0 97.8 %all-gather.3.cloned.1.call-done = bf16[1,2048,1792]{2,1,0:T(8,128)(2,1)} async-done(((bf16[1,128,1792]{2,1,0:T(8,128)(2,1)}), bf16[1,2048,1792]{2,1,0:T(8,128)(2,1)}) %all-gather.3.cloned.1.call-update) | async-done | bytes 7340048 | tf_op jit(solution)/shard_map/all_gather | solution.py:46
  109.8 5.2 %fusion.13 = bf16[2048,256]{0,1:T(8,128)(2,1)S(1)} fusion(bf16[1,2048,1792]{2,1,0:T(8,128)(2,1)} %all-gather.3.cloned.1.call-done, bf16[224,8,2,128]{3,2,1,0:T(2,128)(2,1)S(1)} %bitcast.164), kind=kOutput, calls=%fused_computation.8 | convolution fusion | flops 1879572480 | bytes 9306112 | tf_op jit(solution)/shard_map/dot_general | solution.py:64
  115.0 1.4 copy.35
  116.3 7.4 %all-to-all-start = ((bf16[32,64,256]{2,1,0:T(8,128)(2,1)}), bf16[32,64,256]{2,1,0:T(8,128)(2,1)S(1)}, u32[]{:S(2)}, u32[]{:S(2)}) async-start(bf16[32,64,256]{2,1,0:T(8,128)(2,1)} %bitcast.5), calls=%async_computation | async-start | bytes 2097152 | tf_op jit(solution)/shard_map/all_to_all | solution.py:65
  123.8 0.1 dynamic-slice.15
  123.9 0.8 convert_multiply_fusion.3
  124.6 6.4 %collective-permute-start.5 = (f32[64,256]{1,0:T(8,128)S(1)}, f32[64,256]{1,0:T(8,128)S(1)}, u32[]{:S(2)}, u32[]{:S(2)}) collective-permute-start(f32[64,256]{1,0:T(8,128)S(1)} %convert_multiply_fusion.3), channel_id=1, source_target_pairs={{0,0},{1,16},{2,32},{3,48},{4,64},{5,80},{6,96},{7,112},{8,2},{9,1... | collective-permute-start | bytes 196616 | tf_op jit(solution)/shard_map/ppermute | solution.py:62
  131.1 0.8 dynamic_slice.105
  131.8 5.4 %collective-permute-start = (bf16[64,256]{1,0:T(8,128)(2,1)S(1)}, bf16[64,256]{1,0:T(8,128)(2,1)S(1)}, u32[]{:S(2)}, u32[]{:S(2)}) collective-permute-start(bf16[64,256]{1,0:T(8,128)(2,1)S(1)} %dynamic_slice.105), channel_id=1, source_target_pairs={{0,0},{1,16},{2,32},{3,48},{4,64},{5,80},{6,96},{7,112},{8,2},{9,1... | collective-permute-start | bytes 98312 | tf_op jit(solution)/shard_map/ppermute | solution.py:60
  137.3 0.2 convert_reduce_fusion
  137.4 10.7 %collective-permute-done = bf16[64,256]{1,0:T(8,128)(2,1)S(1)} collective-permute-done((bf16[64,256]{1,0:T(8,128)(2,1)S(1)}, bf16[64,256]{1,0:T(8,128)(2,1)S(1)}, u32[]{:S(2)}, u32[]{:S(2)}) %collective-permute-start) | collective-permute-done | bytes 32800 | tf_op jit(solution)/shard_map/ppermute | solution.py:60
  148.2 0.1 fusion.18
  148.3 0.1 pad_maximum_fusion.2
  148.4 20.1 %all_to_all.15 = f32[16,1,128]{2,1,0:T(1,128)S(1)} all-to-all(f32[16,1,128]{2,1,0:T(1,128)S(1)} %broadcast_in_dim.48), channel_id=1, replica_groups=mesh['section'=4,'dp'=16,'tensor'=8] {'dp'}, dimensions={0} | all-to-all | bytes 16384 | tf_op jit(solution)/shard_map/all_to_all | solution.py:78
  168.5 0.1 fusion.22
  168.6 1.1 broadcast_in_dim.49
  169.8 8.5 %all-to-all-start.2 = ((bf16[32,64,256]{2,1,0:T(8,128)(2,1)}), bf16[32,64,256]{2,1,0:T(8,128)(2,1)S(1)}, u32[]{:S(2)}, u32[]{:S(2)}) async-start(bf16[32,64,256]{2,1,0:T(8,128)(2,1)} %broadcast_in_dim.49), calls=%async_computation.2 | async-start | bytes 2097152 | tf_op jit(solution)/shard_map/all_to_all | solution.py:86
  178.4 3.2 %collective-permute-start.4 = (bf16[64,256]{1,0:T(8,128)(2,1)S(1)}, bf16[64,256]{1,0:T(8,128)(2,1)S(1)}, u32[]{:S(2)}, u32[]{:S(2)}) collective-permute-start(bf16[64,256]{1,0:T(8,128)(2,1)S(1)} %get-tuple-element.28), channel_id=1, source_target_pairs={{0,384},{1,128},{2,392},{3,136},{4,400},{5,144},{6,408},{7,152},{8... | collective-permute-start | bytes 98312 | tf_op jit(solution)/shard_map/ppermute | solution.py:98
  181.6 4.0 %collective-permute-start.3 = (bf16[64,256]{1,0:T(8,128)(2,1)S(1)}, bf16[64,256]{1,0:T(8,128)(2,1)S(1)}, u32[]{:S(2)}, u32[]{:S(2)}) collective-permute-start(bf16[64,256]{1,0:T(8,128)(2,1)S(1)} %get-tuple-element.29), channel_id=1, source_target_pairs={{0,256},{1,0},{2,264},{3,8},{4,272},{5,16},{6,280},{7,24},{8,384},... | collective-permute-start | bytes 98312 | tf_op jit(solution)/shard_map/ppermute | solution.py:98
  185.6 14.4 %collective-permute-start.2 = (bf16[64,256]{1,0:T(8,128)(2,1)S(1)}, bf16[64,256]{1,0:T(8,128)(2,1)S(1)}, u32[]{:S(2)}, u32[]{:S(2)}) collective-permute-start(bf16[64,256]{1,0:T(8,128)(2,1)S(1)} %get-tuple-element.30), channel_id=1, source_target_pairs={{0,128},{1,384},{2,136},{3,392},{4,144},{5,400},{6,152},{7,408},{8... | collective-permute-start | bytes 98312 | tf_op jit(solution)/shard_map/ppermute | solution.py:98
  200.0 12.1 %collective-permute-start.1 = (bf16[64,256]{1,0:T(8,128)(2,1)S(1)}, bf16[64,256]{1,0:T(8,128)(2,1)S(1)}, u32[]{:S(2)}, u32[]{:S(2)}) collective-permute-start(bf16[64,256]{1,0:T(8,128)(2,1)S(1)} %get-tuple-element.27), channel_id=1, source_target_pairs={{0,0},{1,256},{2,8},{3,264},{4,16},{5,272},{6,24},{7,280},{8,128},... | collective-permute-start | bytes 98312 | tf_op jit(solution)/shard_map/ppermute | solution.py:98
  212.1 0.7 fusion.36
  239.0 0.7 maximum_bitcast_fusion.1
  239.7 5.2 %fusion.10 = bf16[1792,256]{0,1:T(8,128)(2,1)S(1)} fusion(bf16[2048,256]{1,0:T(8,128)(2,1)S(1)} %bitcast.162, bf16[1,2048,1792]{2,1,0:T(8,128)(2,1)} %all-gather.3.cloned.1.call-done), kind=kOutput, calls=%fused_computation.7 | convolution fusion | flops 1879506944 | bytes 9306112 | tf_op jit(solution)/shard_map/dot_general | solution.py:107
  244.9 0.7 reshape.62
  245.6 0.2 fusion.35
  245.8 1.2 constant_dynamic-slice_fusion
  247.0 0.1 copy.46
  247.1 0.1 copy.47
  247.2 0.1 copy.48
  247.4 0.1 copy.49
  247.5 0.1 copy.50
  247.6 0.1 copy.51
  247.7 0.1 copy.52
  247.9 0.1 copy.39
  248.0 0.1 copy.40
  248.1 0.1 copy.41
  248.3 0.1 copy.42
  248.4 0.1 copy.43
  248.5 0.1 copy.44
  248.6 0.1 copy.45
  249.0 0.8 maximum_bitcast_fusion
  (36 shorter events, 0.4 us)
Async XLA Ops:
  7.2 0.8 copy-start
  7.2 102.6 %all-gather.3.cloned.1.call-start = ((), (), s32[]{:S(2)}) async-start(), calls=%async_computation.3 | async-start | bytes 7798784 | tf_op jit(solution)/shard_map/all_gather | solution.py:46
  109.8 14.0 %copy-start.1 = (f32[512]{0:T(512)S(1)}, f32[512]{0:T(512)}, u32[]{:S(2)}) copy-start(f32[512]{0:T(512)} %param.11) | copy-start | bytes 6148
  116.3 20.9 %all-to-all-start = ((bf16[32,64,256]{2,1,0:T(8,128)(2,1)}), bf16[32,64,256]{2,1,0:T(8,128)(2,1)S(1)}, u32[]{:S(2)}, u32[]{:S(2)}) async-start(bf16[32,64,256]{2,1,0:T(8,128)(2,1)} %bitcast.5), calls=%async_computation | async-start | bytes 2097152 | tf_op jit(solution)/shard_map/all_to_all | solution.py:65
  124.6 23.5 %collective-permute-start.5 = (f32[64,256]{1,0:T(8,128)S(1)}, f32[64,256]{1,0:T(8,128)S(1)}, u32[]{:S(2)}, u32[]{:S(2)}) collective-permute-start(f32[64,256]{1,0:T(8,128)S(1)} %convert_multiply_fusion.3), channel_id=1, source_target_pairs={{0,0},{1,16},{2,32},{3,48},{4,64},{5,80},{6,96},{7,112},{8,2},{9,1... | collective-permute-start | bytes 196616 | tf_op jit(solution)/shard_map/ppermute | solution.py:62
  131.8 16.3 %collective-permute-start = (bf16[64,256]{1,0:T(8,128)(2,1)S(1)}, bf16[64,256]{1,0:T(8,128)(2,1)S(1)}, u32[]{:S(2)}, u32[]{:S(2)}) collective-permute-start(bf16[64,256]{1,0:T(8,128)(2,1)S(1)} %dynamic_slice.105), channel_id=1, source_target_pairs={{0,0},{1,16},{2,32},{3,48},{4,64},{5,80},{6,96},{7,112},{8,2},{9,1... | collective-permute-start | bytes 98312 | tf_op jit(solution)/shard_map/ppermute | solution.py:60
  169.8 69.9 %all-to-all-start.2 = ((bf16[32,64,256]{2,1,0:T(8,128)(2,1)}), bf16[32,64,256]{2,1,0:T(8,128)(2,1)S(1)}, u32[]{:S(2)}, u32[]{:S(2)}) async-start(bf16[32,64,256]{2,1,0:T(8,128)(2,1)} %broadcast_in_dim.49), calls=%async_computation.2 | async-start | bytes 2097152 | tf_op jit(solution)/shard_map/all_to_all | solution.py:86
  178.4 60.5 %collective-permute-start.4 = (bf16[64,256]{1,0:T(8,128)(2,1)S(1)}, bf16[64,256]{1,0:T(8,128)(2,1)S(1)}, u32[]{:S(2)}, u32[]{:S(2)}) collective-permute-start(bf16[64,256]{1,0:T(8,128)(2,1)S(1)} %get-tuple-element.28), channel_id=1, source_target_pairs={{0,384},{1,128},{2,392},{3,136},{4,400},{5,144},{6,408},{7,152},{8... | collective-permute-start | bytes 98312 | tf_op jit(solution)/shard_map/ppermute | solution.py:98
  181.6 57.3 %collective-permute-start.3 = (bf16[64,256]{1,0:T(8,128)(2,1)S(1)}, bf16[64,256]{1,0:T(8,128)(2,1)S(1)}, u32[]{:S(2)}, u32[]{:S(2)}) collective-permute-start(bf16[64,256]{1,0:T(8,128)(2,1)S(1)} %get-tuple-element.29), channel_id=1, source_target_pairs={{0,256},{1,0},{2,264},{3,8},{4,272},{5,16},{6,280},{7,24},{8,384},... | collective-permute-start | bytes 98312 | tf_op jit(solution)/shard_map/ppermute | solution.py:98
  185.6 53.4 %collective-permute-start.2 = (bf16[64,256]{1,0:T(8,128)(2,1)S(1)}, bf16[64,256]{1,0:T(8,128)(2,1)S(1)}, u32[]{:S(2)}, u32[]{:S(2)}) collective-permute-start(bf16[64,256]{1,0:T(8,128)(2,1)S(1)} %get-tuple-element.30), channel_id=1, source_target_pairs={{0,128},{1,384},{2,136},{3,392},{4,144},{5,400},{6,152},{7,408},{8... | collective-permute-start | bytes 98312 | tf_op jit(solution)/shard_map/ppermute | solution.py:98
  200.0 39.0 %collective-permute-start.1 = (bf16[64,256]{1,0:T(8,128)(2,1)S(1)}, bf16[64,256]{1,0:T(8,128)(2,1)S(1)}, u32[]{:S(2)}, u32[]{:S(2)}) collective-permute-start(bf16[64,256]{1,0:T(8,128)(2,1)S(1)} %get-tuple-element.27), channel_id=1, source_target_pairs={{0,0},{1,256},{2,8},{3,264},{4,16},{5,272},{6,24},{7,280},{8,128},... | collective-permute-start | bytes 98312 | tf_op jit(solution)/shard_map/ppermute | solution.py:98
Sparse Core Ops, SparseCore 0:
  10.1 99.6 all-gather.2

commit v2 on v1

--- a/solution.py
+++ b/solution.py
@@ -1,6 +1,8 @@
 import jax
 import jax.numpy as jnp
 from jax import lax
+from jax.experimental import pallas as pl
+from jax.experimental.pallas import tpu as pltpu
 from jax.sharding import PartitionSpec as P
 
 D = 4096
@@ -35,6 +37,104 @@
     return pairs
 
 
+def forward_kernel(acts_ref, dense_ref, residual_ref, scaled_ref, out_ref):
+    out_ref[...] = jnp.dot(
+        acts_ref[...], dense_ref[...], preferred_element_type=jnp.float32
+    ).astype(out_ref.dtype)
+
+
+def forward(every, dense, residual, scaled):
+    tokens, units = every.shape
+    width = dense.shape[1]
+    tile = 256
+    return pl.pallas_call(
+        forward_kernel,
+        grid=(tokens // tile,),
+        in_specs=[
+            pl.BlockSpec((tile, units), lambda i: (i, 0)),
+            pl.BlockSpec((units, width), lambda i: (0, 0)),
+            pl.BlockSpec(memory_space=pl.ANY),
+            pl.BlockSpec(memory_space=pl.ANY),
+        ],
+        out_specs=pl.BlockSpec((tile, width), lambda i: (i, 0)),
+        out_shape=jax.ShapeDtypeStruct((tokens, width), jnp.bfloat16),
+        compiler_params=pltpu.CompilerParams(vmem_limit_bytes=32 << 20),
+        cost_estimate=pl.CostEstimate(
+            flops=2 * tokens * units * width, bytes_accessed=2 * tokens * units, transcendentals=0
+        ),
+        name="forward_matmul",
+    )(every, dense, residual, scaled)
+
+
+def gradient_kernel(slot_ref, grad_ref, acts_ref, out_ref, turned_ref):
+    step = pl.program_id(0)
+
+    @pl.when(step == 0)
+    def _():
+        turned_ref[...] = grad_ref[...].T
+
+    cols, keep, blk, _ = out_ref.shape
+    per_step = acts_ref.shape[1] // blk
+    found = jnp.dot(turned_ref[...], acts_ref[...], preferred_element_type=jnp.float32)
+    for part in range(per_step):
+        for c in range(cols):
+            slot = slot_ref[c, step * per_step + part]
+
+            @pl.when(slot >= 0)
+            def _(part=part, c=c, slot=slot):
+                block = found[c * blk : (c + 1) * blk, part * blk : (part + 1) * blk]
+                out_ref[c, slot] = block.T.astype(out_ref.dtype)
+
+
+def gradient(slots, full_grad, every, keep, blk):
+    tokens, units = every.shape
+    width = full_grad.shape[1]
+    cols = width // blk
+    per_step = 2
+    return pl.pallas_call(
+        gradient_kernel,
+        grid_spec=pltpu.PrefetchScalarGridSpec(
+            num_scalar_prefetch=1,
+            grid=(units // (per_step * blk),),
+            in_specs=[
+                pl.BlockSpec((tokens, width), lambda i, _: (0, 0)),
+                pl.BlockSpec((tokens, per_step * blk), lambda i, _: (0, i)),
+            ],
+            out_specs=pl.BlockSpec((cols, keep, blk, blk), lambda i, _: (0, 0, 0, 0)),
+            scratch_shapes=[pltpu.VMEM((width, tokens), jnp.bfloat16)],
+        ),
+        out_shape=jax.ShapeDtypeStruct((cols, keep, blk, blk), jnp.bfloat16),
+        compiler_params=pltpu.CompilerParams(vmem_limit_bytes=32 << 20),
+        cost_estimate=pl.CostEstimate(
+            flops=2 * tokens * units * width, bytes_accessed=2 * tokens * units, transcendentals=0
+        ),
+        name="gradient_matmul",
+    )(slots, full_grad, every)
+
+
+def turn_kernel(shift_ref, stacked_ref, after_ref, out_ref):
+    ns = stacked_ref.shape[0]
+    for turn in range(ns):
+        out_ref[turn] = stacked_ref[lax.rem(turn + shift_ref[0], ns)]
+
+
+def turned(shift, stacked, after):
+    return pl.pallas_call(
+        turn_kernel,
+        grid_spec=pltpu.PrefetchScalarGridSpec(
+            num_scalar_prefetch=1,
+            grid=(1,),
+            in_specs=[
+                pl.BlockSpec(stacked.shape, lambda i, _: (0, 0, 0)),
+                pl.BlockSpec(memory_space=pl.ANY),
+            ],
+            out_specs=pl.BlockSpec(stacked.shape, lambda i, _: (0, 0, 0)),
+        ),
+        out_shape=jax.ShapeDtypeStruct(stacked.shape, stacked.dtype),
+        name="turn_sections",
+    )(shift, stacked, after)
+
+
 def body(hidden, residual_in, weights, kept, cotangent, norm_gain):
     ns, nz, nt = (lax.axis_size(a) for a in ALL)
     section, plane, shard = (lax.axis_index(a) for a in ALL)
@@ -57,17 +157,17 @@
     down, across = section // 2, section % 2
     corner = lambda a: lax.dynamic_slice(a, (down * piece, across * width), (piece, width))
     pairs = to_columns_pairs(ns, nz, nt)
-    residual = lax.ppermute(corner(residual_in), ALL, pairs).astype(jnp.float32)
+    residual = lax.ppermute(corner(residual_in), ALL, pairs)
     scaled = corner(cotangent.astype(jnp.float32) * norm_gain[None, :])
     scaled = lax.ppermute(scaled, ALL, pairs)
 
-    partial_out = jnp.dot(every, dense, preferred_element_type=jnp.float32).astype(jnp.bfloat16)
+    partial_out = forward(every, dense, residual, scaled)
     received = lax.all_to_all(
         partial_out.reshape(ns * nt, piece, width), PLANE, split_axis=0, concat_axis=0, tiled=True
     )
     contrib = jnp.sum(received.reshape(ns, nt, piece, width).astype(jnp.float32), axis=1)
     outs = []
-    current = residual
+    current = residual.astype(jnp.float32)
     for turn in range(ns):
         outs.append((current + contrib[turn]).astype(jnp.bfloat16))
         current = outs[-1].astype(jnp.float32)
@@ -92,10 +192,8 @@
     ).reshape(tokens, width)
 
     quarter = 2 * (shard % 2) + plane % 2
-    back = []
-    for turn in range(ns):
-        chosen = lax.dynamic_index_in_dim(stacked, (turn + quarter) % ns, 0, keepdims=False)
-        back.append(lax.ppermute(chosen, ALL, to_tokens_pairs(ns, nz, nt, turn)))
+    sent = turned(quarter.astype(jnp.int32).reshape(1), stacked, full_grad)
+    back = [lax.ppermute(sent[turn], ALL, to_tokens_pairs(ns, nz, nt, turn)) for turn in range(ns)]
     back = jnp.stack(back)
     corners = [
         lax.dynamic_index_in_dim(back, (section - q) % ns, 0, keepdims=False) for q in range(ns)
@@ -104,21 +202,10 @@
         [jnp.concatenate(corners[:2], axis=1), jnp.concatenate(corners[2:], axis=1)], axis=0
     )
 
-    grads = lax.dot_general(
-        every, full_grad, (((0,), (0,)), ((), ())), preferred_element_type=jnp.float32
-    ).astype(jnp.bfloat16)
-    grads = grads.reshape(hidden_blocks, blk, cols, blk)
-    picked = []
-    for c in range(cols):
-        picked.append(
-            jnp.stack(
-                [
-                    lax.dynamic_index_in_dim(grads[:, :, c], own_kept[c, k], 0, keepdims=False)
-                    for k in range(keep)
-                ]
-            )
-        )
-    return (section_out[None], jnp.stack(picked)[None, None])
+    found = jnp.any(hit, axis=2)
+    slots = jnp.where(found, jnp.argmax(hit, axis=2), -1).T.astype(jnp.int32)
+    grads = gradient(slots, full_grad, every, keep, blk)
+    return (section_out[None], grads[None, None])
 
 
 def solution(mesh):

time: 258 us -> 238 us (0.922)
  the two profiles are of different devices: /device:TPU:22 before, /device:TPU:83 now
where the time goes in v2:
time: 238 us; the launch traced here: 237 us
  waiting for transfers between devices  91.1 us (38%)
  starting transfers between devices  58.2 us (24%)
  blocking collectives  42.3 us (18%)
  between operations  14.4 us (6%)
  local copies, waits for them, and re-layouts  13.3 us (6%)
  Pallas kernels  11.5 us (5%)
  other arithmetic  6.18 us (3%)
    all_gather x1, waiting for transfers between devices, body(): every = lax.all_gather(acts, 'dp', axis=0, tiled=True)  76.1 us
    ppermute x4, starting transfers between devices, body(): lax.ppermute(sent[turn], ALL, to_tokens_pairs(ns, nz, nt, turn))  32.1 us
    all_to_all x1, blocking collectives, body(): lax.all_to_all(partial_out.reshape(ns * nt, piece, width), PLANE, split_a...  21.6 us
    all_to_all x1, blocking collectives, body(): lax.all_to_all(spread, 'dp', split_axis=0, concat_axis=0, tiled=True)  20.7 us
    all_to_all x1, waiting for transfers between devices, body(): lax.all_to_all(jnp.broadcast_to(out_grad[None], (ns * nt, piece, width)),...  13.4 us
    ppermute x1, starting transfers between devices, body(): residual = lax.ppermute(corner(residual_in), ALL, pairs)  9.51 us
    ppermute x1, starting transfers between devices, body(): scaled = lax.ppermute(scaled, ALL, pairs)  8.58 us
    unnamed x11, local copies, waits for them, and re-layouts  8.49 us
  transfers between devices with their start and end apart: 8, of which 3 were waited for; matrix products, arithmetic and copies ran while one was open for 3% of the time, Pallas kernels for 3%

profile of v2, /device:TPU:83, one launch (start us, length us, event | category | flops | bytes accessed | tf_op | source)
XLA Modules:
  0.0 237.0 jit_solution(9922055319787484912)
XLA Ops:
  7.2 0.0 copy-start
  7.2 0.0 all-gather.3.cloned.1.call-start
  7.2 0.7 all-gather.3.cloned.1.call-update
  7.9 0.8 dynamic_slice.22
  8.7 9.5 %collective-permute-start = (bf16[64,256]{1,0:T(8,128)(2,1)S(1)}, bf16[64,256]{1,0:T(8,128)(2,1)S(1)}, u32[]{:S(2)}, u32[]{:S(2)}) collective-permute-start(bf16[64,256]{1,0:T(8,128)(2,1)S(1)} %dynamic_slice.22), channel_id=1, source_target_pairs={{0,0},{1,16},{2,32},{3,48},{4,64},{5,80},{6,96},{7,112},{8,2},{9,1... | collective-permute-start | bytes 98312 | tf_op jit(solution)/shard_map/ppermute | solution.py:160
  18.2 0.8 dynamic-slice.1
  19.0 0.8 convert_multiply_fusion.3
  19.8 8.6 %collective-permute-start.1 = (f32[64,256]{1,0:T(8,128)S(1)}, f32[64,256]{1,0:T(8,128)S(1)}, u32[]{:S(2)}, u32[]{:S(2)}) collective-permute-start(f32[64,256]{1,0:T(8,128)S(1)} %convert_multiply_fusion.3), channel_id=1, source_target_pairs={{0,0},{1,16},{2,32},{3,48},{4,64},{5,80},{6,96},{7,112},{8,2},{9,1... | collective-permute-start | bytes 196616 | tf_op jit(solution)/shard_map/ppermute | solution.py:162
  28.4 0.1 constant_dynamic-slice_fusion
  28.4 0.1 copy.15
  28.5 0.1 copy.16
  28.6 0.1 fusion.15
  28.7 0.1 copy.17
  28.8 1.1 bitcast_convert_fusion
  30.0 1.8 select_reduce_fusion
  31.7 0.9 copy.18
  32.7 0.1 copy.24
  32.8 0.0 collective-permute-done.residual_ref
  32.8 0.9 collective-permute-done.1.scaled_ref
  33.7 76.1 %all-gather.3.cloned.1.call-done = bf16[1,2048,1792]{2,1,0:T(8,128)(2,1)} async-done(((bf16[1,128,1792]{2,1,0:T(8,128)(2,1)}), bf16[1,2048,1792]{2,1,0:T(8,128)(2,1)}) %all-gather.3.cloned.1.call-update) | async-done | bytes 7340048 | tf_op jit(solution)/shard_map/all_gather | solution.py:146
  109.9 3.1 %copy-done.1 = bf16[1,2048,1792]{2,1,0:T(8,128)(2,1)S(1)} copy-done((bf16[1,2048,1792]{2,1,0:T(8,128)(2,1)S(1)}, bf16[1,2048,1792]{2,1,0:T(8,128)(2,1)}, u32[]{:S(2)}) %copy-start.1) | copy-done | bytes 7340056
  112.9 3.3 %forward_matmul.1 = bf16[2048,256]{1,0:T(8,128)(2,1)S(1)} custom-call(bf16[2048,1792]{1,0:T(8,128)(2,1)S(1)} %bitcast.87, bf16[1792,256]{1,0:T(8,128)(2,1)S(1)} %bitcast.92, bf16[64,256]{1,0:T(8,128)(2,1)S(1)} %collective-permute-done.residual_ref, f32[64,256]{1,0:T(8,128)S(1)} %collective-permute-done.1.scaled_ref), custom_call_target="tpu_custom_call" | custom-call | flops 1879048192 | bytes 7340032 | tf_op jit(solution)/shard_map/forward_matmul/pallas_call | solution.py:50
  116.3 21.6 %all_to_all.15 = bf16[32,64,256]{2,1,0:T(8,128)(2,1)S(1)} all-to-all(bf16[32,64,256]{2,1,0:T(8,128)(2,1)S(1)} %bitcast.91), channel_id=1, replica_groups=mesh['section'=4,'dp'=16,'tensor'=8] {'section','tensor'}, dimensions={0} | all-to-all | bytes 2097152 | tf_op jit(solution)/shard_map/all_to_all | solution.py:165
  137.9 0.2 convert_reduce_fusion
  138.1 0.1 fusion
  138.2 0.1 pad_maximum_fusion.2
  138.3 20.7 %all_to_all.16 = f32[16,1,128]{2,1,0:T(1,128)S(1)} all-to-all(f32[16,1,128]{2,1,0:T(1,128)S(1)} %broadcast_in_dim.51), channel_id=1, replica_groups=mesh['section'=4,'dp'=16,'tensor'=8] {'dp'}, dimensions={0} | all-to-all | bytes 16384 | tf_op jit(solution)/shard_map/all_to_all | solution.py:178
  159.0 0.1 add_rsqrt_fusion
  159.0 0.1 fusion.4
  159.1 1.1 broadcast_in_dim.52
  160.2 7.9 %all-to-all-start.2 = ((bf16[32,64,256]{2,1,0:T(8,128)(2,1)}), bf16[32,64,256]{2,1,0:T(8,128)(2,1)S(1)}, u32[]{:S(2)}, u32[]{:S(2)}) async-start(bf16[32,64,256]{2,1,0:T(8,128)(2,1)} %broadcast_in_dim.52), calls=%async_computation.2 | async-start | bytes 2097152 | tf_op jit(solution)/shard_map/all_to_all | solution.py:186
  168.3 0.5 iota_reduce_fusion
  168.8 0.7 pad_maximum_fusion.stacked_ref
  169.5 13.4 %all-to-all-done.2 = bf16[32,64,256]{2,1,0:T(8,128)(2,1)S(1)} async-done(((bf16[32,64,256]{2,1,0:T(8,128)(2,1)}), bf16[32,64,256]{2,1,0:T(8,128)(2,1)S(1)}, u32[]{:S(2)}, u32[]{:S(2)}) %all-to-all-start.2) | async-done | bytes 1048608 | tf_op jit(solution)/shard_map/all_to_all | solution.py:186
  182.9 1.0 copy-done.3
  183.9 1.6 turn_sections.1
  185.5 0.8 slice_bitcast_fusion.7
  186.3 3.7 %collective-permute-start.2 = (bf16[64,256]{1,0:T(8,128)(2,1)S(1)}, bf16[64,256]{1,0:T(8,128)(2,1)S(1)}, u32[]{:S(2)}, u32[]{:S(2)}) collective-permute-start(bf16[64,256]{1,0:T(8,128)(2,1)S(1)} %get-tuple-element.15), channel_id=1, source_target_pairs={{0,0},{1,256},{2,8},{3,264},{4,16},{5,272},{6,24},{7,280},{8,128},... | collective-permute-start | bytes 98312 | tf_op jit(solution)/shard_map/ppermute | solution.py:196
  190.1 9.6 %collective-permute-start.5 = (bf16[64,256]{1,0:T(8,128)(2,1)S(1)}, bf16[64,256]{1,0:T(8,128)(2,1)S(1)}, u32[]{:S(2)}, u32[]{:S(2)}) collective-permute-start(bf16[64,256]{1,0:T(8,128)(2,1)S(1)} %get-tuple-element.16), channel_id=1, source_target_pairs={{0,384},{1,128},{2,392},{3,136},{4,400},{5,144},{6,408},{7,152},{8... | collective-permute-start | bytes 98312 | tf_op jit(solution)/shard_map/ppermute | solution.py:196
  199.7 10.6 %collective-permute-start.4 = (bf16[64,256]{1,0:T(8,128)(2,1)S(1)}, bf16[64,256]{1,0:T(8,128)(2,1)S(1)}, u32[]{:S(2)}, u32[]{:S(2)}) collective-permute-start(bf16[64,256]{1,0:T(8,128)(2,1)S(1)} %get-tuple-element.17), channel_id=1, source_target_pairs={{0,256},{1,0},{2,264},{3,8},{4,272},{5,16},{6,280},{7,24},{8,384},... | collective-permute-start | bytes 98312 | tf_op jit(solution)/shard_map/ppermute | solution.py:196
  210.2 8.3 %collective-permute-start.3 = (bf16[64,256]{1,0:T(8,128)(2,1)S(1)}, bf16[64,256]{1,0:T(8,128)(2,1)S(1)}, u32[]{:S(2)}, u32[]{:S(2)}) collective-permute-start(bf16[64,256]{1,0:T(8,128)(2,1)S(1)} %get-tuple-element.18), channel_id=1, source_target_pairs={{0,128},{1,384},{2,136},{3,392},{4,144},{5,400},{6,152},{7,408},{8... | collective-permute-start | bytes 98312 | tf_op jit(solution)/shard_map/ppermute | solution.py:196
  218.5 3.1 %copy-done.2 = bf16[1,2048,1792]{2,1,0:T(8,128)(2,1)S(1)} copy-done((bf16[1,2048,1792]{2,1,0:T(8,128)(2,1)S(1)}, bf16[1,2048,1792]{2,1,0:T(8,128)(2,1)}, u32[]{:S(2)}) %copy-start.2) | copy-done | bytes 7340056
  221.6 1.2 copy-done.4
  222.8 6.6 %gradient_matmul.1 = bf16[2,7,128,128]{3,2,1,0:T(8,128)(2,1)} custom-call(s32[2,14]{1,0:T(2,128)S(1)} %select_bitcast_fusion.slot_ref, bf16[2048,256]{1,0:T(8,128)(2,1)S(1)} %bitcast.90, bf16[2048,1792]{1,0:T(8,128)(2,1)S(1)} %bitcast.88), custom_call_target="tpu_custom_call" | custom-call | flops 1879048192 | bytes 7340032 | tf_op jit(solution)/shard_map/gradient_matmul/pallas_call | solution.py:94
  229.4 0.0 collective-permute-done.2
  229.4 0.0 collective-permute-done.5
  229.4 0.0 collective-permute-done.4
  229.5 0.7 maximum_bitcast_fusion
  (13 shorter events, 0.1 us)
Async XLA Ops:
  7.2 21.2 %copy-start = (s32[1,1,32,7]{2,1,3,0:T(1,128)S(1)}, s32[1,1,32,7]{2,1,3,0:T(1,128)}, u32[]{:S(2)}) copy-start(s32[1,1,32,7]{2,1,3,0:T(1,128)} %param.9) | copy-start | bytes 2692
  7.2 102.7 %all-gather.3.cloned.1.call-start = ((), (), s32[]{:S(2)}) async-start(), calls=%async_computation.3 | async-start | bytes 7798784 | tf_op jit(solution)/shard_map/all_gather | solution.py:146
  8.7 24.1 %collective-permute-start = (bf16[64,256]{1,0:T(8,128)(2,1)S(1)}, bf16[64,256]{1,0:T(8,128)(2,1)S(1)}, u32[]{:S(2)}, u32[]{:S(2)}) collective-permute-start(bf16[64,256]{1,0:T(8,128)(2,1)S(1)} %dynamic_slice.22), channel_id=1, source_target_pairs={{0,0},{1,16},{2,32},{3,48},{4,64},{5,80},{6,96},{7,112},{8,2},{9,1... | collective-permute-start | bytes 98312 | tf_op jit(solution)/shard_map/ppermute | solution.py:160
  19.8 14.0 %collective-permute-start.1 = (f32[64,256]{1,0:T(8,128)S(1)}, f32[64,256]{1,0:T(8,128)S(1)}, u32[]{:S(2)}, u32[]{:S(2)}) collective-permute-start(f32[64,256]{1,0:T(8,128)S(1)} %convert_multiply_fusion.3), channel_id=1, source_target_pairs={{0,0},{1,16},{2,32},{3,48},{4,64},{5,80},{6,96},{7,112},{8,2},{9,1... | collective-permute-start | bytes 196616 | tf_op jit(solution)/shard_map/ppermute | solution.py:162
  109.9 3.1 %copy-start.1 = (bf16[1,2048,1792]{2,1,0:T(8,128)(2,1)S(1)}, bf16[1,2048,1792]{2,1,0:T(8,128)(2,1)}, u32[]{:S(2)}) copy-start(bf16[1,2048,1792]{2,1,0:T(8,128)(2,1)} %all-gather.3.cloned.1.call-done) | copy-start | bytes 22020100
  160.2 22.7 %all-to-all-start.2 = ((bf16[32,64,256]{2,1,0:T(8,128)(2,1)}), bf16[32,64,256]{2,1,0:T(8,128)(2,1)S(1)}, u32[]{:S(2)}, u32[]{:S(2)}) async-start(bf16[32,64,256]{2,1,0:T(8,128)(2,1)} %broadcast_in_dim.52), calls=%async_computation.2 | async-start | bytes 2097152 | tf_op jit(solution)/shard_map/all_to_all | solution.py:186
  182.9 1.0 copy-start.3
  186.3 43.1 %collective-permute-start.2 = (bf16[64,256]{1,0:T(8,128)(2,1)S(1)}, bf16[64,256]{1,0:T(8,128)(2,1)S(1)}, u32[]{:S(2)}, u32[]{:S(2)}) collective-permute-start(bf16[64,256]{1,0:T(8,128)(2,1)S(1)} %get-tuple-element.15), channel_id=1, source_target_pairs={{0,0},{1,256},{2,8},{3,264},{4,16},{5,272},{6,24},{7,280},{8,128},... | collective-permute-start | bytes 98312 | tf_op jit(solution)/shard_map/ppermute | solution.py:196
  190.1 39.4 %collective-permute-start.5 = (bf16[64,256]{1,0:T(8,128)(2,1)S(1)}, bf16[64,256]{1,0:T(8,128)(2,1)S(1)}, u32[]{:S(2)}, u32[]{:S(2)}) collective-permute-start(bf16[64,256]{1,0:T(8,128)(2,1)S(1)} %get-tuple-element.16), channel_id=1, source_target_pairs={{0,384},{1,128},{2,392},{3,136},{4,400},{5,144},{6,408},{7,152},{8... | collective-permute-start | bytes 98312 | tf_op jit(solution)/shard_map/ppermute | solution.py:196
  199.7 29.8 %collective-permute-start.4 = (bf16[64,256]{1,0:T(8,128)(2,1)S(1)}, bf16[64,256]{1,0:T(8,128)(2,1)S(1)}, u32[]{:S(2)}, u32[]{:S(2)}) collective-permute-start(bf16[64,256]{1,0:T(8,128)(2,1)S(1)} %get-tuple-element.17), channel_id=1, source_target_pairs={{0,256},{1,0},{2,264},{3,8},{4,272},{5,16},{6,280},{7,24},{8,384},... | collective-permute-start | bytes 98312 | tf_op jit(solution)/shard_map/ppermute | solution.py:196
  210.2 19.2 %collective-permute-start.3 = (bf16[64,256]{1,0:T(8,128)(2,1)S(1)}, bf16[64,256]{1,0:T(8,128)(2,1)S(1)}, u32[]{:S(2)}, u32[]{:S(2)}) collective-permute-start(bf16[64,256]{1,0:T(8,128)(2,1)S(1)} %get-tuple-element.18), channel_id=1, source_target_pairs={{0,128},{1,384},{2,136},{3,392},{4,144},{5,400},{6,152},{7,408},{8... | collective-permute-start | bytes 98312 | tf_op jit(solution)/shard_map/ppermute | solution.py:196
  218.5 3.1 %copy-start.2 = (bf16[1,2048,1792]{2,1,0:T(8,128)(2,1)S(1)}, bf16[1,2048,1792]{2,1,0:T(8,128)(2,1)}, u32[]{:S(2)}) copy-start(bf16[1,2048,1792]{2,1,0:T(8,128)(2,1)} %all-gather.3.cloned.1.call-done) | copy-start | bytes 22020100
  221.6 1.2 copy-start.4
Sparse Core Ops, SparseCore 0:
  10.1 99.7 all-gather.2

commit v3 on v0

v3 whole, which is shorter than its diff:
```python
import jax
import jax.numpy as jnp
from jax import lax
from jax.experimental import pallas as pl
from jax.experimental.pallas import tpu as pltpu
from jax.sharding import PartitionSpec as P

D = 4096
PLANE = ("section", "tensor")
ALL = ("section", "dp", "tensor")
VMEM = 56 << 20
HALF = 4


def regroup(even, odd):
    upper = lax.broadcasted_iota(jnp.int32, even.shape, even.ndim - 2) < HALF
    axis = even.ndim - 2
    first = jnp.where(upper, even, pltpu.roll(odd, HALF, axis))
    second = jnp.where(upper, pltpu.roll(even, HALF, axis), odd)
    return first, second


def call(kernel, name, flops, moved, **kwargs):
    return pl.pallas_call(
        kernel,
        compiler_params=pltpu.CompilerParams(vmem_limit_bytes=VMEM),
        cost_estimate=pl.CostEstimate(flops=flops, bytes_accessed=moved, transcendentals=0),
        name=name,
        **kwargs,
    )


def forward_kernel(acts_ref, dense_ref, residual_ref, cot_ref, gain_ref, out_ref):
    found = jnp.dot(acts_ref[...], dense_ref[...], preferred_element_type=jnp.float32)
    rows = found.shape[0] // 4
    groups = [
        found[q * rows : (q + 1) * rows].reshape(rows // 8, 8, found.shape[1]) for q in range(4)
    ]
    left, right = regroup(*groups[:2]), regroup(*groups[2:])
    for parity in range(2):
        joined = jnp.concatenate([left[parity], right[parity]], axis=1)
        out_ref[:, parity] = joined.astype(out_ref.dtype)


def forward(every, dense, rows, after):
    tokens, units = every.shape
    width = dense.shape[1]
    groups = tokens // rows
    pairs = rows // 8
    out = call(
        forward_kernel,
        "forward_matmul",
        2 * tokens * units * width,
        2 * tokens * units,
        grid=(groups // 4,),
        in_specs=[
            pl.BlockSpec((4 * rows, units), lambda i: (i, 0)),
            pl.BlockSpec((units, width), lambda i: (0, 0)),
        ]
        + [pl.BlockSpec(memory_space=pl.ANY)] * 3,
        out_specs=pl.BlockSpec((pairs, 2, 16, width), lambda i: (0, 0, i, 0)),
        out_shape=jax.ShapeDtypeStruct((pairs, 2, HALF * groups, width), jnp.bfloat16),
    )(every, dense, *after)
    return out.reshape(2 * pairs, HALF * groups, width)


def cascade_kernel(parts_ref, residual_ref, cot_ref, gain_ref, out_ref, final_ref, scaled_ref):
    shards = parts_ref.shape[0] // 4
    rows, width = residual_ref.shape
    current = residual_ref[...].astype(jnp.float32)
    tiles = []
    for section in range(4):
        contrib = parts_ref[section * shards].astype(jnp.float32)
        for shard in range(1, shards):
            contrib += parts_ref[section * shards + shard].astype(jnp.float32)
        current = (current + contrib).astype(jnp.bfloat16).astype(jnp.float32)
        tiles.append(current.reshape(rows // 8, 8, width))
    scaled = cot_ref[...].astype(jnp.float32) * gain_ref[...]
    final_ref[...] = current
    scaled_ref[...] = scaled

    lane = lax.broadcasted_iota(jnp.int32, (rows, 128), 1)
    table = jnp.zeros((rows, 128), jnp.float32)
    for at, factor in enumerate((current, scaled)):
        left = jnp.sum(factor * current, axis=1, keepdims=True)
        for term in range(3):
            head = left.astype(jnp.bfloat16).astype(jnp.float32)
            table = jnp.where(lane == 3 * at + term, head, table)
            left = left - head
    table = jnp.concatenate([table, jnp.zeros((width - rows, 128), jnp.float32)], axis=0)
    sums = jnp.broadcast_to(table.T[None, :8], (rows // 8, 8, width))

    low, high = regroup(*tiles[:2]), regroup(*tiles[2:])
    for parity in range(2):
        joined = jnp.concatenate([low[parity], high[parity], sums], axis=1)
        out_ref[:, parity] = joined.astype(out_ref.dtype)


def cascade(parts, residual, cotangent, gain):
    rows, width = residual.shape
    half = jax.ShapeDtypeStruct((rows, width), jnp.float32)
    out, final, scaled = call(
        cascade_kernel,
        "cascade",
        parts.size,
        2 * parts.size,
        out_shape=(
            jax.ShapeDtypeStruct((rows // 8, 2, 24, width), jnp.bfloat16),
            half,
            half,
        ),
    )(parts, residual, cotangent, gain)
    return out.reshape(rows // 4, 24, width), final, scaled


def norm_kernel(got_ref, final_ref, scaled_ref, out_ref):
    planes = got_ref.shape[0]
    rows, width = final_ref.shape
    sums = got_ref[0, 16:24].astype(jnp.float32)
    for plane in range(1, planes):
        sums += got_ref[plane, 16:24].astype(jnp.float32)
    table = jnp.concatenate([sums, jnp.zeros((120, width), jnp.float32)], axis=0).T[:rows]
    lane = lax.broadcasted_iota(jnp.int32, table.shape, 1)
    square = jnp.sum(jnp.where(lane < 3, table, 0.0), axis=1, keepdims=True) / D
    mixed = jnp.sum(jnp.where(lane < 3, 0.0, table), axis=1, keepdims=True) / D
    inverse = lax.rsqrt(square + 1e-05)
    grad = inverse * (scaled_ref[...] - final_ref[...] * (inverse * inverse * mixed))

    shards = planes // 2
    spread = jnp.broadcast_to(grad[None], (shards, rows, width))
    pairs = got_ref[...].astype(jnp.float32).reshape(shards, 2, 24, width)
    for at in range(2):
        part = slice(8 * at, 8 * at + 8)
        for parity, tile in enumerate(regroup(pairs[:, 0, part], pairs[:, 1, part])):
            joined = jnp.concatenate([spread, tile], axis=1)
            out_ref[2 * at + parity] = joined.astype(out_ref.dtype)


def norm(got, final, scaled):
    rows, width = final.shape
    shards = got.shape[0] // 2
    out = call(
        norm_kernel,
        "norm_gradient",
        got.size,
        4 * got.size,
        out_shape=jax.ShapeDtypeStruct((4, shards, rows + 8, width), jnp.bfloat16),
    )(got, final, scaled)
    return out.reshape(4 * shards, rows + 8, width)


def gradient_kernel(slot_ref, full_ref, acts_ref, out_ref, section_ref, turned_ref):
    step = pl.program_id(0)
    cols, keep, blk, _ = out_ref.shape
    pairs, _, rows, width = full_ref.shape

    @pl.when(step == 0)
    def _():
        def tiles(at):
            even = full_ref[:, 0, at : at + 8].astype(jnp.float32)
            odd = full_ref[:, 1, at : at + 8].astype(jnp.float32)
            return [t.reshape(pairs * 8, width) for t in regroup(even, odd)]

        for two in range((rows - 8) // 8):
            for parity, tile in enumerate(tiles(8 * two)):
                at = (2 * two + parity) * pairs * 8
                turned_ref[:, at : at + pairs * 8] = tile.T.astype(turned_ref.dtype)
        for parity, tile in enumerate(tiles(rows - 8)):
            section_ref[:, parity * width : (parity + 1) * width] = tile.astype(section_ref.dtype)

    per_step = acts_ref.shape[1] // blk
    found = jnp.dot(turned_ref[...], acts_ref[...], preferred_element_type=jnp.float32)
    for part in range(per_step):
        for c in range(cols):
            slot = slot_ref[c, step * per_step + part]

            @pl.when(slot >= 0)
            def _(part=part, c=c, slot=slot):
                block = found[c * blk : (c + 1) * blk, part * blk : (part + 1) * blk]
                out_ref[c, slot] = block.T.astype(out_ref.dtype)


def gradient(slots, full, every, keep, blk):
    tokens, units = every.shape
    devices, rows, width = full.shape
    cols = width // blk
    per_step = 2
    return call(
        gradient_kernel,
        "gradient_matmul",
        2 * tokens * units * width,
        2 * tokens * units,
        grid_spec=pltpu.PrefetchScalarGridSpec(
            num_scalar_prefetch=1,
            grid=(units // (per_step * blk),),
            in_specs=[
                pl.BlockSpec((devices // 2, 2, rows, width), lambda i, _: (0, 0, 0, 0)),
                pl.BlockSpec((tokens, per_step * blk), lambda i, _: (0, i)),
            ],
            out_specs=[
                pl.BlockSpec((cols, keep, blk, blk), lambda i, _: (0, 0, 0, 0)),
                pl.BlockSpec((devices * HALF, 2 * width), lambda i, _: (0, 0)),
            ],
            scratch_shapes=[pltpu.VMEM((width, tokens), jnp.bfloat16)],
        ),
        out_shape=(
            jax.ShapeDtypeStruct((cols, keep, blk, blk), jnp.bfloat16),
            jax.ShapeDtypeStruct((devices * HALF, 2 * width), jnp.bfloat16),
        ),
    )(slots, full.reshape(devices // 2, 2, rows, width), every)


def exchange(value, axes):
    return lax.all_to_all(value, axes, split_axis=0, concat_axis=0, tiled=True)


def body(hidden, residual_in, weights, kept, cotangent, norm_gain):
    ns, nz, nt = (lax.axis_size(a) for a in ALL)
    section, plane = lax.axis_index("section"), lax.axis_index("dp")
    acts = hidden[0]
    rows = acts.shape[0]
    blocks = weights[0, 0]
    cols, keep, blk, _ = blocks.shape
    width = cols * blk
    hidden_blocks = acts.shape[1] // blk
    every = lax.all_gather(acts, "dp", axis=0, tiled=True)

    own_kept = lax.dynamic_slice_in_dim(kept[0, 0], plane * cols, cols, axis=0)
    hit = own_kept[None] == jnp.arange(hidden_blocks, dtype=own_kept.dtype)[:, None, None]
    dense = jnp.sum(
        jnp.where(hit[..., None, None], blocks[None].astype(jnp.float32), 0.0), axis=2
    ).astype(jnp.bfloat16)
    dense = dense.transpose(0, 2, 1, 3).reshape(hidden_blocks * blk, width)
    slots = jnp.where(jnp.any(hit, axis=2), jnp.argmax(hit, axis=2), -1).T.astype(jnp.int32)

    both = jnp.stack([residual_in, cotangent])
    piece = both.shape[2] // ns
    both = lax.dynamic_slice_in_dim(both, section * piece, piece, axis=2)
    both = both.reshape(2, ns * nt, HALF, piece).transpose(1, 0, 2, 3)
    both = exchange(both.reshape(ns * nt, 2 * HALF, piece), PLANE)
    both = both.reshape(2, 2, nt, 2 * HALF, piece).transpose(2, 0, 3, 1, 4)
    both = exchange(both.reshape(nz, 2 * HALF, width), "dp")
    both = both.reshape(nz, 2, HALF, width).transpose(1, 0, 2, 3).reshape(2, nz * HALF, width)
    residual, cot = both[0], both[1]
    gain = lax.all_gather(norm_gain, "tensor", axis=0, tiled=True)
    gain = lax.dynamic_slice_in_dim(gain, plane * width, width).reshape(1, width)

    partial_out = forward(every, dense, rows, (residual, cot, gain))
    parts = exchange(partial_out, PLANE)
    sent, final, scaled = cascade(parts, residual, cot, gain)
    spread = norm(exchange(sent, "dp"), final, scaled)
    grads, section_out = gradient(slots, exchange(spread, PLANE), every, keep, blk)
    return (section_out[None], grads[None, None])


def solution(mesh):
    in_specs = (
        P("section", "dp", "tensor"),
        P("dp", "tensor"),
        P("section", "tensor", "dp", None, None, None),
        P("section", "tensor", None, None),
        P("dp", "tensor"),
        P("tensor"),
    )
    out_specs = (P("section", "dp", "tensor"), P("section", "tensor", "dp", None, None, None))
    return jax.shard_map(body, mesh=mesh, in_specs=in_specs, out_specs=out_specs, check_vma=False)
```

time: 598 us -> 215 us (0.36)
  waiting for transfers between devices: 488 us -> 78.5 us
  blocking collectives: 18.3 us -> 58 us
  Pallas kernels: 0 us -> 20.4 us
  matrix products: 17.9 us -> 0 us
  local copies, waits for them, and re-layouts: 21.9 us -> 6.69 us
  other arithmetic: 11 us -> 4.88 us
    all_to_all x1 -> x3, waiting for transfers between devices: 316 us -> 22.5 us  [exchange(): return lax.all_to_all(value, axes, split_axis=0, concat_axis=0, tiled=True)]
    all_gather x2 -> x1, waiting for transfers between devices: 115 us -> 55.3 us  [body(): every = lax.all_gather(acts, 'dp', axis=0, tiled=True)]
    all_to_all x0 -> x2, blocking collectives: none -> 46.3 us  [exchange(): return lax.all_to_all(value, axes, split_axis=0, concat_axis=0, tiled=True)]
    reduce_scatter x1 -> x0, waiting for transfers between devices: 35.8 us -> none  [body(): lax.psum_scatter(partial_out.astype(jnp.bfloat16), 'tensor', scatter_dime...]
    ppermute x6 -> x0, waiting for transfers between devices: 20.5 us -> none  [shifted(): lax.ppermute(value, axis, [(source, source + steps) for source in range(i...]
    pallas_call x0 -> x4, Pallas kernels: none -> 20.4 us  [the longest x1 9.73 us: gradient(): call(gradient_kernel, 'gradient_matmul', 2 * tokens * units * width, 2 *...]
    gather x2 -> x0, local copies, waits for them, and re-layouts: 19.1 us -> none  [body(): jnp.take(acts.reshape(row_count, -1, block_size), kept_table, axis=1)]
    all_to_all x1 -> x3, starting transfers between devices: 11.9 us -> 30.7 us  [exchange(): return lax.all_to_all(value, axes, split_axis=0, concat_axis=0, tiled=True)]
  transfers between devices with their start and end apart: 10 -> 4, of which waited for: 10 -> 3; matrix products, arithmetic and copies ran while one was open for 4% -> 5% of each run, Pallas kernels for 0% -> 0%
where the time goes in v3:
time: 215 us; the launch traced here: 213 us
  waiting for transfers between devices  78.5 us (37%)
  blocking collectives  58 us (27%)
  starting transfers between devices  30.7 us (14%)
  Pallas kernels  20.4 us (9%)
  between operations  14.1 us (7%)
  local copies, waits for them, and re-layouts  6.69 us (3%)
  other arithmetic  4.88 us (2%)
    all_gather x1, waiting for transfers between devices, body(): every = lax.all_gather(acts, 'dp', axis=0, tiled=True)  55.3 us
    all_to_all x2, blocking collectives, exchange(): return lax.all_to_all(value, axes, split_axis=0, concat_axis=0, tiled=True)  46.3 us
    all_to_all x3, starting transfers between devices, exchange(): return lax.all_to_all(value, axes, split_axis=0, concat_axis=0, tiled=True)  30.7 us
    all_to_all x3, waiting for transfers between devices, exchange(): return lax.all_to_all(value, axes, split_axis=0, concat_axis=0, tiled=True)  22.5 us
    all_gather x1, blocking collectives, body(): gain = lax.all_gather(norm_gain, 'tensor', axis=0, tiled=True)  11.7 us
    pallas_call x1, Pallas kernels, gradient(): call(gradient_kernel, 'gradient_matmul', 2 * tokens * units * width, 2 *...  9.73 us
    pallas_call x1, Pallas kernels, forward(): call(forward_kernel, 'forward_matmul', 2 * tokens * units * width, 2 * to...  6.17 us
  transfers between devices with their start and end apart: 4, of which 3 were waited for; matrix products, arithmetic and copies ran while one was open for 5% of the time, Pallas kernels for 0%

profile of v3, /device:TPU:1, one launch (start us, length us, event | category | flops | bytes accessed | tf_op | source)
XLA Modules:
  0.0 213.4 jit_solution(9082419572336364484)
XLA Ops:
  7.2 0.0 copy-start
  7.2 0.0 copy-start.2
  7.2 0.0 all-gather.4.cloned.1.call-start
  7.2 0.7 all-gather.4.cloned.1.call-update
  7.9 0.8 fusion
  8.7 0.7 copy.44
  9.4 10.4 %all-to-all-start = ((bf16[32,8,128]{2,1,0:T(8,128)(2,1)}), bf16[32,8,128]{2,1,0:T(8,128)(2,1)S(1)}, u32[]{:S(2)}, u32[]{:S(2)}) async-start(bf16[32,8,128]{2,1,0:T(8,128)(2,1)} %copy.44), calls=%async_computation | async-start | bytes 131072 | tf_op jit(solution)/shard_map/all_to_all | solution.py:214
  19.8 0.0 copy-done
  19.8 0.1 constant_dynamic-slice_fusion
  19.9 0.1 copy.38
  20.0 0.1 copy.39
  20.1 1.1 bitcast_convert_fusion
  21.2 0.1 fusion.1
  21.3 0.1 copy.41
  21.4 5.8 %all-to-all-done = bf16[32,8,128]{2,1,0:T(8,128)(2,1)S(1)} async-done(((bf16[32,8,128]{2,1,0:T(8,128)(2,1)}), bf16[32,8,128]{2,1,0:T(8,128)(2,1)S(1)}, u32[]{:S(2)}, u32[]{:S(2)}) %all-to-all-start) | async-done | bytes 65568 | tf_op jit(solution)/shard_map/all_to_all | solution.py:214
  27.2 0.6 copy.45
  27.9 13.0 %all-to-all-start.1 = ((bf16[16,8,256]{2,1,0:T(8,128)(2,1)}), bf16[16,8,256]{2,1,0:T(8,128)(2,1)S(1)}, u32[]{:S(2)}, u32[]{:S(2)}) async-start(bf16[16,8,256]{2,1,0:T(8,128)(2,1)} %bitcast.12), calls=%async_computation.1 | async-start | bytes 131072 | tf_op jit(solution)/shard_map/all_to_all | solution.py:214
  40.9 1.8 select_reduce_fusion
  42.7 0.9 copy.42
  43.6 1.0 copy.52
  44.7 0.0 copy-done.2
  44.7 11.7 %all-gather.1 = f32[8,1,512]{2,1,0:T(1,128)S(1)} all-gather(f32[1,1,512]{2,1,0:T(1,128)S(1)} %bitcast.56), channel_id=1, replica_groups=mesh['section'=4,'dp'=16,'tensor'=8] {'tensor'}, dimensions={0}, use_global_device_ids=true | all-gather | bytes 18432 | tf_op jit(solution)/shard_map/all_gather | solution.py:245
  56.4 0.6 dynamic_slice.11
  57.0 0.0 all-to-all-done.1
  57.1 0.6 squeeze.12.cot_ref
  57.7 0.6 squeeze.11.residual_ref
  58.3 55.3 %all-gather.4.cloned.1.call-done = bf16[1,2048,1792]{2,1,0:T(8,128)(2,1)} async-done(((bf16[1,128,1792]{2,1,0:T(8,128)(2,1)}), bf16[1,2048,1792]{2,1,0:T(8,128)(2,1)}) %all-gather.4.cloned.1.call-update) | async-done | bytes 7340048 | tf_op jit(solution)/shard_map/all_gather | solution.py:226
  113.7 6.2 %forward_matmul.1 = bf16[16,2,64,256]{3,2,1,0:T(8,128)(2,1)} custom-call(bf16[2048,1792]{1,0:T(8,128)(2,1)} %bitcast.37, bf16[1792,256]{1,0:T(8,128)(2,1)} %bitcast.42, bf16[64,256]{1,0:T(8,128)(2,1)} %squeeze.11.residual_ref, bf16[64,256]{1,0:T(8,128)(2,1)} %squeeze.12.cot_ref, f32[1,256]{1,0:T(1,128)} %bitcast.53), custom_call_target="tpu_custom_call" | custom-call | flops 1879048192 | bytes 7340032 | tf_op jit(solution)/shard_map/forward_matmul/pallas_call | solution.py:50
  119.8 24.8 %all_to_all.25.parts_ref = bf16[32,64,256]{2,1,0:T(8,128)(2,1)} all-to-all(bf16[32,64,256]{2,1,0:T(8,128)(2,1)} %bitcast.41), channel_id=1, replica_groups=mesh['section'=4,'dp'=16,'tensor'=8] {'section','tensor'}, dimensions={0} | all-to-all | bytes 2097152 | tf_op jit(solution)/shard_map/all_to_all | solution.py:214
  144.6 2.3 %cascade.1 = (bf16[8,2,24,256]{3,2,1,0:T(8,128)(2,1)}, f32[64,256]{1,0:T(8,128)}, f32[64,256]{1,0:T(8,128)}) custom-call(bf16[32,64,256]{2,1,0:T(8,128)(2,1)} %all_to_all.25.parts_ref, bf16[64,256]{1,0:T(8,128)(2,1)} %squeeze.11.residual_ref, bf16[64,256]{1,0:T(8,128)(2,1)} %squeeze.12.cot_ref, f32[1,256]{1,0:T(1,128)} %bitcast.54), custom_call_target="tpu_custom_call" | custom-call | flops 524288 | bytes 1048576 | tf_op jit(solution)/shard_map/cascade/pallas_call | solution.py:102
  146.9 21.5 %all_to_all.26.got_ref = bf16[16,24,256]{2,1,0:T(8,128)(2,1)} all-to-all(bf16[16,24,256]{2,1,0:T(8,128)(2,1)} %bitcast.49), channel_id=1, replica_groups=mesh['section'=4,'dp'=16,'tensor'=8] {'dp'}, dimensions={0} | all-to-all | bytes 393216 | tf_op jit(solution)/shard_map/all_to_all | solution.py:214
  168.4 2.3 %norm_gradient.1 = bf16[4,8,72,256]{3,2,1,0:T(8,128)(2,1)} custom-call(bf16[16,24,256]{2,1,0:T(8,128)(2,1)} %all_to_all.26.got_ref, f32[64,256]{1,0:T(8,128)} %get-tuple-element.10.final_ref, f32[64,256]{1,0:T(8,128)} %get-tuple-element.11.scaled_ref), custom_call_target="tpu_custom_call" | custom-call | flops 98304 | bytes 393216 | tf_op jit(solution)/shard_map/norm_gradient/pallas_call | solution.py:142
  170.7 7.3 %all-to-all-start.4 = ((bf16[32,72,256]{2,1,0:T(8,128)(2,1)}), bf16[32,72,256]{2,1,0:T(8,128)(2,1)S(1)}, u32[]{:S(2)}, u32[]{:S(2)}) async-start(bf16[32,72,256]{2,1,0:T(8,128)(2,1)} %bitcast.40), calls=%async_computation.4 | async-start | bytes 2359296 | tf_op jit(solution)/shard_map/all_to_all | solution.py:214
  178.0 0.5 iota_reduce_fusion
  178.6 0.6 select_bitcast_fusion.slot_ref
  179.1 16.7 %all-to-all-done.4 = bf16[32,72,256]{2,1,0:T(8,128)(2,1)S(1)} async-done(((bf16[32,72,256]{2,1,0:T(8,128)(2,1)}), bf16[32,72,256]{2,1,0:T(8,128)(2,1)S(1)}, u32[]{:S(2)}, u32[]{:S(2)}) %all-to-all-start.4) | async-done | bytes 1179680 | tf_op jit(solution)/shard_map/all_to_all | solution.py:214
  195.8 0.0 copy-start.1
  195.8 1.0 copy-done.1
  196.9 9.7 %gradient_matmul.1 = (bf16[2,7,128,128]{3,2,1,0:T(8,128)(2,1)}, bf16[128,512]{1,0:T(8,128)(2,1)}) custom-call(s32[2,14]{1,0:T(2,128)} %select_bitcast_fusion.slot_ref, bf16[16,2,72,256]{3,2,1,0:T(8,128)(2,1)} %bitcast.39, bf16[2048,1792]{1,0:T(8,128)(2,1)} %bitcast.38), custom_call_target="tpu_custom_call" | custom-call | flops 1879048192 | bytes 7340032 | tf_op jit(solution)/shard_map/gradient_matmul/pallas_call | solution.py:188
  (5 shorter events, 0.1 us)
Async XLA Ops:
  7.2 12.6 %copy-start = (s32[1,1,32,7]{2,1,3,0:T(1,128)S(1)}, s32[1,1,32,7]{2,1,3,0:T(1,128)}, u32[]{:S(2)}) copy-start(s32[1,1,32,7]{2,1,3,0:T(1,128)} %param.9) | copy-start | bytes 2692
  7.2 37.5 %copy-start.2 = (f32[512]{0:T(512)S(1)}, f32[512]{0:T(512)}, u32[]{:S(2)}) copy-start(f32[512]{0:T(512)} %param.11) | copy-start | bytes 6148
  7.2 106.5 %all-gather.4.cloned.1.call-start = ((), (), s32[]{:S(2)}) async-start(), calls=%async_computation.5 | async-start | bytes 7798784 | tf_op jit(solution)/shard_map/all_gather | solution.py:226
  9.4 17.8 %all-to-all-start = ((bf16[32,8,128]{2,1,0:T(8,128)(2,1)}), bf16[32,8,128]{2,1,0:T(8,128)(2,1)S(1)}, u32[]{:S(2)}, u32[]{:S(2)}) async-start(bf16[32,8,128]{2,1,0:T(8,128)(2,1)} %copy.44), calls=%async_computation | async-start | bytes 131072 | tf_op jit(solution)/shard_map/all_to_all | solution.py:214
  27.9 29.2 %all-to-all-start.1 = ((bf16[16,8,256]{2,1,0:T(8,128)(2,1)}), bf16[16,8,256]{2,1,0:T(8,128)(2,1)S(1)}, u32[]{:S(2)}, u32[]{:S(2)}) async-start(bf16[16,8,256]{2,1,0:T(8,128)(2,1)} %bitcast.12), calls=%async_computation.1 | async-start | bytes 131072 | tf_op jit(solution)/shard_map/all_to_all | solution.py:214
  170.7 25.1 %all-to-all-start.4 = ((bf16[32,72,256]{2,1,0:T(8,128)(2,1)}), bf16[32,72,256]{2,1,0:T(8,128)(2,1)S(1)}, u32[]{:S(2)}, u32[]{:S(2)}) async-start(bf16[32,72,256]{2,1,0:T(8,128)(2,1)} %bitcast.40), calls=%async_computation.4 | async-start | bytes 2359296 | tf_op jit(solution)/shard_map/all_to_all | solution.py:214
  195.8 1.0 copy-start.1
Sparse Core Ops, SparseCore 0:
  10.1 103.5 all-gather.3

commit v4 on v3

--- a/solution.py
+++ b/solution.py
@@ -8,7 +8,7 @@
 D = 4096
 PLANE = ("section", "tensor")
 ALL = ("section", "dp", "tensor")
-VMEM = 56 << 20
+MOST_VMEM = 56 << 20
 HALF = 4
 
 
@@ -20,17 +20,75 @@
     return first, second
 
 
-def call(kernel, name, flops, moved, **kwargs):
+def call(kernel, name, flops, moved, vmem=16 << 20, **kwargs):
     return pl.pallas_call(
         kernel,
-        compiler_params=pltpu.CompilerParams(vmem_limit_bytes=VMEM),
+        compiler_params=pltpu.CompilerParams(vmem_limit_bytes=vmem),
         cost_estimate=pl.CostEstimate(flops=flops, bytes_accessed=moved, transcendentals=0),
         name=name,
         **kwargs,
     )
 
 
-def forward_kernel(acts_ref, dense_ref, residual_ref, cot_ref, gain_ref, out_ref):
+def split_kernel(section_ref, residual_ref, cot_ref, gain_ref, out_ref):
+    rows, width = residual_ref.shape
+    shape = (rows // 8, 8, width)
+    scaled = cot_ref[...].astype(jnp.float32) * gain_ref[...]
+    tiles = regroup(residual_ref[...].astype(jnp.float32).reshape(shape), scaled.reshape(shape))
+    for parity in range(2):
+        out_ref[:, parity] = tiles[parity].astype(out_ref.dtype)
+
+
+def split(section, residual, cotangent, gain):
+    rows, width = residual.shape
+    part = width // lax.axis_size("section")
+    block = pl.BlockSpec((rows, part), lambda i, section: (0, section[0]))
+    out = call(
+        split_kernel,
+        "split_rows",
+        rows * part,
+        6 * rows * part,
+        grid_spec=pltpu.PrefetchScalarGridSpec(
+            num_scalar_prefetch=1,
+            grid=(1,),
+            in_specs=[
+                block,
+                block,
+                pl.BlockSpec((1, part), lambda i, section: (0, section[0])),
+            ],
+            out_specs=pl.BlockSpec((rows // 8, 2, 8, part), lambda i, section: (0, 0, 0, 0)),
+        ),
+        out_shape=jax.ShapeDtypeStruct((rows // 8, 2, 8, part), jnp.bfloat16),
+    )(section.astype(jnp.int32).reshape(1), residual, cotangent, gain.reshape(1, width))
+    return out.reshape(rows // 4, 8, part)
+
+
+def join_kernel(got_ref, out_ref):
+    part = got_ref.shape[2]
+    shards = out_ref.shape[0] // 2
+    for half in range(2):
+        for shard in range(shards):
+            for side in range(2):
+                tile = got_ref[(2 * half + side) * shards + shard]
+                out_ref[2 * shard + half, :, side * part : (side + 1) * part] = tile
+
+
+def join(got, planes):
+    _, rows, part = got.shape
+    shape = (planes, rows, 2 * part)
+    return call(
+        join_kernel,
+        "join_columns",
+        got.size,
+        4 * got.size,
+        grid=(1,),
+        in_specs=[pl.BlockSpec(got.shape, lambda i: (0, 0, 0))],
+        out_specs=pl.BlockSpec(shape, lambda i: (0, 0, 0)),
+        out_shape=jax.ShapeDtypeStruct(shape, got.dtype),
+    )(got)
+
+
+def forward_kernel(acts_ref, dense_ref, after_ref, out_ref):
     found = jnp.dot(acts_ref[...], dense_ref[...], preferred_element_type=jnp.float32)
     rows = found.shape[0] // 4
     groups = [
@@ -52,22 +110,24 @@
         "forward_matmul",
         2 * tokens * units * width,
         2 * tokens * units,
+        MOST_VMEM,
         grid=(groups // 4,),
         in_specs=[
             pl.BlockSpec((4 * rows, units), lambda i: (i, 0)),
             pl.BlockSpec((units, width), lambda i: (0, 0)),
         ]
-        + [pl.BlockSpec(memory_space=pl.ANY)] * 3,
+        + [pl.BlockSpec(memory_space=pl.ANY)],
         out_specs=pl.BlockSpec((pairs, 2, 16, width), lambda i: (0, 0, i, 0)),
         out_shape=jax.ShapeDtypeStruct((pairs, 2, HALF * groups, width), jnp.bfloat16),
-    )(every, dense, *after)
+    )(every, dense, after)
     return out.reshape(2 * pairs, HALF * groups, width)
 
 
-def cascade_kernel(parts_ref, residual_ref, cot_ref, gain_ref, out_ref, final_ref, scaled_ref):
+def cascade_kernel(parts_ref, start_ref, out_ref, final_ref, scaled_ref):
+    rows, width = final_ref.shape
     shards = parts_ref.shape[0] // 4
-    rows, width = residual_ref.shape
-    current = residual_ref[...].astype(jnp.float32)
+    start = start_ref[...].astype(jnp.float32).reshape(rows // 8, 2, 8, width)
+    current, scaled = (t.reshape(rows, width) for t in regroup(start[:, 0], start[:, 1]))
     tiles = []
     for section in range(4):
         contrib = parts_ref[section * shards].astype(jnp.float32)
@@ -75,7 +135,6 @@
             contrib += parts_ref[section * shards + shard].astype(jnp.float32)
         current = (current + contrib).astype(jnp.bfloat16).astype(jnp.float32)
         tiles.append(current.reshape(rows // 8, 8, width))
-    scaled = cot_ref[...].astype(jnp.float32) * gain_ref[...]
     final_ref[...] = current
     scaled_ref[...] = scaled
 
@@ -96,20 +155,16 @@
         out_ref[:, parity] = joined.astype(out_ref.dtype)
 
 
-def cascade(parts, residual, cotangent, gain):
-    rows, width = residual.shape
+def cascade(parts, start):
+    _, rows, width = parts.shape
     half = jax.ShapeDtypeStruct((rows, width), jnp.float32)
     out, final, scaled = call(
         cascade_kernel,
         "cascade",
         parts.size,
         2 * parts.size,
-        out_shape=(
-            jax.ShapeDtypeStruct((rows // 8, 2, 24, width), jnp.bfloat16),
-            half,
-            half,
-        ),
-    )(parts, residual, cotangent, gain)
+        out_shape=(jax.ShapeDtypeStruct((rows // 8, 2, 24, width), jnp.bfloat16), half, half),
+    )(parts, start)
     return out.reshape(rows // 4, 24, width), final, scaled
 
 
@@ -149,13 +204,25 @@
     return out.reshape(4 * shards, rows + 8, width)
 
 
-def gradient_kernel(slot_ref, full_ref, acts_ref, out_ref, section_ref, turned_ref):
+def gradient_kernel(
+    slot_ref, full_ref, acts_ref, out_ref, section_ref, turned_ref, held_ref, sems
+):
     step = pl.program_id(0)
     cols, keep, blk, _ = out_ref.shape
     pairs, _, rows, width = full_ref.shape
+    chunks, _, piece = held_ref.shape
+
+    def fetch(chunk):
+        start = pl.multiple_of(chunk * piece, piece)
+        return pltpu.make_async_copy(
+            acts_ref.at[:, pl.ds(start, piece)], held_ref.at[chunk], sems.at[chunk]
+        )
 
     @pl.when(step == 0)
     def _():
+        for chunk in range(chunks):
+            fetch(chunk).start()
+
         def tiles(at):
             even = full_ref[:, 0, at : at + 8].astype(jnp.float32)
             odd = full_ref[:, 1, at : at + 8].astype(jnp.float32)
@@ -168,8 +235,9 @@
         for parity, tile in enumerate(tiles(rows - 8)):
             section_ref[:, parity * width : (parity + 1) * width] = tile.astype(section_ref.dtype)
 
-    per_step = acts_ref.shape[1] // blk
-    found = jnp.dot(turned_ref[...], acts_ref[...], preferred_element_type=jnp.float32)
+    per_step = piece // blk
+    fetch(step).wait()
+    found = jnp.dot(turned_ref[...], held_ref[step], preferred_element_type=jnp.float32)
     for part in range(per_step):
         for c in range(cols):
             slot = slot_ref[c, step * per_step + part]
@@ -190,18 +258,23 @@
         "gradient_matmul",
         2 * tokens * units * width,
         2 * tokens * units,
+        MOST_VMEM,
         grid_spec=pltpu.PrefetchScalarGridSpec(
             num_scalar_prefetch=1,
             grid=(units // (per_step * blk),),
             in_specs=[
                 pl.BlockSpec((devices // 2, 2, rows, width), lambda i, _: (0, 0, 0, 0)),
-                pl.BlockSpec((tokens, per_step * blk), lambda i, _: (0, i)),
+                pl.BlockSpec(memory_space=pl.ANY),
             ],
             out_specs=[
                 pl.BlockSpec((cols, keep, blk, blk), lambda i, _: (0, 0, 0, 0)),
                 pl.BlockSpec((devices * HALF, 2 * width), lambda i, _: (0, 0)),
             ],
-            scratch_shapes=[pltpu.VMEM((width, tokens), jnp.bfloat16)],
+            scratch_shapes=[
+                pltpu.VMEM((width, tokens), jnp.bfloat16),
+                pltpu.VMEM((units // (per_step * blk), tokens, per_step * blk), every.dtype),
+                pltpu.SemaphoreType.DMA((units // (per_step * blk),)),
+            ],
         ),
         out_shape=(
             jax.ShapeDtypeStruct((cols, keep, blk, blk), jnp.bfloat16),
@@ -224,7 +297,6 @@
     width = cols * blk
     hidden_blocks = acts.shape[1] // blk
     every = lax.all_gather(acts, "dp", axis=0, tiled=True)
-
     own_kept = lax.dynamic_slice_in_dim(kept[0, 0], plane * cols, cols, axis=0)
     hit = own_kept[None] == jnp.arange(hidden_blocks, dtype=own_kept.dtype)[:, None, None]
     dense = jnp.sum(
@@ -233,21 +305,10 @@
     dense = dense.transpose(0, 2, 1, 3).reshape(hidden_blocks * blk, width)
     slots = jnp.where(jnp.any(hit, axis=2), jnp.argmax(hit, axis=2), -1).T.astype(jnp.int32)
 
-    both = jnp.stack([residual_in, cotangent])
-    piece = both.shape[2] // ns
-    both = lax.dynamic_slice_in_dim(both, section * piece, piece, axis=2)
-    both = both.reshape(2, ns * nt, HALF, piece).transpose(1, 0, 2, 3)
-    both = exchange(both.reshape(ns * nt, 2 * HALF, piece), PLANE)
-    both = both.reshape(2, 2, nt, 2 * HALF, piece).transpose(2, 0, 3, 1, 4)
-    both = exchange(both.reshape(nz, 2 * HALF, width), "dp")
-    both = both.reshape(nz, 2, HALF, width).transpose(1, 0, 2, 3).reshape(2, nz * HALF, width)
-    residual, cot = both[0], both[1]
-    gain = lax.all_gather(norm_gain, "tensor", axis=0, tiled=True)
-    gain = lax.dynamic_slice_in_dim(gain, plane * width, width).reshape(1, width)
-
-    partial_out = forward(every, dense, rows, (residual, cot, gain))
-    parts = exchange(partial_out, PLANE)
-    sent, final, scaled = cascade(parts, residual, cot, gain)
+    start = exchange(split(section, residual_in, cotangent, norm_gain), PLANE)
+    start = exchange(join(start, nz), "dp")
+    parts = exchange(forward(every, dense, rows, start), PLANE)
+    sent, final, scaled = cascade(parts, start)
     spread = norm(exchange(sent, "dp"), final, scaled)
     grads, section_out = gradient(slots, exchange(spread, PLANE), every, keep, blk)
     return (section_out[None], grads[None, None])

time: 215 us -> 211 us (0.981)
  blocking collectives: 58 us -> 45.9 us
  waiting for transfers between devices: 78.5 us -> 90.4 us
  Pallas kernels: 20.4 us -> 17.7 us
    all_gather x1 -> x0, blocking collectives: 11.7 us -> none  [body(): gain = lax.all_gather(norm_gain, 'tensor', axis=0, tiled=True)]
    all_to_all x3, waiting for transfers between devices: 22.5 us -> 30.6 us  [exchange(): return lax.all_to_all(value, axes, split_axis=0, concat_axis=0, tiled=True)]
    all_gather x1, waiting for transfers between devices: 55.3 us -> 59.1 us  [body(): every = lax.all_gather(acts, 'dp', axis=0, tiled=True)]
    unnamed x7 -> x15, local copies, waits for them, and re-layouts: 2.1 us -> 5.49 us
  transfers between devices with their start and end apart: 4 -> 4, of which waited for: 3 -> 4; matrix products, arithmetic and copies ran while one was open for 5% -> 3% of each run, Pallas kernels for 0% -> 1%
where the time goes in v4:
time: 211 us; the launch traced here: 210 us
  waiting for transfers between devices  90.4 us (43%)
  blocking collectives  45.9 us (22%)
  starting transfers between devices  30.7 us (15%)
  Pallas kernels  17.7 us (8%)
  between operations  14.1 us (7%)
  local copies, waits for them, and re-layouts  6.84 us (3%)
  other arithmetic  4.12 us (2%)
    all_gather x1, waiting for transfers between devices, body(): every = lax.all_gather(acts, 'dp', axis=0, tiled=True)  59.1 us
    all_to_all x2, blocking collectives, exchange(): return lax.all_to_all(value, axes, split_axis=0, concat_axis=0, tiled=True)  45.9 us
    all_to_all x3, starting transfers between devices, exchange(): return lax.all_to_all(value, axes, split_axis=0, concat_axis=0, tiled=True)  30.7 us
    all_to_all x3, waiting for transfers between devices, exchange(): return lax.all_to_all(value, axes, split_axis=0, concat_axis=0, tiled=True)  30.6 us
    pallas_call x1, Pallas kernels, gradient(): call(gradient_kernel, 'gradient_matmul', 2 * tokens * units * width, 2 *...  8.55 us
    pallas_call x1, Pallas kernels, forward(): call(forward_kernel, 'forward_matmul', 2 * tokens * units * width, 2 * to...  6.19 us
    unnamed x15, local copies, waits for them, and re-layouts  5.49 us
  transfers between devices with their start and end apart: 4, of which 4 were waited for; matrix products, arithmetic and copies ran while one was open for 3% of the time, Pallas kernels for 1%

profile of v4, /device:TPU:1, one launch (start us, length us, event | category | flops | bytes accessed | tf_op | source)
XLA Modules:
  0.0 209.9 jit_solution(4792801877551044597)
XLA Ops:
  7.2 0.0 copy-start
  7.2 0.0 all-gather.3.cloned.1.call-start
  7.2 0.7 all-gather.3.cloned.1.call-update
  7.9 0.0 copy-start.3
  7.9 0.9 copy-done.3
  8.8 0.0 copy-start.4
  8.8 0.9 copy-done.4
  9.7 0.0 copy-start.5
  9.7 0.7 copy-done.5
  10.4 0.7 split_rows.1
  11.1 10.4 %all-to-all-start = ((bf16[32,8,128]{2,1,0:T(8,128)(2,1)}), bf16[32,8,128]{2,1,0:T(8,128)(2,1)S(1)}, u32[]{:S(2)}, u32[]{:S(2)}) async-start(bf16[32,8,128]{2,1,0:T(8,128)(2,1)} %bitcast.7), calls=%async_computation | async-start | bytes 131072 | tf_op jit(solution)/shard_map/all_to_all | solution.py:287
  21.5 0.0 copy-done
  21.5 0.1 constant_dynamic-slice_fusion
  21.6 0.1 copy.10
  21.7 0.1 copy.11
  21.8 1.1 bitcast_convert_fusion
  22.9 0.1 fusion
  23.0 0.1 copy.13
  23.1 5.8 %all-to-all-done.got_ref = bf16[32,8,128]{2,1,0:T(8,128)(2,1)S(1)} async-done(((bf16[32,8,128]{2,1,0:T(8,128)(2,1)}), bf16[32,8,128]{2,1,0:T(8,128)(2,1)S(1)}, u32[]{:S(2)}, u32[]{:S(2)}) %all-to-all-start) | async-done | bytes 65568 | tf_op jit(solution)/shard_map/all_to_all | solution.py:287
  28.9 0.6 join_columns.1
  29.5 13.0 %all-to-all-start.1 = ((bf16[16,8,256]{2,1,0:T(8,128)(2,1)}), bf16[16,8,256]{2,1,0:T(8,128)(2,1)S(1)}, u32[]{:S(2)}, u32[]{:S(2)}) async-start(bf16[16,8,256]{2,1,0:T(8,128)(2,1)} %join_columns.1), calls=%async_computation.1 | async-start | bytes 131072 | tf_op jit(solution)/shard_map/all_to_all | solution.py:287
  42.6 1.8 select_reduce_fusion
  44.4 0.9 copy.14
  45.3 1.1 copy.18
  46.4 8.1 %all-to-all-done.1.after_ref.start_ref = bf16[16,8,256]{2,1,0:T(8,128)(2,1)S(1)} async-done(((bf16[16,8,256]{2,1,0:T(8,128)(2,1)}), bf16[16,8,256]{2,1,0:T(8,128)(2,1)S(1)}, u32[]{:S(2)}, u32[]{:S(2)}) %all-to-all-start.1) | async-done | bytes 65568 | tf_op jit(solution)/shard_map/all_to_all | solution.py:287
  54.5 0.0 copy-start.1
  54.5 59.1 %all-gather.3.cloned.1.call-done = bf16[1,2048,1792]{2,1,0:T(8,128)(2,1)} async-done(((bf16[1,128,1792]{2,1,0:T(8,128)(2,1)}), bf16[1,2048,1792]{2,1,0:T(8,128)(2,1)}) %all-gather.3.cloned.1.call-update) | async-done | bytes 7340048 | tf_op jit(solution)/shard_map/all_gather | solution.py:299
  113.7 0.0 copy-done.1
  113.7 6.2 %forward_matmul.1 = bf16[16,2,64,256]{3,2,1,0:T(8,128)(2,1)} custom-call(bf16[2048,1792]{1,0:T(8,128)(2,1)} %bitcast.26, bf16[1792,256]{1,0:T(8,128)(2,1)} %bitcast.30, bf16[16,8,256]{2,1,0:T(8,128)(2,1)} %copy-done.1), custom_call_target="tpu_custom_call" | custom-call | flops 1879048192 | bytes 7340032 | tf_op jit(solution)/shard_map/forward_matmul/pallas_call | solution.py:108
  119.8 24.7 %all_to_all.25.parts_ref = bf16[32,64,256]{2,1,0:T(8,128)(2,1)S(1)} all-to-all(bf16[32,64,256]{2,1,0:T(8,128)(2,1)} %bitcast.29), channel_id=1, replica_groups=mesh['section'=4,'dp'=16,'tensor'=8] {'section','tensor'}, dimensions={0} | all-to-all | bytes 2097152 | tf_op jit(solution)/shard_map/all_to_all | solution.py:287
  144.6 0.0 copy-start.2
  144.6 0.8 copy-done.2
  145.4 0.3 cascade.1
  145.7 21.2 %all_to_all.26.got_ref = bf16[16,24,256]{2,1,0:T(8,128)(2,1)S(1)} all-to-all(bf16[16,24,256]{2,1,0:T(8,128)(2,1)S(1)} %bitcast.24), channel_id=1, replica_groups=mesh['section'=4,'dp'=16,'tensor'=8] {'dp'}, dimensions={0} | all-to-all | bytes 393216 | tf_op jit(solution)/shard_map/all_to_all | solution.py:287
  167.0 1.3 norm_gradient.1
  168.3 7.3 %all-to-all-start.4 = ((bf16[32,72,256]{2,1,0:T(8,128)(2,1)}), bf16[32,72,256]{2,1,0:T(8,128)(2,1)S(1)}, u32[]{:S(2)}, u32[]{:S(2)}) async-start(bf16[32,72,256]{2,1,0:T(8,128)(2,1)} %bitcast.10), calls=%async_computation.4 | async-start | bytes 2359296 | tf_op jit(solution)/shard_map/all_to_all | solution.py:287
  175.6 0.5 iota_reduce_fusion
  176.1 0.6 select_bitcast_fusion.slot_ref
  176.7 16.7 %all-to-all-done.4 = bf16[32,72,256]{2,1,0:T(8,128)(2,1)S(1)} async-done(((bf16[32,72,256]{2,1,0:T(8,128)(2,1)}), bf16[32,72,256]{2,1,0:T(8,128)(2,1)S(1)}, u32[]{:S(2)}, u32[]{:S(2)}) %all-to-all-start.4) | async-done | bytes 1179680 | tf_op jit(solution)/shard_map/all_to_all | solution.py:287
  193.4 0.0 copy-start.6
  193.4 1.1 copy-done.6
  194.4 8.6 %gradient_matmul.1 = (bf16[2,7,128,128]{3,2,1,0:T(8,128)(2,1)}, bf16[128,512]{1,0:T(8,128)(2,1)}) custom-call(s32[2,14]{1,0:T(2,128)} %select_bitcast_fusion.slot_ref, bf16[16,2,72,256]{3,2,1,0:T(8,128)(2,1)} %bitcast.28, bf16[2048,1792]{1,0:T(8,128)(2,1)} %bitcast.27), custom_call_target="tpu_custom_call" | custom-call | flops 1879048192 | bytes 7340032 | tf_op jit(solution)/shard_map/gradient_matmul/pallas_call | solution.py:256
Async XLA Ops:
  7.2 14.3 %copy-start = (s32[1,1,32,7]{2,1,3,0:T(1,128)S(1)}, s32[1,1,32,7]{2,1,3,0:T(1,128)}, u32[]{:S(2)}) copy-start(s32[1,1,32,7]{2,1,3,0:T(1,128)} %param.9) | copy-start | bytes 2692
  7.2 106.5 %all-gather.3.cloned.1.call-start = ((), (), s32[]{:S(2)}) async-start(), calls=%async_computation.5 | async-start | bytes 7798784 | tf_op jit(solution)/shard_map/all_gather | solution.py:299
  7.9 0.9 copy-start.3
  8.8 0.9 copy-start.4
  9.7 0.7 copy-start.5
  11.1 17.8 %all-to-all-start = ((bf16[32,8,128]{2,1,0:T(8,128)(2,1)}), bf16[32,8,128]{2,1,0:T(8,128)(2,1)S(1)}, u32[]{:S(2)}, u32[]{:S(2)}) async-start(bf16[32,8,128]{2,1,0:T(8,128)(2,1)} %bitcast.7), calls=%async_computation | async-start | bytes 131072 | tf_op jit(solution)/shard_map/all_to_all | solution.py:287
  29.5 25.0 %all-to-all-start.1 = ((bf16[16,8,256]{2,1,0:T(8,128)(2,1)}), bf16[16,8,256]{2,1,0:T(8,128)(2,1)S(1)}, u32[]{:S(2)}, u32[]{:S(2)}) async-start(bf16[16,8,256]{2,1,0:T(8,128)(2,1)} %join_columns.1), calls=%async_computation.1 | async-start | bytes 131072 | tf_op jit(solution)/shard_map/all_to_all | solution.py:287
  54.5 59.2 %copy-start.1 = (bf16[16,8,256]{2,1,0:T(8,128)(2,1)}, bf16[16,8,256]{2,1,0:T(8,128)(2,1)S(1)}, u32[]{:S(2)}) copy-start(bf16[16,8,256]{2,1,0:T(8,128)(2,1)S(1)} %all-to-all-done.1.after_ref.start_ref) | copy-start | bytes 196612
  144.6 0.8 copy-start.2
  168.3 25.1 %all-to-all-start.4 = ((bf16[32,72,256]{2,1,0:T(8,128)(2,1)}), bf16[32,72,256]{2,1,0:T(8,128)(2,1)S(1)}, u32[]{:S(2)}, u32[]{:S(2)}) async-start(bf16[32,72,256]{2,1,0:T(8,128)(2,1)} %bitcast.10), calls=%async_computation.4 | async-start | bytes 2359296 | tf_op jit(solution)/shard_map/all_to_all | solution.py:287
  193.4 1.1 copy-start.6
Sparse Core Ops, SparseCore 0:
  10.1 103.5 all-gather.2

commit v5 on v4

--- a/solution.py
+++ b/solution.py
@@ -8,7 +8,6 @@
 D = 4096
 PLANE = ("section", "tensor")
 ALL = ("section", "dp", "tensor")
-MOST_VMEM = 56 << 20
 HALF = 4
 
 
@@ -88,16 +87,18 @@
     )(got)
 
 
-def forward_kernel(acts_ref, dense_ref, after_ref, out_ref):
-    found = jnp.dot(acts_ref[...], dense_ref[...], preferred_element_type=jnp.float32)
-    rows = found.shape[0] // 4
-    groups = [
-        found[q * rows : (q + 1) * rows].reshape(rows // 8, 8, found.shape[1]) for q in range(4)
-    ]
-    left, right = regroup(*groups[:2]), regroup(*groups[2:])
-    for parity in range(2):
-        joined = jnp.concatenate([left[parity], right[parity]], axis=1)
-        out_ref[:, parity] = joined.astype(out_ref.dtype)
+def forward_kernel(acts_ref, dense_ref, after_ref, out_ref, held_ref):
+    pairs, _, _, width = out_ref.shape
+    rows = 8 * pairs
+    for step in range(acts_ref.shape[0] // (4 * rows)):
+        acts = acts_ref[4 * step * rows : 4 * (step + 1) * rows]
+        held_ref[4 * step * rows : 4 * (step + 1) * rows] = acts
+        found = jnp.dot(acts, dense_ref[...], preferred_element_type=jnp.float32)
+        groups = [found[q * rows : (q + 1) * rows].reshape(pairs, 8, width) for q in range(4)]
+        left, right = regroup(*groups[:2]), regroup(*groups[2:])
+        for parity in range(2):
+            joined = jnp.concatenate([left[parity], right[parity]], axis=1)
+            out_ref[:, parity, 16 * step : 16 * (step + 1)] = joined.astype(out_ref.dtype)
 
 
 def forward(every, dense, rows, after):
@@ -105,22 +106,20 @@
     width = dense.shape[1]
     groups = tokens // rows
     pairs = rows // 8
-    out = call(
+    whole = pl.BlockSpec(memory_space=pltpu.VMEM)
+    out, held = call(
         forward_kernel,
         "forward_matmul",
         2 * tokens * units * width,
         2 * tokens * units,
-        MOST_VMEM,
-        grid=(groups // 4,),
-        in_specs=[
-            pl.BlockSpec((4 * rows, units), lambda i: (i, 0)),
-            pl.BlockSpec((units, width), lambda i: (0, 0)),
-        ]
-        + [pl.BlockSpec(memory_space=pl.ANY)],
-        out_specs=pl.BlockSpec((pairs, 2, 16, width), lambda i: (0, 0, i, 0)),
-        out_shape=jax.ShapeDtypeStruct((pairs, 2, HALF * groups, width), jnp.bfloat16),
+        in_specs=[whole, whole, pl.BlockSpec(memory_space=pl.ANY)],
+        out_specs=[whole, whole],
+        out_shape=(
+            jax.ShapeDtypeStruct((pairs, 2, HALF * groups, width), jnp.bfloat16),
+            pltpu.VMEM(every.shape, every.dtype),
+        ),
     )(every, dense, after)
-    return out.reshape(2 * pairs, HALF * groups, width)
+    return out.reshape(2 * pairs, HALF * groups, width), held
 
 
 def cascade_kernel(parts_ref, start_ref, out_ref, final_ref, scaled_ref):
@@ -204,83 +203,52 @@
     return out.reshape(4 * shards, rows + 8, width)
 
 
-def gradient_kernel(
-    slot_ref, full_ref, acts_ref, out_ref, section_ref, turned_ref, held_ref, sems
-):
-    step = pl.program_id(0)
+def gradient_kernel(kept_ref, full_ref, acts_ref, out_ref, section_ref, turned_ref, found_ref):
     cols, keep, blk, _ = out_ref.shape
     pairs, _, rows, width = full_ref.shape
-    chunks, _, piece = held_ref.shape
-
-    def fetch(chunk):
-        start = pl.multiple_of(chunk * piece, piece)
-        return pltpu.make_async_copy(
-            acts_ref.at[:, pl.ds(start, piece)], held_ref.at[chunk], sems.at[chunk]
-        )
-
-    @pl.when(step == 0)
-    def _():
-        for chunk in range(chunks):
-            fetch(chunk).start()
-
-        def tiles(at):
-            even = full_ref[:, 0, at : at + 8].astype(jnp.float32)
-            odd = full_ref[:, 1, at : at + 8].astype(jnp.float32)
-            return [t.reshape(pairs * 8, width) for t in regroup(even, odd)]
-
-        for two in range((rows - 8) // 8):
-            for parity, tile in enumerate(tiles(8 * two)):
-                at = (2 * two + parity) * pairs * 8
-                turned_ref[:, at : at + pairs * 8] = tile.T.astype(turned_ref.dtype)
-        for parity, tile in enumerate(tiles(rows - 8)):
-            section_ref[:, parity * width : (parity + 1) * width] = tile.astype(section_ref.dtype)
-
-    per_step = piece // blk
-    fetch(step).wait()
-    found = jnp.dot(turned_ref[...], held_ref[step], preferred_element_type=jnp.float32)
-    for part in range(per_step):
-        for c in range(cols):
-            slot = slot_ref[c, step * per_step + part]
-
-            @pl.when(slot >= 0)
-            def _(part=part, c=c, slot=slot):
-                block = found[c * blk : (c + 1) * blk, part * blk : (part + 1) * blk]
-                out_ref[c, slot] = block.T.astype(out_ref.dtype)
-
-
-def gradient(slots, full, every, keep, blk):
-    tokens, units = every.shape
+
+    def tiles(at):
+        even = full_ref[:, 0, at : at + 8].astype(jnp.float32)
+        odd = full_ref[:, 1, at : at + 8].astype(jnp.float32)
+        return [t.reshape(pairs * 8, width) for t in regroup(even, odd)]
+
+    for two in range((rows - 8) // 8):
+        for parity, tile in enumerate(tiles(8 * two)):
+            at = (2 * two + parity) * pairs * 8
+            turned_ref[:, at : at + pairs * 8] = tile.T.astype(turned_ref.dtype)
+    for parity, tile in enumerate(tiles(rows - 8)):
+        section_ref[:, parity * width : (parity + 1) * width] = tile.astype(section_ref.dtype)
+
+    found_ref[...] = jnp.dot(
+        turned_ref[...], acts_ref[...], preferred_element_type=jnp.float32
+    ).astype(found_ref.dtype)
+    for c in range(cols):
+        for slot in range(keep):
+            start = pl.multiple_of(kept_ref[c, slot] * blk, blk)
+            out_ref[c, slot] = found_ref[c * blk : (c + 1) * blk, pl.ds(start, blk)].T
+
+
+def gradient(own_kept, full, held, blk):
+    tokens, units = held.shape
     devices, rows, width = full.shape
-    cols = width // blk
-    per_step = 2
+    cols, keep = own_kept.shape
+    whole = pl.BlockSpec(memory_space=pltpu.VMEM)
     return call(
         gradient_kernel,
         "gradient_matmul",
         2 * tokens * units * width,
         2 * tokens * units,
-        MOST_VMEM,
-        grid_spec=pltpu.PrefetchScalarGridSpec(
-            num_scalar_prefetch=1,
-            grid=(units // (per_step * blk),),
-            in_specs=[
-                pl.BlockSpec((devices // 2, 2, rows, width), lambda i, _: (0, 0, 0, 0)),
-                pl.BlockSpec(memory_space=pl.ANY),
-            ],
-            out_specs=[
-                pl.BlockSpec((cols, keep, blk, blk), lambda i, _: (0, 0, 0, 0)),
-                pl.BlockSpec((devices * HALF, 2 * width), lambda i, _: (0, 0)),
-            ],
-            scratch_shapes=[
-                pltpu.VMEM((width, tokens), jnp.bfloat16),
-                pltpu.VMEM((units // (per_step * blk), tokens, per_step * blk), every.dtype),
-                pltpu.SemaphoreType.DMA((units // (per_step * blk),)),
-            ],
-        ),
+        in_specs=[pl.BlockSpec(memory_space=pltpu.SMEM), whole, whole],
+        out_specs=[whole, whole],
+        scratch_shapes=[
+            pltpu.VMEM((width, tokens), jnp.bfloat16),
+            pltpu.VMEM((width, units), jnp.bfloat16),
+        ],
         out_shape=(
             jax.ShapeDtypeStruct((cols, keep, blk, blk), jnp.bfloat16),
             jax.ShapeDtypeStruct((devices * HALF, 2 * width), jnp.bfloat16),
         ),
-    )(slots, full.reshape(devices // 2, 2, rows, width), every)
+    )(own_kept, full.reshape(devices // 2, 2, rows, width), held)
 
 
 def exchange(value, axes):
@@ -293,7 +261,7 @@
     acts = hidden[0]
     rows = acts.shape[0]
     blocks = weights[0, 0]
-    cols, keep, blk, _ = blocks.shape
+    cols, _, blk, _ = blocks.shape
     width = cols * blk
     hidden_blocks = acts.shape[1] // blk
     every = lax.all_gather(acts, "dp", axis=0, tiled=True)
@@ -303,14 +271,14 @@
         jnp.where(hit[..., None, None], blocks[None].astype(jnp.float32), 0.0), axis=2
     ).astype(jnp.bfloat16)
     dense = dense.transpose(0, 2, 1, 3).reshape(hidden_blocks * blk, width)
-    slots = jnp.where(jnp.any(hit, axis=2), jnp.argmax(hit, axis=2), -1).T.astype(jnp.int32)
 
     start = exchange(split(section, residual_in, cotangent, norm_gain), PLANE)
     start = exchange(join(start, nz), "dp")
-    parts = exchange(forward(every, dense, rows, start), PLANE)
+    partial_out, held = forward(every, dense, rows, start)
+    parts = exchange(partial_out, PLANE)
     sent, final, scaled = cascade(parts, start)
     spread = norm(exchange(sent, "dp"), final, scaled)
-    grads, section_out = gradient(slots, exchange(spread, PLANE), every, keep, blk)
+    grads, section_out = gradient(own_kept, exchange(spread, PLANE), held, blk)
     return (section_out[None], grads[None, None])
 
 

time: 211 us -> 202 us (0.957)
  blocking collectives: 45.9 us -> 71.4 us
  waiting for transfers between devices: 90.4 us -> 75 us
  Pallas kernels: 17.7 us -> 7.79 us
  starting transfers between devices: 30.7 us -> 23.4 us
    all_to_all x2 -> x3, blocking collectives: 45.9 us -> 71.4 us  [exchange(): return lax.all_to_all(value, axes, split_axis=0, concat_axis=0, tiled=True)]
    all_to_all x3 -> x2, waiting for transfers between devices: 30.6 us -> 15.2 us  [exchange(): return lax.all_to_all(value, axes, split_axis=0, concat_axis=0, tiled=True)]
    all_to_all x3 -> x2, starting transfers between devices: 30.7 us -> 23.4 us  [exchange(): return lax.all_to_all(value, axes, split_axis=0, concat_axis=0, tiled=True)]
    pallas_call x1, Pallas kernels: 8.55 us -> 3.81 us  [gradient(): call(gradient_kernel, 'gradient_matmul', 2 * tokens * units * width, 2 *...]
    pallas_call x1, Pallas kernels: 6.19 us -> 2.11 us  [forward(): call(forward_kernel, 'forward_matmul', 2 * tokens * units * width, 2 * to...]
    unnamed x15 -> x11, local copies, waits for them, and re-layouts: 5.49 us -> 5.7 us
  transfers between devices with their start and end apart: 4 -> 3, of which waited for: 4 -> 3; matrix products, arithmetic and copies ran while one was open for 3% -> 2% of each run, Pallas kernels for 1% -> 1%
where the time goes in v5:
time: 202 us; the launch traced here: 201 us
  waiting for transfers between devices  75 us (37%)
  blocking collectives  71.4 us (35%)
  starting transfers between devices  23.4 us (12%)
  between operations  14.1 us (7%)
  Pallas kernels  7.79 us (4%)
  local copies, waits for them, and re-layouts  6.82 us (3%)
  other arithmetic  2.92 us (1%)
    all_to_all x3, blocking collectives, exchange(): return lax.all_to_all(value, axes, split_axis=0, concat_axis=0, tiled=True)  71.4 us
    all_gather x1, waiting for transfers between devices, body(): every = lax.all_gather(acts, 'dp', axis=0, tiled=True)  59.1 us
    all_to_all x2, starting transfers between devices, exchange(): return lax.all_to_all(value, axes, split_axis=0, concat_axis=0, tiled=True)  23.4 us
    all_to_all x2, waiting for transfers between devices, exchange(): return lax.all_to_all(value, axes, split_axis=0, concat_axis=0, tiled=True)  15.2 us
    unnamed x11, local copies, waits for them, and re-layouts  5.7 us
  transfers between devices with their start and end apart: 3, of which 3 were waited for; matrix products, arithmetic and copies ran while one was open for 2% of the time, Pallas kernels for 1%

profile of v5, /device:TPU:1, one launch (start us, length us, event | category | flops | bytes accessed | tf_op | source)
XLA Modules:
  0.0 201.5 jit_solution(4022461273874383582)
XLA Ops:
  7.2 0.0 copy-start
  7.2 0.0 all-gather.3.cloned.1.call-start
  7.2 0.7 all-gather.3.cloned.1.call-update
  7.9 0.0 copy-start.2
  7.9 0.9 copy-done.2
  8.8 0.0 copy-start.3
  8.8 0.9 copy-done.3
  9.7 0.0 copy-start.4
  9.7 0.7 copy-done.4
  10.4 0.7 split_rows.1
  11.1 10.4 %all-to-all-start = ((bf16[32,8,128]{2,1,0:T(8,128)(2,1)}), bf16[32,8,128]{2,1,0:T(8,128)(2,1)S(1)}, u32[]{:S(2)}, u32[]{:S(2)}) async-start(bf16[32,8,128]{2,1,0:T(8,128)(2,1)} %bitcast.6), calls=%async_computation | async-start | bytes 131072 | tf_op jit(solution)/shard_map/all_to_all | solution.py:255
  21.5 0.0 copy-done
  21.5 0.1 constant_dynamic-slice_fusion
  21.6 0.1 copy.9
  21.7 1.1 bitcast_convert_fusion
  22.8 6.1 %all-to-all-done.got_ref = bf16[32,8,128]{2,1,0:T(8,128)(2,1)S(1)} async-done(((bf16[32,8,128]{2,1,0:T(8,128)(2,1)}), bf16[32,8,128]{2,1,0:T(8,128)(2,1)S(1)}, u32[]{:S(2)}, u32[]{:S(2)}) %all-to-all-start) | async-done | bytes 65568 | tf_op jit(solution)/shard_map/all_to_all | solution.py:255
  28.9 0.6 join_columns.1
  29.5 13.0 %all-to-all-start.1 = ((bf16[16,8,256]{2,1,0:T(8,128)(2,1)}), bf16[16,8,256]{2,1,0:T(8,128)(2,1)S(1)}, u32[]{:S(2)}, u32[]{:S(2)}) async-start(bf16[16,8,256]{2,1,0:T(8,128)(2,1)} %join_columns.1), calls=%async_computation.1 | async-start | bytes 131072 | tf_op jit(solution)/shard_map/all_to_all | solution.py:255
  42.6 1.8 select_reduce_fusion
  44.4 0.9 copy.10
  45.3 0.1 copy.13
  45.5 9.0 %all-to-all-done.1.after_ref.start_ref = bf16[16,8,256]{2,1,0:T(8,128)(2,1)S(1)} async-done(((bf16[16,8,256]{2,1,0:T(8,128)(2,1)}), bf16[16,8,256]{2,1,0:T(8,128)(2,1)S(1)}, u32[]{:S(2)}, u32[]{:S(2)}) %all-to-all-start.1) | async-done | bytes 65568 | tf_op jit(solution)/shard_map/all_to_all | solution.py:255
  54.5 59.1 %all-gather.3.cloned.1.call-done = bf16[1,2048,1792]{2,1,0:T(8,128)(2,1)} async-done(((bf16[1,128,1792]{2,1,0:T(8,128)(2,1)}), bf16[1,2048,1792]{2,1,0:T(8,128)(2,1)}) %all-gather.3.cloned.1.call-update) | async-done | bytes 7340048 | tf_op jit(solution)/shard_map/all_gather | solution.py:267
  113.7 0.0 copy-start.1
  113.7 3.1 %copy-done.1 = bf16[1,2048,1792]{2,1,0:T(8,128)(2,1)S(1)} copy-done((bf16[1,2048,1792]{2,1,0:T(8,128)(2,1)S(1)}, bf16[1,2048,1792]{2,1,0:T(8,128)(2,1)}, u32[]{:S(2)}) %copy-start.1) | copy-done | bytes 7340056
  116.7 2.1 %forward_matmul.1 = (bf16[16,2,64,256]{3,2,1,0:T(8,128)(2,1)S(1)}, bf16[2048,1792]{1,0:T(8,128)(2,1)S(1)}) custom-call(bf16[2048,1792]{1,0:T(8,128)(2,1)S(1)} %bitcast.22, bf16[1792,256]{1,0:T(8,128)(2,1)S(1)} %bitcast.25, bf16[16,8,256]{2,1,0:T(8,128)(2,1)S(1)} %all-to-all-done.1.after_ref.start_ref), custom_call_target="tpu_custom_call" | custom-call | flops 1879048192 | bytes 7340032 | tf_op jit(solution)/shard_map/forward_matmul/pallas_call | solution.py:110
  118.8 24.5 %all_to_all.25.parts_ref = bf16[32,64,256]{2,1,0:T(8,128)(2,1)S(1)} all-to-all(bf16[32,64,256]{2,1,0:T(8,128)(2,1)S(1)} %bitcast.26), channel_id=1, replica_groups=mesh['section'=4,'dp'=16,'tensor'=8] {'section','tensor'}, dimensions={0} | all-to-all | bytes 2097152 | tf_op jit(solution)/shard_map/all_to_all | solution.py:255
  143.4 0.3 cascade.1
  143.7 21.2 %all_to_all.26.got_ref = bf16[16,24,256]{2,1,0:T(8,128)(2,1)S(1)} all-to-all(bf16[16,24,256]{2,1,0:T(8,128)(2,1)S(1)} %bitcast.27), channel_id=1, replica_groups=mesh['section'=4,'dp'=16,'tensor'=8] {'dp'}, dimensions={0} | all-to-all | bytes 393216 | tf_op jit(solution)/shard_map/all_to_all | solution.py:255
  164.9 0.2 norm_gradient.1
  165.2 25.7 %all_to_all.27 = bf16[32,72,256]{2,1,0:T(8,128)(2,1)S(1)} all-to-all(bf16[32,72,256]{2,1,0:T(8,128)(2,1)S(1)} %bitcast.24), channel_id=1, replica_groups=mesh['section'=4,'dp'=16,'tensor'=8] {'section','tensor'}, dimensions={0} | all-to-all | bytes 2359296 | tf_op jit(solution)/shard_map/all_to_all | solution.py:255
  190.8 3.8 %gradient_matmul.1 = (bf16[2,7,128,128]{3,2,1,0:T(8,128)(2,1)}, bf16[128,512]{1,0:T(8,128)(2,1)}) custom-call(s32[2,7]{1,0:T(2,128)S(1)} %bitcast.29, bf16[16,2,72,256]{3,2,1,0:T(8,128)(2,1)S(1)} %bitcast.23, bf16[2048,1792]{1,0:T(8,128)(2,1)S(1)} %get-tuple-element.13.acts_ref), custom_call_target="tpu_custom_call" | custom-call | flops 1879048192 | bytes 7340032 | tf_op jit(solution)/shard_map/gradient_matmul/pallas_call | solution.py:236
  (1 shorter events, 0.0 us)
Async XLA Ops:
  7.2 14.3 %copy-start = (s32[1,1,32,7]{2,1,3,0:T(1,128)S(1)}, s32[1,1,32,7]{2,1,3,0:T(1,128)}, u32[]{:S(2)}) copy-start(s32[1,1,32,7]{2,1,3,0:T(1,128)} %param.9) | copy-start | bytes 2692
  7.2 106.5 %all-gather.3.cloned.1.call-start = ((), (), s32[]{:S(2)}) async-start(), calls=%async_computation.5 | async-start | bytes 7798784 | tf_op jit(solution)/shard_map/all_gather | solution.py:267
  7.9 0.9 copy-start.2
  8.8 0.9 copy-start.3
  9.7 0.7 copy-start.4
  11.1 17.8 %all-to-all-start = ((bf16[32,8,128]{2,1,0:T(8,128)(2,1)}), bf16[32,8,128]{2,1,0:T(8,128)(2,1)S(1)}, u32[]{:S(2)}, u32[]{:S(2)}) async-start(bf16[32,8,128]{2,1,0:T(8,128)(2,1)} %bitcast.6), calls=%async_computation | async-start | bytes 131072 | tf_op jit(solution)/shard_map/all_to_all | solution.py:255
  29.5 25.0 %all-to-all-start.1 = ((bf16[16,8,256]{2,1,0:T(8,128)(2,1)}), bf16[16,8,256]{2,1,0:T(8,128)(2,1)S(1)}, u32[]{:S(2)}, u32[]{:S(2)}) async-start(bf16[16,8,256]{2,1,0:T(8,128)(2,1)} %join_columns.1), calls=%async_computation.1 | async-start | bytes 131072 | tf_op jit(solution)/shard_map/all_to_all | solution.py:255
  113.7 3.1 %copy-start.1 = (bf16[1,2048,1792]{2,1,0:T(8,128)(2,1)S(1)}, bf16[1,2048,1792]{2,1,0:T(8,128)(2,1)}, u32[]{:S(2)}) copy-start(bf16[1,2048,1792]{2,1,0:T(8,128)(2,1)} %all-gather.3.cloned.1.call-done) | copy-start | bytes 22020100
Sparse Core Ops, SparseCore 0:
  10.1 103.5 all-gather.2

commit v6 on v5

v6 whole, which is shorter than its diff:
```python
import jax
import jax.numpy as jnp
from jax import lax
from jax.experimental import pallas as pl
from jax.experimental.pallas import tpu as pltpu
from jax.sharding import Mesh
from jax.sharding import PartitionSpec as P

D = 4096
TENSOR = ("x", "core")
CHIPS = ("section", "x")
HALF = 4


def regroup(even, odd):
    upper = lax.broadcasted_iota(jnp.int32, even.shape, even.ndim - 2) < HALF
    axis = even.ndim - 2
    first = jnp.where(upper, even, pltpu.roll(odd, HALF, axis))
    second = jnp.where(upper, pltpu.roll(even, HALF, axis), odd)
    return first, second


def call(kernel, name, flops, moved, vmem=16 << 20, **kwargs):
    return pl.pallas_call(
        kernel,
        compiler_params=pltpu.CompilerParams(vmem_limit_bytes=vmem),
        cost_estimate=pl.CostEstimate(flops=flops, bytes_accessed=moved, transcendentals=0),
        name=name,
        **kwargs,
    )


def split_kernel(section_ref, residual_ref, cot_ref, gain_ref, out_ref):
    rows, width = residual_ref.shape
    shape = (rows // 8, 8, width)
    scaled = cot_ref[...].astype(jnp.float32) * gain_ref[...]
    tiles = regroup(residual_ref[...].astype(jnp.float32).reshape(shape), scaled.reshape(shape))
    for half in range(2):
        for core in range(2):
            part = tiles[half][8 * core : 8 * core + 8].astype(out_ref.dtype)
            out_ref[half, :, core] = part


def split(section, residual, cotangent, gain):
    rows, width = residual.shape
    part = width // lax.axis_size("section")
    block = pl.BlockSpec((rows, part), lambda i, section: (0, section[0]))
    out = call(
        split_kernel,
        "split_rows",
        rows * part,
        6 * rows * part,
        grid_spec=pltpu.PrefetchScalarGridSpec(
            num_scalar_prefetch=1,
            grid=(1,),
            in_specs=[
                block,
                block,
                pl.BlockSpec((1, part), lambda i, section: (0, section[0])),
            ],
            out_specs=pl.BlockSpec((2, rows // 16, 2, 8, part), lambda i, section: (0,) * 5),
        ),
        out_shape=jax.ShapeDtypeStruct((2, rows // 16, 2, 8, part), jnp.bfloat16),
    )(section.astype(jnp.int32).reshape(1), residual, cotangent, gain.reshape(1, width))
    return out.reshape(rows // 4, 8, part)


def join_kernel(got_ref, out_ref):
    part = got_ref.shape[2]
    shards = out_ref.shape[0] // 2
    for half in range(2):
        for shard in range(shards):
            for side in range(2):
                tile = got_ref[(2 * half + side) * shards + shard]
                out_ref[2 * shard + half, :, side * part : (side + 1) * part] = tile


def join(got, planes):
    _, rows, part = got.shape
    shape = (planes, rows, 2 * part)
    return call(
        join_kernel,
        "join_columns",
        got.size,
        4 * got.size,
        grid=(1,),
        in_specs=[pl.BlockSpec(got.shape, lambda i: (0, 0, 0))],
        out_specs=pl.BlockSpec(shape, lambda i: (0, 0, 0)),
        out_shape=jax.ShapeDtypeStruct(shape, got.dtype),
    )(got)


def partial_sums(core, acts_ref, dense_ref, out_ref, added_ref=None):
    groups, _, rows, units = acts_ref.shape
    width = dense_ref.shape[1]
    for step in range(groups // 8):
        acts = acts_ref[8 * step : 8 * step + 8, core].reshape(8 * rows, units)
        found = jnp.dot(acts, dense_ref[...], preferred_element_type=jnp.float32)
        found = found.reshape(8, rows // 8, 8, width)
        pairs = [regroup(found[2 * q], found[2 * q + 1]) for q in range(4)]
        at = slice(32 * step, 32 * step + 32)
        for half in range(2):
            joined = jnp.concatenate([pair[half] for pair in pairs], axis=1)
            if added_ref is not None:
                joined += added_ref[half, :, at].astype(jnp.float32)
            out_ref[half, :, at] = joined.astype(out_ref.dtype)


def other_kernel(core_ref, acts_ref, dense_ref, after_ref, out_ref, held_ref):
    for group in range(acts_ref.shape[0]):
        held_ref[group] = acts_ref[group]
    partial_sums(1 - core_ref[0], acts_ref, dense_ref, out_ref)


def own_kernel(core_ref, held_ref, dense_ref, added_ref, out_ref):
    partial_sums(core_ref[0], held_ref, dense_ref, out_ref, added_ref)


def forward(core, every, dense, rows, after):
    tokens, units = every.shape
    width = dense.shape[1]
    groups = tokens // rows
    shape = (groups, 2, rows // 2, units)
    out = jax.ShapeDtypeStruct((2, rows // 16, HALF * groups, width), jnp.bfloat16)
    whole = pl.BlockSpec(memory_space=pltpu.VMEM)
    scalar = pl.BlockSpec(memory_space=pltpu.SMEM)
    sent, held = call(
        other_kernel,
        "other_core_matmul",
        tokens * units * width,
        2 * tokens * units,
        in_specs=[scalar, whole, whole, pl.BlockSpec(memory_space=pl.ANY)],
        out_specs=[whole, whole],
        out_shape=(out, pltpu.VMEM(shape, every.dtype)),
    )(core, every.reshape(shape), dense, after)
    got = lax.ppermute(sent, "core", [(0, 1), (1, 0)])
    both = call(
        own_kernel,
        "own_core_matmul",
        tokens * units * width,
        tokens * units,
        in_specs=[scalar, whole, whole, whole],
        out_specs=whole,
        out_shape=out,
    )(core, held, dense, got)
    return both.reshape(rows // 8, HALF * groups, width), held


def cascade_kernel(parts_ref, start_ref, out_ref, final_ref, scaled_ref):
    rows, width = final_ref.shape
    shards = parts_ref.shape[0] // 4
    start = start_ref[...].astype(jnp.float32).reshape(rows // 8, 2, 8, width)
    current, scaled = (t.reshape(rows, width) for t in regroup(start[:, 0], start[:, 1]))
    tiles = []
    for section in range(4):
        contrib = parts_ref[section * shards].astype(jnp.float32)
        for shard in range(1, shards):
            contrib += parts_ref[section * shards + shard].astype(jnp.float32)
        current = (current + contrib).astype(jnp.bfloat16).astype(jnp.float32)
        tiles.append(current.reshape(rows // 8, 8, width))
    final_ref[...] = current
    scaled_ref[...] = scaled

    lane = lax.broadcasted_iota(jnp.int32, (rows, 128), 1)
    table = jnp.zeros((rows, 128), jnp.float32)
    for at, factor in enumerate((current, scaled)):
        left = jnp.sum(factor * current, axis=1, keepdims=True)
        for term in range(3):
            head = left.astype(jnp.bfloat16).astype(jnp.float32)
            table = jnp.where(lane == 3 * at + term, head, table)
            left = left - head
    table = jnp.concatenate([table, jnp.zeros((128 - rows, 128), jnp.float32)], axis=0)
    sums = jnp.broadcast_to(table.T[None, :8], (rows // 8, 8, 128))

    low, high = regroup(*tiles[:2]), regroup(*tiles[2:])
    for parity in range(2):
        sides = [
            part[parity][:, :, at : at + 128] for at in range(0, width, 128) for part in (low, high)
        ]
        out_ref[:, parity] = jnp.concatenate(sides + [sums], axis=1).astype(out_ref.dtype)


def cascade(parts, start):
    _, rows, width = parts.shape
    half = jax.ShapeDtypeStruct((rows, width), jnp.float32)
    out, final, scaled = call(
        cascade_kernel,
        "cascade",
        parts.size,
        2 * parts.size,
        out_shape=(jax.ShapeDtypeStruct((rows // 8, 2, 40, 128), jnp.bfloat16), half, half),
    )(parts, start)
    return out.reshape(rows // 4, 40, 128), final, scaled


def norm_kernel(core_ref, got_ref, final_ref, scaled_ref, out_ref):
    planes = got_ref.shape[0]
    rows, width = final_ref.shape
    sums = got_ref[0, 32:40].astype(jnp.float32)
    for plane in range(1, planes):
        sums += got_ref[plane, 32:40].astype(jnp.float32)
    table = jnp.concatenate([sums, jnp.zeros((120, 128), jnp.float32)], axis=0).T[:rows]
    lane = lax.broadcasted_iota(jnp.int32, table.shape, 1)
    square = jnp.sum(jnp.where(lane < 3, table, 0.0), axis=1, keepdims=True) / D
    mixed = jnp.sum(jnp.where(lane < 3, 0.0, table), axis=1, keepdims=True) / D
    inverse = lax.rsqrt(square + 1e-05)
    grad = inverse * (scaled_ref[...] - final_ref[...] * (inverse * inverse * mixed))

    shards = planes // 2
    first = core_ref[0] == 0
    spread = jnp.broadcast_to(grad[None], (shards // 2, rows, width))
    pairs = got_ref[...].astype(jnp.float32).reshape(shards, 2, 40, 128)
    for at in range(2):
        even, odd = (
            jnp.concatenate([pairs[:, q, row : row + 8] for row in (8 * at, 8 * at + 16)], axis=2)
            for q in range(2)
        )
        for parity, tile in enumerate(regroup(even, odd)):
            tile = tile.reshape(shards // 2, 2, 8, width)
            same = jnp.where(first, tile[:, 0], tile[:, 1])
            other = jnp.where(first, tile[:, 1], tile[:, 0])
            joined = jnp.concatenate([spread, same, other], axis=1)
            out_ref[2 * at + parity] = joined.astype(out_ref.dtype)


def norm(core, got, final, scaled):
    rows, width = final.shape
    chips = got.shape[0] // 4
    whole = pl.BlockSpec(memory_space=pltpu.VMEM)
    out = call(
        norm_kernel,
        "norm_gradient",
        got.size,
        4 * got.size,
        in_specs=[pl.BlockSpec(memory_space=pltpu.SMEM), whole, whole, whole],
        out_specs=whole,
        out_shape=jax.ShapeDtypeStruct((4, chips, rows + 16, width), jnp.bfloat16),
    )(core, got, final, scaled)
    return out.reshape(4 * chips, rows + 16, width)


def products(core, full_ref, acts_ref, turned_ref, section_at):
    groups, _, rows, units = acts_ref.shape
    _, tiles, _, width = full_ref.shape

    def regrouped(at):
        even = full_ref[0, :, at : at + 8].astype(jnp.float32)
        odd = full_ref[1, :, at : at + 8].astype(jnp.float32)
        return [t.reshape(8 * tiles, width) for t in regroup(even, odd)]

    for two in range(groups // 2):
        pair = jnp.concatenate(regrouped(8 * two), axis=0)
        at = 2 * two * rows
        turned_ref[:, at : at + 2 * rows] = pair.T.astype(turned_ref.dtype)
    found = None
    for step in range(2):
        part = groups // 2
        acts = acts_ref[step * part : (step + 1) * part, core].reshape(part * rows, units)
        term = jnp.dot(
            turned_ref[:, step * part * rows : (step + 1) * part * rows],
            acts,
            preferred_element_type=jnp.float32,
        )
        found = term if found is None else found + term
    return found, jnp.concatenate(regrouped(section_at), axis=1)


def near_kernel(core_ref, full_ref, acts_ref, found_ref, section_ref, turned_ref):
    rows = full_ref.shape[2]
    found, section = products(core_ref[0], full_ref, acts_ref, turned_ref, rows - 16)
    found_ref[...] = found
    section_ref[...] = section.astype(section_ref.dtype)


def far_kernel(
    core_ref,
    kept_ref,
    full_ref,
    acts_ref,
    near_ref,
    near_section_ref,
    out_ref,
    section_ref,
    turned_ref,
    found_ref,
):
    cols, keep, blk, _ = out_ref.shape
    core, rows = core_ref[0], full_ref.shape[2]
    found, section = products(1 - core, full_ref, acts_ref, turned_ref, rows - 8)
    half = section_ref.shape[0] // 2
    section_ref[pl.ds(pl.multiple_of(core * half, half), half)] = near_section_ref[...]
    section_ref[pl.ds(pl.multiple_of((1 - core) * half, half), half)] = section.astype(
        section_ref.dtype
    )
    found_ref[...] = (near_ref[...] + found).astype(found_ref.dtype)
    for c in range(cols):
        for slot in range(keep):
            start = pl.multiple_of(kept_ref[c, slot] * blk, blk)
            out_ref[c, slot] = found_ref[c * blk : (c + 1) * blk, pl.ds(start, blk)].T


def gradient(core, own_kept, full, held, blk):
    groups, _, rows, units = held.shape
    chips, _, width = full.shape
    cols, keep = own_kept.shape
    full = full.reshape(2, chips // 2, *full.shape[1:])
    whole = pl.BlockSpec(memory_space=pltpu.VMEM)
    scalar = pl.BlockSpec(memory_space=pltpu.SMEM)
    turned = pltpu.VMEM((width, groups * rows), jnp.bfloat16)
    flops = 2 * groups * rows * units * width
    other = lax.ppermute(full, "core", [(0, 1), (1, 0)])
    found, section = call(
        near_kernel,
        "own_core_gradient",
        flops,
        held.size,
        in_specs=[scalar, whole, whole],
        out_specs=[whole, whole],
        scratch_shapes=[turned],
        out_shape=(
            jax.ShapeDtypeStruct((width, units), jnp.float32),
            jax.ShapeDtypeStruct((rows, 2 * width), jnp.bfloat16),
        ),
    )(core, full, held)
    return call(
        far_kernel,
        "other_core_gradient",
        flops,
        held.size,
        in_specs=[scalar, scalar] + [whole] * 4,
        out_specs=[whole, whole],
        scratch_shapes=[turned, pltpu.VMEM((width, units), jnp.bfloat16)],
        out_shape=(
            jax.ShapeDtypeStruct((cols, keep, blk, blk), jnp.bfloat16),
            jax.ShapeDtypeStruct((2 * rows, 2 * width), jnp.bfloat16),
        ),
    )(core, own_kept, other, held, found, section)


def exchange(value, axes):
    return lax.all_to_all(value, axes, split_axis=0, concat_axis=0, tiled=True)


def body(hidden, residual_in, weights, kept, cotangent, norm_gain):
    nz = lax.axis_size("dp")
    core = lax.axis_index("core").astype(jnp.int32).reshape(1)
    section, plane = lax.axis_index("section"), lax.axis_index("dp")
    acts = hidden[0]
    rows = acts.shape[0]
    blocks = weights[0, 0]
    cols, _, blk, _ = blocks.shape
    width = cols * blk
    hidden_blocks = acts.shape[1] // blk
    every = lax.all_gather(acts, "dp", axis=0, tiled=True)
    own_kept = lax.dynamic_slice_in_dim(kept[0, 0], plane * cols, cols, axis=0)
    hit = own_kept[None] == jnp.arange(hidden_blocks, dtype=own_kept.dtype)[:, None, None]
    dense = jnp.sum(
        jnp.where(hit[..., None, None], blocks[None].astype(jnp.float32), 0.0), axis=2
    ).astype(jnp.bfloat16)
    dense = dense.transpose(0, 2, 1, 3).reshape(hidden_blocks * blk, width)

    start = exchange(split(section, residual_in, cotangent, norm_gain), ("section",) + TENSOR)
    start = exchange(join(start, nz), "dp")
    partial_out, held = forward(core, every, dense, rows, start)
    sent, final, scaled = cascade(exchange(partial_out, CHIPS), start)
    spread = norm(core, exchange(sent, "dp"), final, scaled)
    grads, section_out = gradient(core, own_kept, exchange(spread, CHIPS), held, blk)
    return (section_out[None], grads[None, None])


def solution(mesh):
    sizes = mesh.shape
    shape = (sizes["section"], sizes["dp"], sizes["tensor"] // 2, 2)
    chips = Mesh(mesh.devices.reshape(shape), ("section", "dp") + TENSOR)
    in_specs = (
        P("section", "dp", TENSOR),
        P("dp", TENSOR),
        P("section", TENSOR, "dp", None, None, None),
        P("section", TENSOR, None, None),
        P("dp", TENSOR),
        P(TENSOR),
    )
    out_specs = (P("section", "dp", TENSOR), P("section", TENSOR, "dp", None, None, None))
    return jax.shard_map(body, mesh=chips, in_specs=in_specs, out_specs=out_specs, check_vma=False)
```

time: 202 us -> 194 us (0.960)
  blocking collectives: 71.4 us -> 50.5 us
  starting transfers between devices: 23.4 us -> 33.6 us
    all_to_all x3, blocking collectives: 71.4 us -> 50.5 us  [exchange(): return lax.all_to_all(value, axes, split_axis=0, concat_axis=0, tiled=True)]
    ppermute x0 -> x2, starting transfers between devices: none -> 10.1 us  [the longest x1 7.55 us: gradient(): other = lax.ppermute(full, 'core', [(0, 1), (1, 0)])]
    pallas_call x3 -> x5, Pallas kernels: 6.15 us -> 6.87 us  [the longest x1 2.73 us: gradient(): call(far_kernel, 'other_core_gradient', flops, held.size, in_specs=[scala...]
  transfers between devices with their start and end apart: 3 -> 5, of which waited for: 3 -> 5; matrix products, arithmetic and copies ran while one was open for 2% -> 2% of each run, Pallas kernels for 1% -> 1%
where the time goes in v6:
time: 194 us; the launch traced here: 193 us
  waiting for transfers between devices  77 us (40%)
  blocking collectives  50.5 us (26%)
  starting transfers between devices  33.6 us (17%)
  between operations  14.2 us (7%)
  Pallas kernels  8.44 us (4%)
  local copies, waits for them, and re-layouts  6.82 us (4%)
  other arithmetic  2.92 us (2%)
    all_gather x1, waiting for transfers between devices, body(): every = lax.all_gather(acts, 'dp', axis=0, tiled=True)  59.1 us
    all_to_all x3, blocking collectives, exchange(): return lax.all_to_all(value, axes, split_axis=0, concat_axis=0, tiled=True)  50.5 us
    all_to_all x2, starting transfers between devices, exchange(): return lax.all_to_all(value, axes, split_axis=0, concat_axis=0, tiled=True)  23.4 us
    all_to_all x2, waiting for transfers between devices, exchange(): return lax.all_to_all(value, axes, split_axis=0, concat_axis=0, tiled=True)  15.2 us
    ppermute x1, starting transfers between devices, gradient(): other = lax.ppermute(full, 'core', [(0, 1), (1, 0)])  7.55 us
    unnamed x11, local copies, waits for them, and re-layouts  5.7 us
  transfers between devices with their start and end apart: 5, of which 5 were waited for; matrix products, arithmetic and copies ran while one was open for 2% of the time, Pallas kernels for 1%

profile of v6, /device:TPU:1, one launch (start us, length us, event | category | flops | bytes accessed | tf_op | source)
XLA Modules:
  0.0 193.4 jit_solution(16591569066186109423)
XLA Ops:
  7.2 0.0 copy-start
  7.2 0.0 all-gather.3.cloned.1.call-start
  7.2 0.7 all-gather.3.cloned.1.call-update
  7.9 0.0 copy-start.2
  7.9 0.9 copy-done.2
  8.8 0.0 copy-start.3
  8.8 0.9 copy-done.3
  9.7 0.0 copy-start.4
  9.7 0.7 copy-done.4
  10.4 0.7 split_rows.1
  11.1 10.4 %all-to-all-start = ((bf16[32,8,128]{2,1,0:T(8,128)(2,1)}), bf16[32,8,128]{2,1,0:T(8,128)(2,1)S(1)}, u32[]{:S(2)}, u32[]{:S(2)}) async-start(bf16[32,8,128]{2,1,0:T(8,128)(2,1)} %bitcast.7), calls=%async_computation | async-start | bytes 131072 | tf_op jit(solution)/shard_map/all_to_all | solution.py:341
  21.5 0.0 copy-done
  21.5 0.1 constant_dynamic-slice_fusion
  21.6 0.1 copy.9
  21.7 1.1 bitcast_convert_fusion
  22.8 6.1 %all-to-all-done.got_ref = bf16[32,8,128]{2,1,0:T(8,128)(2,1)S(1)} async-done(((bf16[32,8,128]{2,1,0:T(8,128)(2,1)}), bf16[32,8,128]{2,1,0:T(8,128)(2,1)S(1)}, u32[]{:S(2)}, u32[]{:S(2)}) %all-to-all-start) | async-done | bytes 65568 | tf_op jit(solution)/shard_map/all_to_all | solution.py:341
  28.9 0.6 join_columns.1
  29.5 13.0 %all-to-all-start.1 = ((bf16[16,8,256]{2,1,0:T(8,128)(2,1)}), bf16[16,8,256]{2,1,0:T(8,128)(2,1)S(1)}, u32[]{:S(2)}, u32[]{:S(2)}) async-start(bf16[16,8,256]{2,1,0:T(8,128)(2,1)} %join_columns.1), calls=%async_computation.1 | async-start | bytes 131072 | tf_op jit(solution)/shard_map/all_to_all | solution.py:341
  42.6 1.8 select_reduce_fusion
  44.4 0.9 copy.10
  45.3 0.1 copy.13
  45.5 9.0 %all-to-all-done.1.after_ref.start_ref = bf16[16,8,256]{2,1,0:T(8,128)(2,1)S(1)} async-done(((bf16[16,8,256]{2,1,0:T(8,128)(2,1)}), bf16[16,8,256]{2,1,0:T(8,128)(2,1)S(1)}, u32[]{:S(2)}, u32[]{:S(2)}) %all-to-all-start.1) | async-done | bytes 65568 | tf_op jit(solution)/shard_map/all_to_all | solution.py:341
  54.5 59.1 %all-gather.3.cloned.1.call-done = bf16[1,2048,1792]{2,1,0:T(8,128)(2,1)} async-done(((bf16[1,128,1792]{2,1,0:T(8,128)(2,1)}), bf16[1,2048,1792]{2,1,0:T(8,128)(2,1)}) %all-gather.3.cloned.1.call-update) | async-done | bytes 7340048 | tf_op jit(solution)/shard_map/all_gather | solution.py:354
  113.7 0.0 copy-start.1
  113.7 3.1 %copy-done.1 = bf16[1,2048,1792]{2,1,0:T(8,128)(2,1)S(1)} copy-done((bf16[1,2048,1792]{2,1,0:T(8,128)(2,1)S(1)}, bf16[1,2048,1792]{2,1,0:T(8,128)(2,1)}, u32[]{:S(2)}) %copy-start.1) | copy-done | bytes 7340056
  116.7 1.6 other_core_matmul.1
  118.3 2.6 %collective-permute-start = (bf16[2,8,64,256]{3,2,1,0:T(8,128)(2,1)S(1)}, bf16[2,8,64,256]{3,2,1,0:T(8,128)(2,1)S(1)}, u32[]{:S(2)}, u32[]{:S(2)}) collective-permute-start(bf16[2,8,64,256]{3,2,1,0:T(8,128)(2,1)S(1)} %get-tuple-element.12), channel_id=1, source_target_pairs={{0,1},{1,0},{2,3},{3,2},{4,5},{5,4},{6,7},{7,6},{8,9},{9,8},{10,11... | collective-permute-start | bytes 1572872 | tf_op jit(solution)/shard_map/ppermute | solution.py:136
  120.9 1.5 collective-permute-done.added_ref
  122.4 1.2 own_core_matmul.1
  123.6 17.0 %all_to_all.25.parts_ref = bf16[16,64,256]{2,1,0:T(8,128)(2,1)S(1)} all-to-all(bf16[16,64,256]{2,1,0:T(8,128)(2,1)S(1)} %bitcast.29), channel_id=1, replica_groups=mesh['section'=4,'dp'=16,'x'=4,'core'=2] {'section','x'}, dimensions={0} | all-to-all | bytes 1048576 | tf_op jit(solution)/shard_map/all_to_all | solution.py:341
  140.6 0.3 cascade.1
  140.9 20.6 %all_to_all.26.got_ref = bf16[16,40,128]{2,1,0:T(8,128)(2,1)S(1)} all-to-all(bf16[16,40,128]{2,1,0:T(8,128)(2,1)S(1)} %bitcast.30), channel_id=1, replica_groups=mesh['section'=4,'dp'=16,'x'=4,'core'=2] {'dp'}, dimensions={0} | all-to-all | bytes 327680 | tf_op jit(solution)/shard_map/all_to_all | solution.py:341
  161.4 0.2 norm_gradient.1
  161.6 13.0 %all_to_all.27 = bf16[16,80,256]{2,1,0:T(8,128)(2,1)S(1)} all-to-all(bf16[16,80,256]{2,1,0:T(8,128)(2,1)S(1)} %bitcast.28), channel_id=1, replica_groups=mesh['section'=4,'dp'=16,'x'=4,'core'=2] {'section','x'}, dimensions={0} | all-to-all | bytes 1310720 | tf_op jit(solution)/shard_map/all_to_all | solution.py:341
  174.6 7.5 %collective-permute-start.1 = (bf16[2,8,80,256]{3,2,1,0:T(8,128)(2,1)S(1)}, bf16[2,8,80,256]{3,2,1,0:T(8,128)(2,1)S(1)}, u32[]{:S(2)}, u32[]{:S(2)}) collective-permute-start(bf16[2,8,80,256]{3,2,1,0:T(8,128)(2,1)S(1)} %bitcast.26), channel_id=1, source_target_pairs={{0,1},{1,0},{2,3},{3,2},{4,5},{5,4},{6,7},{7,6},{8,9},{9,8},{10,11... | collective-permute-start | bytes 1966088 | tf_op jit(solution)/shard_map/ppermute | solution.py:311
  182.1 1.2 own_core_gradient.1
  183.4 0.5 collective-permute-done.1.full_ref
  183.8 2.7 %other_core_gradient.1 = (bf16[2,7,128,128]{3,2,1,0:T(8,128)(2,1)}, bf16[128,512]{1,0:T(8,128)(2,1)}) custom-call(s32[1]{0:T(128)} %bitcast.core_ref, s32[2,7]{1,0:T(2,128)S(1)} %bitcast.32, bf16[2,8,80,256]{3,2,1,0:T(8,128)(2,1)S(1)} %collective-permute-done.1.full_ref, bf16[16,2,64,1792]{3,2,1,0:T(8,128)(2,1)S(1)} %get-tuple-element.11.held_ref.acts_ref, ...), custom_call_target="tpu_custom_call" | custom-call | flops 939524096 | bytes 3670016 | tf_op jit(solution)/shard_map/other_core_gradient/pallas_call | solution.py:325
  (1 shorter events, 0.0 us)
Async XLA Ops:
  7.2 14.3 %copy-start = (s32[1,1,32,7]{2,1,3,0:T(1,128)S(1)}, s32[1,1,32,7]{2,1,3,0:T(1,128)}, u32[]{:S(2)}) copy-start(s32[1,1,32,7]{2,1,3,0:T(1,128)} %param.9) | copy-start | bytes 2692
  7.2 106.5 %all-gather.3.cloned.1.call-start = ((), (), s32[]{:S(2)}) async-start(), calls=%async_computation.5 | async-start | bytes 7798784 | tf_op jit(solution)/shard_map/all_gather | solution.py:354
  7.9 0.9 copy-start.2
  8.8 0.9 copy-start.3
  9.7 0.7 copy-start.4
  11.1 17.8 %all-to-all-start = ((bf16[32,8,128]{2,1,0:T(8,128)(2,1)}), bf16[32,8,128]{2,1,0:T(8,128)(2,1)S(1)}, u32[]{:S(2)}, u32[]{:S(2)}) async-start(bf16[32,8,128]{2,1,0:T(8,128)(2,1)} %bitcast.7), calls=%async_computation | async-start | bytes 131072 | tf_op jit(solution)/shard_map/all_to_all | solution.py:341
  29.5 25.0 %all-to-all-start.1 = ((bf16[16,8,256]{2,1,0:T(8,128)(2,1)}), bf16[16,8,256]{2,1,0:T(8,128)(2,1)S(1)}, u32[]{:S(2)}, u32[]{:S(2)}) async-start(bf16[16,8,256]{2,1,0:T(8,128)(2,1)} %join_columns.1), calls=%async_computation.1 | async-start | bytes 131072 | tf_op jit(solution)/shard_map/all_to_all | solution.py:341
  113.7 3.1 %copy-start.1 = (bf16[1,2048,1792]{2,1,0:T(8,128)(2,1)S(1)}, bf16[1,2048,1792]{2,1,0:T(8,128)(2,1)}, u32[]{:S(2)}) copy-start(bf16[1,2048,1792]{2,1,0:T(8,128)(2,1)} %all-gather.3.cloned.1.call-done) | copy-start | bytes 22020100
  118.3 4.1 %collective-permute-start = (bf16[2,8,64,256]{3,2,1,0:T(8,128)(2,1)S(1)}, bf16[2,8,64,256]{3,2,1,0:T(8,128)(2,1)S(1)}, u32[]{:S(2)}, u32[]{:S(2)}) collective-permute-start(bf16[2,8,64,256]{3,2,1,0:T(8,128)(2,1)S(1)} %get-tuple-element.12), channel_id=1, source_target_pairs={{0,1},{1,0},{2,3},{3,2},{4,5},{5,4},{6,7},{7,6},{8,9},{9,8},{10,11... | collective-permute-start | bytes 1572872 | tf_op jit(solution)/shard_map/ppermute | solution.py:136
  174.6 9.3 %collective-permute-start.1 = (bf16[2,8,80,256]{3,2,1,0:T(8,128)(2,1)S(1)}, bf16[2,8,80,256]{3,2,1,0:T(8,128)(2,1)S(1)}, u32[]{:S(2)}, u32[]{:S(2)}) collective-permute-start(bf16[2,8,80,256]{3,2,1,0:T(8,128)(2,1)S(1)} %bitcast.26), channel_id=1, source_target_pairs={{0,1},{1,0},{2,3},{3,2},{4,5},{5,4},{6,7},{7,6},{8,9},{9,8},{10,11... | collective-permute-start | bytes 1966088 | tf_op jit(solution)/shard_map/ppermute | solution.py:311
Sparse Core Ops, SparseCore 0:
  10.1 103.5 all-gather.2

commit v7 on v6

--- a/solution.py
+++ b/solution.py
@@ -65,19 +65,17 @@
     return out.reshape(rows // 4, 8, part)
 
 
-def join_kernel(got_ref, out_ref):
-    part = got_ref.shape[2]
-    shards = out_ref.shape[0] // 2
+def join_kernel(got_ref, left_ref, right_ref):
+    shards = left_ref.shape[0] // 2
     for half in range(2):
         for shard in range(shards):
-            for side in range(2):
-                tile = got_ref[(2 * half + side) * shards + shard]
-                out_ref[2 * shard + half, :, side * part : (side + 1) * part] = tile
+            for side, out_ref in enumerate((left_ref, right_ref)):
+                out_ref[2 * shard + half] = got_ref[(2 * half + side) * shards + shard]
 
 
 def join(got, planes):
     _, rows, part = got.shape
-    shape = (planes, rows, 2 * part)
+    shape = (planes, rows, part)
     return call(
         join_kernel,
         "join_columns",
@@ -85,12 +83,12 @@
         4 * got.size,
         grid=(1,),
         in_specs=[pl.BlockSpec(got.shape, lambda i: (0, 0, 0))],
-        out_specs=pl.BlockSpec(shape, lambda i: (0, 0, 0)),
-        out_shape=jax.ShapeDtypeStruct(shape, got.dtype),
+        out_specs=[pl.BlockSpec(shape, lambda i: (0, 0, 0))] * 2,
+        out_shape=[jax.ShapeDtypeStruct(shape, got.dtype)] * 2,
     )(got)
 
 
-def partial_sums(core, acts_ref, dense_ref, out_ref, added_ref=None):
+def partial_sums(core, acts_ref, dense_ref, out_ref):
     groups, _, rows, units = acts_ref.shape
     width = dense_ref.shape[1]
     for step in range(groups // 8):
@@ -101,19 +99,21 @@
         at = slice(32 * step, 32 * step + 32)
         for half in range(2):
             joined = jnp.concatenate([pair[half] for pair in pairs], axis=1)
-            if added_ref is not None:
-                joined += added_ref[half, :, at].astype(jnp.float32)
             out_ref[half, :, at] = joined.astype(out_ref.dtype)
 
 
-def other_kernel(core_ref, acts_ref, dense_ref, after_ref, out_ref, held_ref):
+def other_kernel(core_ref, acts_ref, dense_ref, left_ref, right_ref, out_ref, held_ref):
     for group in range(acts_ref.shape[0]):
         held_ref[group] = acts_ref[group]
     partial_sums(1 - core_ref[0], acts_ref, dense_ref, out_ref)
 
 
-def own_kernel(core_ref, held_ref, dense_ref, added_ref, out_ref):
-    partial_sums(core_ref[0], held_ref, dense_ref, out_ref, added_ref)
+def own_kernel(core_ref, held_ref, dense_ref, out_ref):
+    partial_sums(core_ref[0], held_ref, dense_ref, out_ref)
+
+
+def add_kernel(own_ref, got_ref, out_ref):
+    out_ref[...] = (own_ref[...] + got_ref[...].astype(jnp.float32)).astype(out_ref.dtype)
 
 
 def forward(core, every, dense, rows, after):
@@ -129,27 +129,37 @@
         "other_core_matmul",
         tokens * units * width,
         2 * tokens * units,
-        in_specs=[scalar, whole, whole, pl.BlockSpec(memory_space=pl.ANY)],
+        in_specs=[scalar, whole, whole] + [pl.BlockSpec(memory_space=pl.ANY)] * 2,
         out_specs=[whole, whole],
         out_shape=(out, pltpu.VMEM(shape, every.dtype)),
-    )(core, every.reshape(shape), dense, after)
+    )(core, every.reshape(shape), dense, *after)
     got = lax.ppermute(sent, "core", [(0, 1), (1, 0)])
-    both = call(
+    own = call(
         own_kernel,
         "own_core_matmul",
         tokens * units * width,
         tokens * units,
-        in_specs=[scalar, whole, whole, whole],
+        in_specs=[scalar, whole, whole],
+        out_specs=whole,
+        out_shape=jax.ShapeDtypeStruct(out.shape, jnp.float32),
+    )(core, held, dense)
+    both = call(
+        add_kernel,
+        "add_cores",
+        out.size,
+        8 * out.size,
+        in_specs=[whole] * 2,
         out_specs=whole,
         out_shape=out,
-    )(core, held, dense, got)
+    )(own, got)
     return both.reshape(rows // 8, HALF * groups, width), held
 
 
-def cascade_kernel(parts_ref, start_ref, out_ref, final_ref, scaled_ref):
+def cascade_kernel(parts_ref, left_ref, right_ref, out_ref, final_ref, scaled_ref):
     rows, width = final_ref.shape
     shards = parts_ref.shape[0] // 4
-    start = start_ref[...].astype(jnp.float32).reshape(rows // 8, 2, 8, width)
+    start = jnp.concatenate([left_ref[...], right_ref[...]], axis=2).astype(jnp.float32)
+    start = start.reshape(rows // 8, 2, 8, width)
     current, scaled = (t.reshape(rows, width) for t in regroup(start[:, 0], start[:, 1]))
     tiles = []
     for section in range(4):
@@ -189,7 +199,7 @@
         parts.size,
         2 * parts.size,
         out_shape=(jax.ShapeDtypeStruct((rows // 8, 2, 40, 128), jnp.bfloat16), half, half),
-    )(parts, start)
+    )(parts, *start)
     return out.reshape(rows // 4, 40, 128), final, scaled
 
 
@@ -360,7 +370,7 @@
     dense = dense.transpose(0, 2, 1, 3).reshape(hidden_blocks * blk, width)
 
     start = exchange(split(section, residual_in, cotangent, norm_gain), ("section",) + TENSOR)
-    start = exchange(join(start, nz), "dp")
+    start = [exchange(side, "dp") for side in join(start, nz)]
     partial_out, held = forward(core, every, dense, rows, start)
     sent, final, scaled = cascade(exchange(partial_out, CHIPS), start)
     spread = norm(core, exchange(sent, "dp"), final, scaled)

time: 194 us -> 193 us (level)
  waiting for transfers between devices: 77 us -> 72.4 us
  starting transfers between devices: 33.6 us -> 37.1 us
    all_gather x1, waiting for transfers between devices: 59.1 us -> 44.5 us  [body(): every = lax.all_gather(acts, 'dp', axis=0, tiled=True)]
    all_to_all x2 -> x3, waiting for transfers between devices: 15.2 us -> 26.3 us  [exchange(): return lax.all_to_all(value, axes, split_axis=0, concat_axis=0, tiled=True)]
    all_to_all x2 -> x3, starting transfers between devices: 23.4 us -> 26.9 us  [exchange(): return lax.all_to_all(value, axes, split_axis=0, concat_axis=0, tiled=True)]
  transfers between devices with their start and end apart: 5 -> 6, of which waited for: 5 -> 6; matrix products, arithmetic and copies ran while one was open for 2% -> 2% of each run, Pallas kernels for 1% -> 2%
where the time goes in v7:
time: 193 us; the launch traced here: 192 us
  waiting for transfers between devices  72.4 us (38%)
  blocking collectives  50.5 us (26%)
  starting transfers between devices  37.1 us (19%)
  between operations  14.2 us (7%)
  Pallas kernels  8.52 us (4%)
  local copies, waits for them, and re-layouts  6.82 us (4%)
  other arithmetic  2.92 us (2%)
    all_to_all x3, blocking collectives, exchange(): return lax.all_to_all(value, axes, split_axis=0, concat_axis=0, tiled=True)  50.5 us
    all_gather x1, waiting for transfers between devices, body(): every = lax.all_gather(acts, 'dp', axis=0, tiled=True)  44.5 us
    all_to_all x3, starting transfers between devices, exchange(): return lax.all_to_all(value, axes, split_axis=0, concat_axis=0, tiled=True)  26.9 us
    all_to_all x3, waiting for transfers between devices, exchange(): return lax.all_to_all(value, axes, split_axis=0, concat_axis=0, tiled=True)  26.3 us
    ppermute x1, starting transfers between devices, gradient(): other = lax.ppermute(full, 'core', [(0, 1), (1, 0)])  7.55 us
    unnamed x11, local copies, waits for them, and re-layouts  5.7 us
  transfers between devices with their start and end apart: 6, of which 6 were waited for; matrix products, arithmetic and copies ran while one was open for 2% of the time, Pallas kernels for 2%

profile of v7, /device:TPU:1, one launch (start us, length us, event | category | flops | bytes accessed | tf_op | source)
XLA Modules:
  0.0 192.4 jit_solution(4927133260663791356)
XLA Ops:
  7.2 0.0 copy-start
  7.2 0.0 all-gather.3.cloned.1.call-start
  7.2 0.7 all-gather.3.cloned.1.call-update
  7.9 0.0 copy-start.2
  7.9 0.9 copy-done.2
  8.8 0.0 copy-start.3
  8.8 0.9 copy-done.3
  9.7 0.0 copy-start.4
  9.7 0.7 copy-done.4
  10.4 0.7 split_rows.1
  11.1 10.4 %all-to-all-start = ((bf16[32,8,128]{2,1,0:T(8,128)(2,1)}), bf16[32,8,128]{2,1,0:T(8,128)(2,1)S(1)}, u32[]{:S(2)}, u32[]{:S(2)}) async-start(bf16[32,8,128]{2,1,0:T(8,128)(2,1)} %bitcast.7), calls=%async_computation | async-start | bytes 131072 | tf_op jit(solution)/shard_map/all_to_all | solution.py:351
  21.5 1.1 bitcast_convert_fusion
  22.6 0.0 copy-done
  22.6 0.1 constant_dynamic-slice_fusion
  22.7 0.1 copy.9
  22.8 6.1 %all-to-all-done.got_ref = bf16[32,8,128]{2,1,0:T(8,128)(2,1)S(1)} async-done(((bf16[32,8,128]{2,1,0:T(8,128)(2,1)}), bf16[32,8,128]{2,1,0:T(8,128)(2,1)S(1)}, u32[]{:S(2)}, u32[]{:S(2)}) %all-to-all-start) | async-done | bytes 65568 | tf_op jit(solution)/shard_map/all_to_all | solution.py:351
  28.9 0.6 join_columns.1
  29.5 13.0 %all-to-all-start.1 = ((bf16[16,8,128]{2,1,0:T(8,128)(2,1)}), bf16[16,8,128]{2,1,0:T(8,128)(2,1)S(1)}, u32[]{:S(2)}, u32[]{:S(2)}) async-start(bf16[16,8,128]{2,1,0:T(8,128)(2,1)} %get-tuple-element.13), calls=%async_computation.1 | async-start | bytes 65536 | tf_op jit(solution)/shard_map/all_to_all | solution.py:351
  42.6 11.6 %all-to-all-done.1.left_ref = bf16[16,8,128]{2,1,0:T(8,128)(2,1)S(1)} async-done(((bf16[16,8,128]{2,1,0:T(8,128)(2,1)}), bf16[16,8,128]{2,1,0:T(8,128)(2,1)S(1)}, u32[]{:S(2)}, u32[]{:S(2)}) %all-to-all-start.1) | async-done | bytes 32800 | tf_op jit(solution)/shard_map/all_to_all | solution.py:351
  54.2 3.5 %all-to-all-start.2 = ((bf16[16,8,128]{2,1,0:T(8,128)(2,1)}), bf16[16,8,128]{2,1,0:T(8,128)(2,1)S(1)}, u32[]{:S(2)}, u32[]{:S(2)}) async-start(bf16[16,8,128]{2,1,0:T(8,128)(2,1)} %get-tuple-element.14), calls=%async_computation.2 | async-start | bytes 65536 | tf_op jit(solution)/shard_map/all_to_all | solution.py:351
  57.7 1.8 select_reduce_fusion
  59.5 0.9 copy.10
  60.4 0.1 copy.13
  60.6 8.6 %all-to-all-done.2.right_ref = bf16[16,8,128]{2,1,0:T(8,128)(2,1)S(1)} async-done(((bf16[16,8,128]{2,1,0:T(8,128)(2,1)}), bf16[16,8,128]{2,1,0:T(8,128)(2,1)S(1)}, u32[]{:S(2)}, u32[]{:S(2)}) %all-to-all-start.2) | async-done | bytes 32800 | tf_op jit(solution)/shard_map/all_to_all | solution.py:351
  69.1 44.5 %all-gather.3.cloned.1.call-done = bf16[1,2048,1792]{2,1,0:T(8,128)(2,1)} async-done(((bf16[1,128,1792]{2,1,0:T(8,128)(2,1)}), bf16[1,2048,1792]{2,1,0:T(8,128)(2,1)}) %all-gather.3.cloned.1.call-update) | async-done | bytes 7340048 | tf_op jit(solution)/shard_map/all_gather | solution.py:364
  113.7 0.0 copy-start.1
  113.7 3.1 %copy-done.1 = bf16[1,2048,1792]{2,1,0:T(8,128)(2,1)S(1)} copy-done((bf16[1,2048,1792]{2,1,0:T(8,128)(2,1)S(1)}, bf16[1,2048,1792]{2,1,0:T(8,128)(2,1)}, u32[]{:S(2)}) %copy-start.1) | copy-done | bytes 7340056
  116.7 1.6 other_core_matmul.1
  118.3 2.6 %collective-permute-start = (bf16[2,8,64,256]{3,2,1,0:T(8,128)(2,1)S(1)}, bf16[2,8,64,256]{3,2,1,0:T(8,128)(2,1)S(1)}, u32[]{:S(2)}, u32[]{:S(2)}) collective-permute-start(bf16[2,8,64,256]{3,2,1,0:T(8,128)(2,1)S(1)} %get-tuple-element.16), channel_id=1, source_target_pairs={{0,1},{1,0},{2,3},{3,2},{4,5},{5,4},{6,7},{7,6},{8,9},{9,8},{10,11... | collective-permute-start | bytes 1572872 | tf_op jit(solution)/shard_map/ppermute | solution.py:136
  120.9 1.1 own_core_matmul.1.own_ref
  122.0 0.4 collective-permute-done.got_ref
  122.4 0.1 add_cores.1
  122.6 17.0 %all_to_all.30.parts_ref = bf16[16,64,256]{2,1,0:T(8,128)(2,1)S(1)} all-to-all(bf16[16,64,256]{2,1,0:T(8,128)(2,1)S(1)} %bitcast.29), channel_id=1, replica_groups=mesh['section'=4,'dp'=16,'x'=4,'core'=2] {'section','x'}, dimensions={0} | all-to-all | bytes 1048576 | tf_op jit(solution)/shard_map/all_to_all | solution.py:351
  139.6 0.3 cascade.1
  139.9 20.6 %all_to_all.31.got_ref = bf16[16,40,128]{2,1,0:T(8,128)(2,1)S(1)} all-to-all(bf16[16,40,128]{2,1,0:T(8,128)(2,1)S(1)} %bitcast.30), channel_id=1, replica_groups=mesh['section'=4,'dp'=16,'x'=4,'core'=2] {'dp'}, dimensions={0} | all-to-all | bytes 327680 | tf_op jit(solution)/shard_map/all_to_all | solution.py:351
  160.4 0.2 norm_gradient.1
  160.6 13.0 %all_to_all.32 = bf16[16,80,256]{2,1,0:T(8,128)(2,1)S(1)} all-to-all(bf16[16,80,256]{2,1,0:T(8,128)(2,1)S(1)} %bitcast.28), channel_id=1, replica_groups=mesh['section'=4,'dp'=16,'x'=4,'core'=2] {'section','x'}, dimensions={0} | all-to-all | bytes 1310720 | tf_op jit(solution)/shard_map/all_to_all | solution.py:351
  173.6 7.5 %collective-permute-start.1 = (bf16[2,8,80,256]{3,2,1,0:T(8,128)(2,1)S(1)}, bf16[2,8,80,256]{3,2,1,0:T(8,128)(2,1)S(1)}, u32[]{:S(2)}, u32[]{:S(2)}) collective-permute-start(bf16[2,8,80,256]{3,2,1,0:T(8,128)(2,1)S(1)} %bitcast.26), channel_id=1, source_target_pairs={{0,1},{1,0},{2,3},{3,2},{4,5},{5,4},{6,7},{7,6},{8,9},{9,8},{10,11... | collective-permute-start | bytes 1966088 | tf_op jit(solution)/shard_map/ppermute | solution.py:321
  181.1 1.2 own_core_gradient.1
  182.3 0.5 collective-permute-done.1.full_ref
  182.8 2.7 %other_core_gradient.1 = (bf16[2,7,128,128]{3,2,1,0:T(8,128)(2,1)}, bf16[128,512]{1,0:T(8,128)(2,1)}) custom-call(s32[1]{0:T(128)} %bitcast.core_ref, s32[2,7]{1,0:T(2,128)S(1)} %bitcast.32, bf16[2,8,80,256]{3,2,1,0:T(8,128)(2,1)S(1)} %collective-permute-done.1.full_ref, bf16[16,2,64,1792]{3,2,1,0:T(8,128)(2,1)S(1)} %get-tuple-element.15.held_ref.acts_ref, ...), custom_call_target="tpu_custom_call" | custom-call | flops 939524096 | bytes 3670016 | tf_op jit(solution)/shard_map/other_core_gradient/pallas_call | solution.py:335
  (1 shorter events, 0.0 us)
Async XLA Ops:
  7.2 15.4 %copy-start = (s32[1,1,32,7]{2,1,3,0:T(1,128)S(1)}, s32[1,1,32,7]{2,1,3,0:T(1,128)}, u32[]{:S(2)}) copy-start(s32[1,1,32,7]{2,1,3,0:T(1,128)} %param.9) | copy-start | bytes 2692
  7.2 106.5 %all-gather.3.cloned.1.call-start = ((), (), s32[]{:S(2)}) async-start(), calls=%async_computation.6 | async-start | bytes 7798784 | tf_op jit(solution)/shard_map/all_gather | solution.py:364
  7.9 0.9 copy-start.2
  8.8 0.9 copy-start.3
  9.7 0.7 copy-start.4
  11.1 17.8 %all-to-all-start = ((bf16[32,8,128]{2,1,0:T(8,128)(2,1)}), bf16[32,8,128]{2,1,0:T(8,128)(2,1)S(1)}, u32[]{:S(2)}, u32[]{:S(2)}) async-start(bf16[32,8,128]{2,1,0:T(8,128)(2,1)} %bitcast.7), calls=%async_computation | async-start | bytes 131072 | tf_op jit(solution)/shard_map/all_to_all | solution.py:351
  29.5 24.6 %all-to-all-start.1 = ((bf16[16,8,128]{2,1,0:T(8,128)(2,1)}), bf16[16,8,128]{2,1,0:T(8,128)(2,1)S(1)}, u32[]{:S(2)}, u32[]{:S(2)}) async-start(bf16[16,8,128]{2,1,0:T(8,128)(2,1)} %get-tuple-element.13), calls=%async_computation.1 | async-start | bytes 65536 | tf_op jit(solution)/shard_map/all_to_all | solution.py:351
  54.2 15.0 %all-to-all-start.2 = ((bf16[16,8,128]{2,1,0:T(8,128)(2,1)}), bf16[16,8,128]{2,1,0:T(8,128)(2,1)S(1)}, u32[]{:S(2)}, u32[]{:S(2)}) async-start(bf16[16,8,128]{2,1,0:T(8,128)(2,1)} %get-tuple-element.14), calls=%async_computation.2 | async-start | bytes 65536 | tf_op jit(solution)/shard_map/all_to_all | solution.py:351
  113.7 3.1 %copy-start.1 = (bf16[1,2048,1792]{2,1,0:T(8,128)(2,1)S(1)}, bf16[1,2048,1792]{2,1,0:T(8,128)(2,1)}, u32[]{:S(2)}) copy-start(bf16[1,2048,1792]{2,1,0:T(8,128)(2,1)} %all-gather.3.cloned.1.call-done) | copy-start | bytes 22020100
  118.3 4.1 %collective-permute-start = (bf16[2,8,64,256]{3,2,1,0:T(8,128)(2,1)S(1)}, bf16[2,8,64,256]{3,2,1,0:T(8,128)(2,1)S(1)}, u32[]{:S(2)}, u32[]{:S(2)}) collective-permute-start(bf16[2,8,64,256]{3,2,1,0:T(8,128)(2,1)S(1)} %get-tuple-element.16), channel_id=1, source_target_pairs={{0,1},{1,0},{2,3},{3,2},{4,5},{5,4},{6,7},{7,6},{8,9},{9,8},{10,11... | collective-permute-start | bytes 1572872 | tf_op jit(solution)/shard_map/ppermute | solution.py:136
  173.6 9.3 %collective-permute-start.1 = (bf16[2,8,80,256]{3,2,1,0:T(8,128)(2,1)S(1)}, bf16[2,8,80,256]{3,2,1,0:T(8,128)(2,1)S(1)}, u32[]{:S(2)}, u32[]{:S(2)}) collective-permute-start(bf16[2,8,80,256]{3,2,1,0:T(8,128)(2,1)S(1)} %bitcast.26), channel_id=1, source_target_pairs={{0,1},{1,0},{2,3},{3,2},{4,5},{5,4},{6,7},{7,6},{8,9},{9,8},{10,11... | collective-permute-start | bytes 1966088 | tf_op jit(solution)/shard_map/ppermute | solution.py:321
Sparse Core Ops, SparseCore 0:
  10.1 103.5 all-gather.2

commit v8 on v7

--- a/solution.py
+++ b/solution.py
@@ -36,56 +36,42 @@
     scaled = cot_ref[...].astype(jnp.float32) * gain_ref[...]
     tiles = regroup(residual_ref[...].astype(jnp.float32).reshape(shape), scaled.reshape(shape))
     for half in range(2):
-        for core in range(2):
-            part = tiles[half][8 * core : 8 * core + 8].astype(out_ref.dtype)
-            out_ref[half, :, core] = part
+        out_ref[half] = tiles[half].astype(out_ref.dtype)
 
 
 def split(section, residual, cotangent, gain):
     rows, width = residual.shape
-    part = width // lax.axis_size("section")
-    block = pl.BlockSpec((rows, part), lambda i, section: (0, section[0]))
+    shape = (rows // 2, width // 2)
+    block = pl.BlockSpec(shape, lambda i, s: (s[0] // 2, lax.rem(s[0], 2)))
     out = call(
         split_kernel,
         "split_rows",
-        rows * part,
-        6 * rows * part,
+        rows * width,
+        2 * rows * width,
         grid_spec=pltpu.PrefetchScalarGridSpec(
             num_scalar_prefetch=1,
             grid=(1,),
             in_specs=[
                 block,
                 block,
-                pl.BlockSpec((1, part), lambda i, section: (0, section[0])),
+                pl.BlockSpec((1, shape[1]), lambda i, s: (0, lax.rem(s[0], 2))),
             ],
-            out_specs=pl.BlockSpec((2, rows // 16, 2, 8, part), lambda i, section: (0,) * 5),
+            out_specs=pl.BlockSpec((2, rows // 16, 8, shape[1]), lambda i, s: (0,) * 4),
         ),
-        out_shape=jax.ShapeDtypeStruct((2, rows // 16, 2, 8, part), jnp.bfloat16),
+        out_shape=jax.ShapeDtypeStruct((2, rows // 16, 8, shape[1]), jnp.bfloat16),
     )(section.astype(jnp.int32).reshape(1), residual, cotangent, gain.reshape(1, width))
-    return out.reshape(rows // 4, 8, part)
-
-
-def join_kernel(got_ref, left_ref, right_ref):
-    shards = left_ref.shape[0] // 2
-    for half in range(2):
-        for shard in range(shards):
-            for side, out_ref in enumerate((left_ref, right_ref)):
-                out_ref[2 * shard + half] = got_ref[(2 * half + side) * shards + shard]
-
-
-def join(got, planes):
-    _, rows, part = got.shape
-    shape = (planes, rows, part)
-    return call(
-        join_kernel,
-        "join_columns",
-        got.size,
-        4 * got.size,
-        grid=(1,),
-        in_specs=[pl.BlockSpec(got.shape, lambda i: (0, 0, 0))],
-        out_specs=[pl.BlockSpec(shape, lambda i: (0, 0, 0))] * 2,
-        out_shape=[jax.ShapeDtypeStruct(shape, got.dtype)] * 2,
-    )(got)
+    return out.reshape(rows // 8, 8, shape[1])
+
+
+def to_columns(ns, nz, nx):
+    pairs = []
+    for s in range(ns):
+        for z in range(nz):
+            for t in range(2 * nx):
+                source = (s * nz + z) * 2 * nx + t
+                plane = 2 * t + s % 2
+                pairs.append((source, ((z // nx * nz + plane) * nx + z % nx) * 2 + s // 2))
+    return pairs
 
 
 def partial_sums(core, acts_ref, dense_ref, out_ref):
@@ -102,7 +88,7 @@
             out_ref[half, :, at] = joined.astype(out_ref.dtype)
 
 
-def other_kernel(core_ref, acts_ref, dense_ref, left_ref, right_ref, out_ref, held_ref):
+def other_kernel(core_ref, acts_ref, dense_ref, after_ref, out_ref, held_ref):
     for group in range(acts_ref.shape[0]):
         held_ref[group] = acts_ref[group]
     partial_sums(1 - core_ref[0], acts_ref, dense_ref, out_ref)
@@ -129,10 +115,10 @@
         "other_core_matmul",
         tokens * units * width,
         2 * tokens * units,
-        in_specs=[scalar, whole, whole] + [pl.BlockSpec(memory_space=pl.ANY)] * 2,
+        in_specs=[scalar, whole, whole, pl.BlockSpec(memory_space=pl.ANY)],
         out_specs=[whole, whole],
         out_shape=(out, pltpu.VMEM(shape, every.dtype)),
-    )(core, every.reshape(shape), dense, *after)
+    )(core, every.reshape(shape), dense, after)
     got = lax.ppermute(sent, "core", [(0, 1), (1, 0)])
     own = call(
         own_kernel,
@@ -155,11 +141,10 @@
     return both.reshape(rows // 8, HALF * groups, width), held
 
 
-def cascade_kernel(parts_ref, left_ref, right_ref, out_ref, final_ref, scaled_ref):
+def cascade_kernel(parts_ref, start_ref, out_ref, final_ref, scaled_ref):
     rows, width = final_ref.shape
     shards = parts_ref.shape[0] // 4
-    start = jnp.concatenate([left_ref[...], right_ref[...]], axis=2).astype(jnp.float32)
-    start = start.reshape(rows // 8, 2, 8, width)
+    start = start_ref[...].astype(jnp.float32).reshape(rows // 8, 2, 8, width)
     current, scaled = (t.reshape(rows, width) for t in regroup(start[:, 0], start[:, 1]))
     tiles = []
     for section in range(4):
@@ -199,7 +184,7 @@
         parts.size,
         2 * parts.size,
         out_shape=(jax.ShapeDtypeStruct((rows // 8, 2, 40, 128), jnp.bfloat16), half, half),
-    )(parts, *start)
+    )(parts, start)
     return out.reshape(rows // 4, 40, 128), final, scaled
 
 
@@ -369,8 +354,10 @@
     ).astype(jnp.bfloat16)
     dense = dense.transpose(0, 2, 1, 3).reshape(hidden_blocks * blk, width)
 
-    start = exchange(split(section, residual_in, cotangent, norm_gain), ("section",) + TENSOR)
-    start = [exchange(side, "dp") for side in join(start, nz)]
+    pairs = to_columns(lax.axis_size("section"), nz, lax.axis_size("x"))
+    start = split(section, residual_in, cotangent, norm_gain)
+    start = lax.ppermute(start, ("section", "dp") + TENSOR, pairs)
+    start = exchange(start, CHIPS)
     partial_out, held = forward(core, every, dense, rows, start)
     sent, final, scaled = cascade(exchange(partial_out, CHIPS), start)
     spread = norm(core, exchange(sent, "dp"), final, scaled)

time: 193 us -> 190 us (0.984)
  waiting for transfers between devices: 72.4 us -> 70.2 us
    all_to_all x3 -> x1, waiting for transfers between devices: 26.3 us -> 3.61 us  [exchange(): return lax.all_to_all(value, axes, split_axis=0, concat_axis=0, tiled=True)]
    all_gather x1, waiting for transfers between devices: 44.5 us -> 64.4 us  [body(): every = lax.all_gather(acts, 'dp', axis=0, tiled=True)]
    ppermute x0 -> x1, starting transfers between devices: none -> 6.29 us  [body(): start = lax.ppermute(start, ('section', 'dp') + TENSOR, pairs)]
    all_to_all x3 -> x1, starting transfers between devices: 26.9 us -> 21.2 us  [exchange(): return lax.all_to_all(value, axes, split_axis=0, concat_axis=0, tiled=True)]
  transfers between devices with their start and end apart: 6 -> 5, of which waited for: 6 -> 5; matrix products, arithmetic and copies ran while one was open for 2% -> 2% of each run, Pallas kernels for 2% -> 1%
where the time goes in v8:
time: 190 us
  waiting for transfers between devices  70.2 us (37%)
  blocking collectives  50.6 us (27%)
  starting transfers between devices  37.6 us (20%)
  between operations  14.2 us (7%)
  Pallas kernels  7.24 us (4%)
  local copies, waits for them, and re-layouts  6.82 us (4%)
  other arithmetic  2.92 us (2%)
    all_gather x1, waiting for transfers between devices, body(): every = lax.all_gather(acts, 'dp', axis=0, tiled=True)  64.4 us
    all_to_all x3, blocking collectives, exchange(): return lax.all_to_all(value, axes, split_axis=0, concat_axis=0, tiled=True)  50.6 us
    all_to_all x1, starting transfers between devices, exchange(): return lax.all_to_all(value, axes, split_axis=0, concat_axis=0, tiled=True)  21.2 us
    ppermute x1, starting transfers between devices, gradient(): other = lax.ppermute(full, 'core', [(0, 1), (1, 0)])  7.55 us
    ppermute x1, starting transfers between devices, body(): start = lax.ppermute(start, ('section', 'dp') + TENSOR, pairs)  6.29 us
    unnamed x11, local copies, waits for them, and re-layouts  5.7 us
  transfers between devices with their start and end apart: 5, of which 5 were waited for; matrix products, arithmetic and copies ran while one was open for 2% of the time, Pallas kernels for 1%

profile of v8, /device:TPU:1, one launch (start us, length us, event | category | flops | bytes accessed | tf_op | source)
XLA Modules:
  0.0 189.6 jit_solution(1299303913527586280)
XLA Ops:
  7.2 0.0 copy-start
  7.2 0.0 all-gather.3.cloned.1.call-start
  7.2 0.7 all-gather.3.cloned.1.call-update
  7.9 0.0 copy-start.2
  7.9 0.9 copy-done.2
  8.8 0.0 copy-start.3
  8.8 0.9 copy-done.3
  9.7 0.0 copy-start.4
  9.7 0.7 copy-done.4
  10.4 6.3 %collective-permute-start = (bf16[16,8,256]{2,1,0:T(8,128)(2,1)S(1)}, bf16[16,8,256]{2,1,0:T(8,128)(2,1)}, u32[]{:S(2)}, u32[]{:S(2)}) collective-permute-start(bf16[16,8,256]{2,1,0:T(8,128)(2,1)S(1)} %bitcast.31), channel_id=1, source_target_pairs={{0,0},{1,16},{2,32},{3,48},{4,64},{5,80},{6,96},{7,112},{8,2},{9,1... | collective-permute-start | bytes 196616 | tf_op jit(solution)/shard_map/ppermute | solution.py:359
  16.7 0.0 copy-done
  16.8 0.1 constant_dynamic-slice_fusion
  16.8 0.1 copy.9
  16.9 1.1 bitcast_convert_fusion
  18.1 0.6 collective-permute-done
  18.7 21.2 %all-to-all-start = ((bf16[16,8,256]{2,1,0:T(8,128)(2,1)}), bf16[16,8,256]{2,1,0:T(8,128)(2,1)S(1)}, u32[]{:S(2)}, u32[]{:S(2)}) async-start(bf16[16,8,256]{2,1,0:T(8,128)(2,1)} %collective-permute-done), calls=%async_computation | async-start | bytes 131072 | tf_op jit(solution)/shard_map/all_to_all | solution.py:336
  39.9 1.8 select_reduce_fusion
  41.7 0.9 copy.10
  42.7 0.1 copy.13
  42.8 3.6 %all-to-all-done.after_ref.start_ref = bf16[16,8,256]{2,1,0:T(8,128)(2,1)S(1)} async-done(((bf16[16,8,256]{2,1,0:T(8,128)(2,1)}), bf16[16,8,256]{2,1,0:T(8,128)(2,1)S(1)}, u32[]{:S(2)}, u32[]{:S(2)}) %all-to-all-start) | async-done | bytes 65568 | tf_op jit(solution)/shard_map/all_to_all | solution.py:336
  46.4 64.4 %all-gather.3.cloned.1.call-done = bf16[1,2048,1792]{2,1,0:T(8,128)(2,1)} async-done(((bf16[1,128,1792]{2,1,0:T(8,128)(2,1)}), bf16[1,2048,1792]{2,1,0:T(8,128)(2,1)}) %all-gather.3.cloned.1.call-update) | async-done | bytes 7340048 | tf_op jit(solution)/shard_map/all_gather | solution.py:349
  110.8 0.0 copy-start.1
  110.8 3.1 %copy-done.1 = bf16[1,2048,1792]{2,1,0:T(8,128)(2,1)S(1)} copy-done((bf16[1,2048,1792]{2,1,0:T(8,128)(2,1)S(1)}, bf16[1,2048,1792]{2,1,0:T(8,128)(2,1)}, u32[]{:S(2)}) %copy-start.1) | copy-done | bytes 7340056
  113.9 1.6 other_core_matmul.1
  115.5 2.6 %collective-permute-start.1 = (bf16[2,8,64,256]{3,2,1,0:T(8,128)(2,1)S(1)}, bf16[2,8,64,256]{3,2,1,0:T(8,128)(2,1)S(1)}, u32[]{:S(2)}, u32[]{:S(2)}) collective-permute-start(bf16[2,8,64,256]{3,2,1,0:T(8,128)(2,1)S(1)} %get-tuple-element.12), channel_id=1, source_target_pairs={{0,1},{1,0},{2,3},{3,2},{4,5},{5,4},{6,7},{7,6},{8,9},{9,8},{10,11... | collective-permute-start | bytes 1572872 | tf_op jit(solution)/shard_map/ppermute | solution.py:122
  118.1 1.1 own_core_matmul.1.own_ref
  119.2 0.4 collective-permute-done.1.got_ref
  119.6 0.1 add_cores.1
  119.7 17.0 %all_to_all.20.parts_ref = bf16[16,64,256]{2,1,0:T(8,128)(2,1)S(1)} all-to-all(bf16[16,64,256]{2,1,0:T(8,128)(2,1)S(1)} %bitcast.29), channel_id=1, replica_groups=mesh['section'=4,'dp'=16,'x'=4,'core'=2] {'section','x'}, dimensions={0} | all-to-all | bytes 1048576 | tf_op jit(solution)/shard_map/all_to_all | solution.py:336
  136.8 0.3 cascade.1
  137.0 20.6 %all_to_all.21.got_ref = bf16[16,40,128]{2,1,0:T(8,128)(2,1)S(1)} all-to-all(bf16[16,40,128]{2,1,0:T(8,128)(2,1)S(1)} %bitcast.30), channel_id=1, replica_groups=mesh['section'=4,'dp'=16,'x'=4,'core'=2] {'dp'}, dimensions={0} | all-to-all | bytes 327680 | tf_op jit(solution)/shard_map/all_to_all | solution.py:336
  157.6 0.2 norm_gradient.1
  157.8 13.0 %all_to_all.22 = bf16[16,80,256]{2,1,0:T(8,128)(2,1)S(1)} all-to-all(bf16[16,80,256]{2,1,0:T(8,128)(2,1)S(1)} %bitcast.28), channel_id=1, replica_groups=mesh['section'=4,'dp'=16,'x'=4,'core'=2] {'section','x'}, dimensions={0} | all-to-all | bytes 1310720 | tf_op jit(solution)/shard_map/all_to_all | solution.py:336
  170.8 7.5 %collective-permute-start.2 = (bf16[2,8,80,256]{3,2,1,0:T(8,128)(2,1)S(1)}, bf16[2,8,80,256]{3,2,1,0:T(8,128)(2,1)S(1)}, u32[]{:S(2)}, u32[]{:S(2)}) collective-permute-start(bf16[2,8,80,256]{3,2,1,0:T(8,128)(2,1)S(1)} %bitcast.26), channel_id=1, source_target_pairs={{0,1},{1,0},{2,3},{3,2},{4,5},{5,4},{6,7},{7,6},{8,9},{9,8},{10,11... | collective-permute-start | bytes 1966088 | tf_op jit(solution)/shard_map/ppermute | solution.py:306
  178.3 1.2 own_core_gradient.1
  179.5 0.5 collective-permute-done.2.full_ref
  180.0 2.7 %other_core_gradient.1 = (bf16[2,7,128,128]{3,2,1,0:T(8,128)(2,1)}, bf16[128,512]{1,0:T(8,128)(2,1)}) custom-call(s32[1]{0:T(128)} %bitcast.core_ref, s32[2,7]{1,0:T(2,128)S(1)} %bitcast.33, bf16[2,8,80,256]{3,2,1,0:T(8,128)(2,1)S(1)} %collective-permute-done.2.full_ref, bf16[16,2,64,1792]{3,2,1,0:T(8,128)(2,1)S(1)} %get-tuple-element.11.held_ref.acts_ref, ...), custom_call_target="tpu_custom_call" | custom-call | flops 939524096 | bytes 3670016 | tf_op jit(solution)/shard_map/other_core_gradient/pallas_call | solution.py:320
  (2 shorter events, 0.0 us)
Async XLA Ops:
  7.2 9.6 %copy-start = (s32[1,1,32,7]{2,1,3,0:T(1,128)S(1)}, s32[1,1,32,7]{2,1,3,0:T(1,128)}, u32[]{:S(2)}) copy-start(s32[1,1,32,7]{2,1,3,0:T(1,128)} %param.9) | copy-start | bytes 2692
  7.2 103.7 %all-gather.3.cloned.1.call-start = ((), (), s32[]{:S(2)}) async-start(), calls=%async_computation.4 | async-start | bytes 7798784 | tf_op jit(solution)/shard_map/all_gather | solution.py:349
  7.9 0.9 copy-start.2
  8.8 0.9 copy-start.3
  9.7 0.7 copy-start.4
  10.4 8.3 %collective-permute-start = (bf16[16,8,256]{2,1,0:T(8,128)(2,1)S(1)}, bf16[16,8,256]{2,1,0:T(8,128)(2,1)}, u32[]{:S(2)}, u32[]{:S(2)}) collective-permute-start(bf16[16,8,256]{2,1,0:T(8,128)(2,1)S(1)} %bitcast.31), channel_id=1, source_target_pairs={{0,0},{1,16},{2,32},{3,48},{4,64},{5,80},{6,96},{7,112},{8,2},{9,1... | collective-permute-start | bytes 196616 | tf_op jit(solution)/shard_map/ppermute | solution.py:359
  18.7 27.7 %all-to-all-start = ((bf16[16,8,256]{2,1,0:T(8,128)(2,1)}), bf16[16,8,256]{2,1,0:T(8,128)(2,1)S(1)}, u32[]{:S(2)}, u32[]{:S(2)}) async-start(bf16[16,8,256]{2,1,0:T(8,128)(2,1)} %collective-permute-done), calls=%async_computation | async-start | bytes 131072 | tf_op jit(solution)/shard_map/all_to_all | solution.py:336
  110.8 3.1 %copy-start.1 = (bf16[1,2048,1792]{2,1,0:T(8,128)(2,1)S(1)}, bf16[1,2048,1792]{2,1,0:T(8,128)(2,1)}, u32[]{:S(2)}) copy-start(bf16[1,2048,1792]{2,1,0:T(8,128)(2,1)} %all-gather.3.cloned.1.call-done) | copy-start | bytes 22020100
  115.5 4.1 %collective-permute-start.1 = (bf16[2,8,64,256]{3,2,1,0:T(8,128)(2,1)S(1)}, bf16[2,8,64,256]{3,2,1,0:T(8,128)(2,1)S(1)}, u32[]{:S(2)}, u32[]{:S(2)}) collective-permute-start(bf16[2,8,64,256]{3,2,1,0:T(8,128)(2,1)S(1)} %get-tuple-element.12), channel_id=1, source_target_pairs={{0,1},{1,0},{2,3},{3,2},{4,5},{5,4},{6,7},{7,6},{8,9},{9,8},{10,11... | collective-permute-start | bytes 1572872 | tf_op jit(solution)/shard_map/ppermute | solution.py:122
  170.8 9.3 %collective-permute-start.2 = (bf16[2,8,80,256]{3,2,1,0:T(8,128)(2,1)S(1)}, bf16[2,8,80,256]{3,2,1,0:T(8,128)(2,1)S(1)}, u32[]{:S(2)}, u32[]{:S(2)}) collective-permute-start(bf16[2,8,80,256]{3,2,1,0:T(8,128)(2,1)S(1)} %bitcast.26), channel_id=1, source_target_pairs={{0,1},{1,0},{2,3},{3,2},{4,5},{5,4},{6,7},{7,6},{8,9},{9,8},{10,11... | collective-permute-start | bytes 1966088 | tf_op jit(solution)/shard_map/ppermute | solution.py:306
Sparse Core Ops, SparseCore 0:
  10.1 100.7 all-gather.2

commit v9 on v8

--- a/solution.py
+++ b/solution.py
@@ -74,12 +74,15 @@
     return pairs
 
 
-def partial_sums(core, acts_ref, dense_ref, out_ref):
+def partial_sums(core, acts_ref, dense_ref, out_ref, held_ref):
     groups, _, rows, units = acts_ref.shape
     width = dense_ref.shape[1]
     for step in range(groups // 8):
-        acts = acts_ref[8 * step : 8 * step + 8, core].reshape(8 * rows, units)
-        found = jnp.dot(acts, dense_ref[...], preferred_element_type=jnp.float32)
+        acts = acts_ref[8 * step : 8 * step + 8, core]
+        held_ref[8 * step : 8 * step + 8] = acts
+        found = jnp.dot(
+            acts.reshape(8 * rows, units), dense_ref[...], preferred_element_type=jnp.float32
+        )
         found = found.reshape(8, rows // 8, 8, width)
         pairs = [regroup(found[2 * q], found[2 * q + 1]) for q in range(4)]
         at = slice(32 * step, 32 * step + 32)
@@ -89,13 +92,11 @@
 
 
 def other_kernel(core_ref, acts_ref, dense_ref, after_ref, out_ref, held_ref):
-    for group in range(acts_ref.shape[0]):
-        held_ref[group] = acts_ref[group]
-    partial_sums(1 - core_ref[0], acts_ref, dense_ref, out_ref)
-
-
-def own_kernel(core_ref, held_ref, dense_ref, out_ref):
-    partial_sums(core_ref[0], held_ref, dense_ref, out_ref)
+    partial_sums(1 - core_ref[0], acts_ref, dense_ref, out_ref, held_ref)
+
+
+def own_kernel(core_ref, acts_ref, dense_ref, out_ref, held_ref):
+    partial_sums(core_ref[0], acts_ref, dense_ref, out_ref, held_ref)
 
 
 def add_kernel(own_ref, got_ref, out_ref):
@@ -106,29 +107,30 @@
     tokens, units = every.shape
     width = dense.shape[1]
     groups = tokens // rows
-    shape = (groups, 2, rows // 2, units)
+    every = every.reshape(groups, 2, rows // 2, units)
+    held = pltpu.VMEM((groups, rows // 2, units), every.dtype)
     out = jax.ShapeDtypeStruct((2, rows // 16, HALF * groups, width), jnp.bfloat16)
     whole = pl.BlockSpec(memory_space=pltpu.VMEM)
     scalar = pl.BlockSpec(memory_space=pltpu.SMEM)
-    sent, held = call(
+    sent, others = call(
         other_kernel,
         "other_core_matmul",
         tokens * units * width,
         2 * tokens * units,
         in_specs=[scalar, whole, whole, pl.BlockSpec(memory_space=pl.ANY)],
         out_specs=[whole, whole],
-        out_shape=(out, pltpu.VMEM(shape, every.dtype)),
-    )(core, every.reshape(shape), dense, after)
+        out_shape=(out, held),
+    )(core, every, dense, after)
     got = lax.ppermute(sent, "core", [(0, 1), (1, 0)])
-    own = call(
+    own, mine = call(
         own_kernel,
         "own_core_matmul",
         tokens * units * width,
         tokens * units,
         in_specs=[scalar, whole, whole],
-        out_specs=whole,
-        out_shape=jax.ShapeDtypeStruct(out.shape, jnp.float32),
-    )(core, held, dense)
+        out_specs=[whole, whole],
+        out_shape=(jax.ShapeDtypeStruct(out.shape, jnp.float32), held),
+    )(core, every, dense)
     both = call(
         add_kernel,
         "add_cores",
@@ -138,7 +140,7 @@
         out_specs=whole,
         out_shape=out,
     )(own, got)
-    return both.reshape(rows // 8, HALF * groups, width), held
+    return both.reshape(rows // 8, HALF * groups, width), mine, others
 
 
 def cascade_kernel(parts_ref, start_ref, out_ref, final_ref, scaled_ref):
@@ -234,8 +236,8 @@
     return out.reshape(4 * chips, rows + 16, width)
 
 
-def products(core, full_ref, acts_ref, turned_ref, section_at):
-    groups, _, rows, units = acts_ref.shape
+def products(full_ref, acts_ref, turned_ref, section_at):
+    groups, rows, units = acts_ref.shape
     _, tiles, _, width = full_ref.shape
 
     def regrouped(at):
@@ -250,7 +252,7 @@
     found = None
     for step in range(2):
         part = groups // 2
-        acts = acts_ref[step * part : (step + 1) * part, core].reshape(part * rows, units)
+        acts = acts_ref[step * part : (step + 1) * part].reshape(part * rows, units)
         term = jnp.dot(
             turned_ref[:, step * part * rows : (step + 1) * part * rows],
             acts,
@@ -260,9 +262,9 @@
     return found, jnp.concatenate(regrouped(section_at), axis=1)
 
 
-def near_kernel(core_ref, full_ref, acts_ref, found_ref, section_ref, turned_ref):
+def near_kernel(full_ref, acts_ref, found_ref, section_ref, turned_ref):
     rows = full_ref.shape[2]
-    found, section = products(core_ref[0], full_ref, acts_ref, turned_ref, rows - 16)
+    found, section = products(full_ref, acts_ref, turned_ref, rows - 16)
     found_ref[...] = found
     section_ref[...] = section.astype(section_ref.dtype)
 
@@ -275,27 +277,37 @@
     near_ref,
     near_section_ref,
     out_ref,
-    section_ref,
+    section_out_ref,
     turned_ref,
     found_ref,
+    blocks_ref,
+    section_ref,
+    sems,
 ):
     cols, keep, blk, _ = out_ref.shape
+    copies = [pltpu.make_async_copy(section_ref, section_out_ref, sems.at[cols])]
+    for c in range(cols):
+        copies.append(pltpu.make_async_copy(blocks_ref.at[c], out_ref.at[c], sems.at[c]))
     core, rows = core_ref[0], full_ref.shape[2]
-    found, section = products(1 - core, full_ref, acts_ref, turned_ref, rows - 8)
+    found, section = products(full_ref, acts_ref, turned_ref, rows - 8)
     half = section_ref.shape[0] // 2
     section_ref[pl.ds(pl.multiple_of(core * half, half), half)] = near_section_ref[...]
     section_ref[pl.ds(pl.multiple_of((1 - core) * half, half), half)] = section.astype(
         section_ref.dtype
     )
+    copies[0].start()
     found_ref[...] = (near_ref[...] + found).astype(found_ref.dtype)
     for c in range(cols):
         for slot in range(keep):
             start = pl.multiple_of(kept_ref[c, slot] * blk, blk)
-            out_ref[c, slot] = found_ref[c * blk : (c + 1) * blk, pl.ds(start, blk)].T
-
-
-def gradient(core, own_kept, full, held, blk):
-    groups, _, rows, units = held.shape
+            blocks_ref[c, slot] = found_ref[c * blk : (c + 1) * blk, pl.ds(start, blk)].T
+        copies[1 + c].start()
+    for copy in copies:
+        copy.wait()
+
+
+def gradient(core, own_kept, full, mine, others, blk):
+    groups, rows, units = mine.shape
     chips, _, width = full.shape
     cols, keep = own_kept.shape
     full = full.reshape(2, chips // 2, *full.shape[1:])
@@ -308,28 +320,34 @@
         near_kernel,
         "own_core_gradient",
         flops,
-        held.size,
-        in_specs=[scalar, whole, whole],
+        2 * mine.size,
+        in_specs=[whole, whole],
         out_specs=[whole, whole],
         scratch_shapes=[turned],
         out_shape=(
             jax.ShapeDtypeStruct((width, units), jnp.float32),
             jax.ShapeDtypeStruct((rows, 2 * width), jnp.bfloat16),
         ),
-    )(core, full, held)
+    )(full, mine)
     return call(
         far_kernel,
         "other_core_gradient",
         flops,
-        held.size,
+        2 * mine.size,
         in_specs=[scalar, scalar] + [whole] * 4,
-        out_specs=[whole, whole],
-        scratch_shapes=[turned, pltpu.VMEM((width, units), jnp.bfloat16)],
+        out_specs=[pl.BlockSpec(memory_space=pl.ANY)] * 2,
+        scratch_shapes=[
+            turned,
+            pltpu.VMEM((width, units), jnp.bfloat16),
+            pltpu.VMEM((cols, keep, blk, blk), jnp.bfloat16),
+            pltpu.VMEM((2 * rows, 2 * width), jnp.bfloat16),
+            pltpu.SemaphoreType.DMA((cols + 1,)),
+        ],
         out_shape=(
             jax.ShapeDtypeStruct((cols, keep, blk, blk), jnp.bfloat16),
             jax.ShapeDtypeStruct((2 * rows, 2 * width), jnp.bfloat16),
         ),
-    )(core, own_kept, other, held, found, section)
+    )(core, own_kept, other, others, found, section)
 
 
 def exchange(value, axes):
@@ -358,10 +376,10 @@
     start = split(section, residual_in, cotangent, norm_gain)
     start = lax.ppermute(start, ("section", "dp") + TENSOR, pairs)
     start = exchange(start, CHIPS)
-    partial_out, held = forward(core, every, dense, rows, start)
+    partial_out, mine, others = forward(core, every, dense, rows, start)
     sent, final, scaled = cascade(exchange(partial_out, CHIPS), start)
     spread = norm(core, exchange(sent, "dp"), final, scaled)
-    grads, section_out = gradient(core, own_kept, exchange(spread, CHIPS), held, blk)
+    grads, section_out = gradient(core, own_kept, exchange(spread, CHIPS), mine, others, blk)
     return (section_out[None], grads[None, None])
 
 

time: 190 us -> 190 us (level)
  no operation moved by 1% of the time
where the time goes in v9:
time: 190 us; the launch traced here: 189 us
  waiting for transfers between devices  70.3 us (37%)
  blocking collectives  50.5 us (27%)
  starting transfers between devices  37.6 us (20%)
  between operations  14.2 us (7%)
  local copies, waits for them, and re-layouts  6.82 us (4%)
  Pallas kernels  6.67 us (4%)
  other arithmetic  2.92 us (2%)
    all_gather x1, waiting for transfers between devices, body(): every = lax.all_gather(acts, 'dp', axis=0, tiled=True)  64.4 us
    all_to_all x3, blocking collectives, exchange(): return lax.all_to_all(value, axes, split_axis=0, concat_axis=0, tiled=True)  50.5 us
    all_to_all x1, starting transfers between devices, exchange(): return lax.all_to_all(value, axes, split_axis=0, concat_axis=0, tiled=True)  21.2 us
    ppermute x1, starting transfers between devices, gradient(): other = lax.ppermute(full, 'core', [(0, 1), (1, 0)])  7.55 us
    ppermute x1, starting transfers between devices, body(): start = lax.ppermute(start, ('section', 'dp') + TENSOR, pairs)  6.29 us
    unnamed x11, local copies, waits for them, and re-layouts  5.7 us
  transfers between devices with their start and end apart: 5, of which 5 were waited for; matrix products, arithmetic and copies ran while one was open for 2% of the time, Pallas kernels for 1%

profile of v9, /device:TPU:1, one launch (start us, length us, event | category | flops | bytes accessed | tf_op | source)
XLA Modules:
  0.0 189.1 jit_solution(7022439687717743663)
XLA Ops:
  7.2 0.0 copy-start
  7.2 0.0 all-gather.3.cloned.1.call-start
  7.2 0.7 all-gather.3.cloned.1.call-update
  7.9 0.0 copy-start.2
  7.9 0.9 copy-done.2
  8.8 0.0 copy-start.3
  8.8 0.9 copy-done.3
  9.7 0.0 copy-start.4
  9.7 0.7 copy-done.4
  10.4 6.3 %collective-permute-start = (bf16[16,8,256]{2,1,0:T(8,128)(2,1)S(1)}, bf16[16,8,256]{2,1,0:T(8,128)(2,1)}, u32[]{:S(2)}, u32[]{:S(2)}) collective-permute-start(bf16[16,8,256]{2,1,0:T(8,128)(2,1)S(1)} %bitcast.32), channel_id=1, source_target_pairs={{0,0},{1,16},{2,32},{3,48},{4,64},{5,80},{6,96},{7,112},{8,2},{9,1... | collective-permute-start | bytes 196616 | tf_op jit(solution)/shard_map/ppermute | solution.py:377
  16.7 0.0 copy-done
  16.8 0.1 constant_dynamic-slice_fusion
  16.8 0.1 copy.9
  16.9 1.1 bitcast_convert_fusion
  18.1 0.6 collective-permute-done
  18.7 21.2 %all-to-all-start = ((bf16[16,8,256]{2,1,0:T(8,128)(2,1)}), bf16[16,8,256]{2,1,0:T(8,128)(2,1)S(1)}, u32[]{:S(2)}, u32[]{:S(2)}) async-start(bf16[16,8,256]{2,1,0:T(8,128)(2,1)} %collective-permute-done), calls=%async_computation | async-start | bytes 131072 | tf_op jit(solution)/shard_map/all_to_all | solution.py:354
  39.9 1.8 select_reduce_fusion
  41.7 0.9 copy.10
  42.7 0.1 copy.13
  42.8 3.6 %all-to-all-done.after_ref.start_ref = bf16[16,8,256]{2,1,0:T(8,128)(2,1)S(1)} async-done(((bf16[16,8,256]{2,1,0:T(8,128)(2,1)}), bf16[16,8,256]{2,1,0:T(8,128)(2,1)S(1)}, u32[]{:S(2)}, u32[]{:S(2)}) %all-to-all-start) | async-done | bytes 65568 | tf_op jit(solution)/shard_map/all_to_all | solution.py:354
  46.4 64.4 %all-gather.3.cloned.1.call-done = bf16[1,2048,1792]{2,1,0:T(8,128)(2,1)} async-done(((bf16[1,128,1792]{2,1,0:T(8,128)(2,1)}), bf16[1,2048,1792]{2,1,0:T(8,128)(2,1)}) %all-gather.3.cloned.1.call-update) | async-done | bytes 7340048 | tf_op jit(solution)/shard_map/all_gather | solution.py:367
  110.8 0.0 copy-start.1
  110.8 3.1 %copy-done.1 = bf16[1,2048,1792]{2,1,0:T(8,128)(2,1)S(1)} copy-done((bf16[1,2048,1792]{2,1,0:T(8,128)(2,1)S(1)}, bf16[1,2048,1792]{2,1,0:T(8,128)(2,1)}, u32[]{:S(2)}) %copy-start.1) | copy-done | bytes 7340056
  113.9 1.1 other_core_matmul.1
  115.1 2.6 %collective-permute-start.1 = (bf16[2,8,64,256]{3,2,1,0:T(8,128)(2,1)S(1)}, bf16[2,8,64,256]{3,2,1,0:T(8,128)(2,1)S(1)}, u32[]{:S(2)}, u32[]{:S(2)}) collective-permute-start(bf16[2,8,64,256]{3,2,1,0:T(8,128)(2,1)S(1)} %get-tuple-element.14), channel_id=1, source_target_pairs={{0,1},{1,0},{2,3},{3,2},{4,5},{5,4},{6,7},{7,6},{8,9},{9,8},{10,11... | collective-permute-start | bytes 1572872 | tf_op jit(solution)/shard_map/ppermute | solution.py:124
  117.6 1.1 own_core_matmul.1
  118.8 0.4 collective-permute-done.1.got_ref
  119.2 0.1 add_cores.1
  119.2 17.0 %all_to_all.20.parts_ref = bf16[16,64,256]{2,1,0:T(8,128)(2,1)S(1)} all-to-all(bf16[16,64,256]{2,1,0:T(8,128)(2,1)S(1)} %bitcast.30), channel_id=1, replica_groups=mesh['section'=4,'dp'=16,'x'=4,'core'=2] {'section','x'}, dimensions={0} | all-to-all | bytes 1048576 | tf_op jit(solution)/shard_map/all_to_all | solution.py:354
  136.3 0.3 cascade.1
  136.5 20.6 %all_to_all.21.got_ref = bf16[16,40,128]{2,1,0:T(8,128)(2,1)S(1)} all-to-all(bf16[16,40,128]{2,1,0:T(8,128)(2,1)S(1)} %bitcast.31), channel_id=1, replica_groups=mesh['section'=4,'dp'=16,'x'=4,'core'=2] {'dp'}, dimensions={0} | all-to-all | bytes 327680 | tf_op jit(solution)/shard_map/all_to_all | solution.py:354
  157.1 0.2 norm_gradient.1
  157.3 13.0 %all_to_all.22 = bf16[16,80,256]{2,1,0:T(8,128)(2,1)S(1)} all-to-all(bf16[16,80,256]{2,1,0:T(8,128)(2,1)S(1)} %bitcast.27), channel_id=1, replica_groups=mesh['section'=4,'dp'=16,'x'=4,'core'=2] {'section','x'}, dimensions={0} | all-to-all | bytes 1310720 | tf_op jit(solution)/shard_map/all_to_all | solution.py:354
  170.3 7.5 %collective-permute-start.2 = (bf16[2,8,80,256]{3,2,1,0:T(8,128)(2,1)S(1)}, bf16[2,8,80,256]{3,2,1,0:T(8,128)(2,1)S(1)}, u32[]{:S(2)}, u32[]{:S(2)}) collective-permute-start(bf16[2,8,80,256]{3,2,1,0:T(8,128)(2,1)S(1)} %bitcast.28), channel_id=1, source_target_pairs={{0,1},{1,0},{2,3},{3,2},{4,5},{5,4},{6,7},{7,6},{8,9},{9,8},{10,11... | collective-permute-start | bytes 1966088 | tf_op jit(solution)/shard_map/ppermute | solution.py:318
  177.8 1.2 own_core_gradient.1
  179.0 0.5 collective-permute-done.2.full_ref
  179.5 2.7 %other_core_gradient.1 = (bf16[2,7,128,128]{3,2,1,0:T(8,128)(2,1)}, bf16[128,512]{1,0:T(8,128)(2,1)}) custom-call(s32[1]{0:T(128)} %bitcast.core_ref, s32[2,7]{1,0:T(2,128)S(1)} %bitcast.34, bf16[2,8,80,256]{3,2,1,0:T(8,128)(2,1)S(1)} %collective-permute-done.2.full_ref, bf16[16,64,1792]{2,1,0:T(8,128)(2,1)S(1)} %get-tuple-element.18.acts_ref, ...), custom_call_target="tpu_custom_call" | custom-call | flops 939524096 | bytes 3670016 | tf_op jit(solution)/shard_map/other_core_gradient/pallas_call | solution.py:332
  (2 shorter events, 0.0 us)
Async XLA Ops:
  7.2 9.6 %copy-start = (s32[1,1,32,7]{2,1,3,0:T(1,128)S(1)}, s32[1,1,32,7]{2,1,3,0:T(1,128)}, u32[]{:S(2)}) copy-start(s32[1,1,32,7]{2,1,3,0:T(1,128)} %param.9) | copy-start | bytes 2692
  7.2 103.7 %all-gather.3.cloned.1.call-start = ((), (), s32[]{:S(2)}) async-start(), calls=%async_computation.4 | async-start | bytes 7798784 | tf_op jit(solution)/shard_map/all_gather | solution.py:367
  7.9 0.9 copy-start.2
  8.8 0.9 copy-start.3
  9.7 0.7 copy-start.4
  10.4 8.3 %collective-permute-start = (bf16[16,8,256]{2,1,0:T(8,128)(2,1)S(1)}, bf16[16,8,256]{2,1,0:T(8,128)(2,1)}, u32[]{:S(2)}, u32[]{:S(2)}) collective-permute-start(bf16[16,8,256]{2,1,0:T(8,128)(2,1)S(1)} %bitcast.32), channel_id=1, source_target_pairs={{0,0},{1,16},{2,32},{3,48},{4,64},{5,80},{6,96},{7,112},{8,2},{9,1... | collective-permute-start | bytes 196616 | tf_op jit(solution)/shard_map/ppermute | solution.py:377
  18.7 27.7 %all-to-all-start = ((bf16[16,8,256]{2,1,0:T(8,128)(2,1)}), bf16[16,8,256]{2,1,0:T(8,128)(2,1)S(1)}, u32[]{:S(2)}, u32[]{:S(2)}) async-start(bf16[16,8,256]{2,1,0:T(8,128)(2,1)} %collective-permute-done), calls=%async_computation | async-start | bytes 131072 | tf_op jit(solution)/shard_map/all_to_all | solution.py:354
  110.8 3.1 %copy-start.1 = (bf16[1,2048,1792]{2,1,0:T(8,128)(2,1)S(1)}, bf16[1,2048,1792]{2,1,0:T(8,128)(2,1)}, u32[]{:S(2)}) copy-start(bf16[1,2048,1792]{2,1,0:T(8,128)(2,1)} %all-gather.3.cloned.1.call-done) | copy-start | bytes 22020100
  115.1 4.1 %collective-permute-start.1 = (bf16[2,8,64,256]{3,2,1,0:T(8,128)(2,1)S(1)}, bf16[2,8,64,256]{3,2,1,0:T(8,128)(2,1)S(1)}, u32[]{:S(2)}, u32[]{:S(2)}) collective-permute-start(bf16[2,8,64,256]{3,2,1,0:T(8,128)(2,1)S(1)} %get-tuple-element.14), channel_id=1, source_target_pairs={{0,1},{1,0},{2,3},{3,2},{4,5},{5,4},{6,7},{7,6},{8,9},{9,8},{10,11... | collective-permute-start | bytes 1572872 | tf_op jit(solution)/shard_map/ppermute | solution.py:124
  170.3 9.3 %collective-permute-start.2 = (bf16[2,8,80,256]{3,2,1,0:T(8,128)(2,1)S(1)}, bf16[2,8,80,256]{3,2,1,0:T(8,128)(2,1)S(1)}, u32[]{:S(2)}, u32[]{:S(2)}) collective-permute-start(bf16[2,8,80,256]{3,2,1,0:T(8,128)(2,1)S(1)} %bitcast.28), channel_id=1, source_target_pairs={{0,1},{1,0},{2,3},{3,2},{4,5},{5,4},{6,7},{7,6},{8,9},{9,8},{10,11... | collective-permute-start | bytes 1966088 | tf_op jit(solution)/shard_map/ppermute | solution.py:318
Sparse Core Ops, SparseCore 0:
  10.1 100.7 all-gather.2

commit v10 on v9

--- a/solution.py
+++ b/solution.py
@@ -9,6 +9,7 @@
 D = 4096
 TENSOR = ("x", "core")
 CHIPS = ("section", "x")
+TURNED = ("x", "section")
 HALF = 4
 
 
@@ -100,7 +101,11 @@
 
 
 def add_kernel(own_ref, got_ref, out_ref):
-    out_ref[...] = (own_ref[...] + got_ref[...].astype(jnp.float32)).astype(out_ref.dtype)
+    both = (own_ref[...] + got_ref[...].astype(jnp.float32)).astype(out_ref.dtype)
+    chips = out_ref.shape[0]
+    for half in range(2):
+        for part in range(2):
+            out_ref[:, half, part] = both[half, part * chips : (part + 1) * chips]
 
 
 def forward(core, every, dense, rows, after):
@@ -138,7 +143,7 @@
         8 * out.size,
         in_specs=[whole] * 2,
         out_specs=whole,
-        out_shape=out,
+        out_shape=jax.ShapeDtypeStruct((out.shape[1] // 2, 2, 2, *out.shape[2:]), out.dtype),
     )(own, got)
     return both.reshape(rows // 8, HALF * groups, width), mine, others
 
@@ -150,9 +155,9 @@
     current, scaled = (t.reshape(rows, width) for t in regroup(start[:, 0], start[:, 1]))
     tiles = []
     for section in range(4):
-        contrib = parts_ref[section * shards].astype(jnp.float32)
+        contrib = parts_ref[section].astype(jnp.float32)
         for shard in range(1, shards):
-            contrib += parts_ref[section * shards + shard].astype(jnp.float32)
+            contrib += parts_ref[4 * shard + section].astype(jnp.float32)
         current = (current + contrib).astype(jnp.bfloat16).astype(jnp.float32)
         tiles.append(current.reshape(rows // 8, 8, width))
     final_ref[...] = current
@@ -217,7 +222,7 @@
             same = jnp.where(first, tile[:, 0], tile[:, 1])
             other = jnp.where(first, tile[:, 1], tile[:, 0])
             joined = jnp.concatenate([spread, same, other], axis=1)
-            out_ref[2 * at + parity] = joined.astype(out_ref.dtype)
+            out_ref[:, 2 * at + parity] = joined.astype(out_ref.dtype)
 
 
 def norm(core, got, final, scaled):
@@ -231,18 +236,22 @@
         4 * got.size,
         in_specs=[pl.BlockSpec(memory_space=pltpu.SMEM), whole, whole, whole],
         out_specs=whole,
-        out_shape=jax.ShapeDtypeStruct((4, chips, rows + 16, width), jnp.bfloat16),
+        out_shape=jax.ShapeDtypeStruct((chips, 4, rows + 16, width), jnp.bfloat16),
     )(core, got, final, scaled)
     return out.reshape(4 * chips, rows + 16, width)
 
 
 def products(full_ref, acts_ref, turned_ref, section_at):
     groups, rows, units = acts_ref.shape
-    _, tiles, _, width = full_ref.shape
+    tiles, width = 2 * full_ref.shape[0], full_ref.shape[4]
 
     def regrouped(at):
-        even = full_ref[0, :, at : at + 8].astype(jnp.float32)
-        odd = full_ref[1, :, at : at + 8].astype(jnp.float32)
+        even, odd = (
+            jnp.concatenate(
+                [full_ref[:, half, part, at : at + 8] for part in range(2)], axis=0
+            ).astype(jnp.float32)
+            for half in range(2)
+        )
         return [t.reshape(8 * tiles, width) for t in regroup(even, odd)]
 
     for two in range(groups // 2):
@@ -263,7 +272,7 @@
 
 
 def near_kernel(full_ref, acts_ref, found_ref, section_ref, turned_ref):
-    rows = full_ref.shape[2]
+    rows = full_ref.shape[3]
     found, section = products(full_ref, acts_ref, turned_ref, rows - 16)
     found_ref[...] = found
     section_ref[...] = section.astype(section_ref.dtype)
@@ -288,7 +297,7 @@
     copies = [pltpu.make_async_copy(section_ref, section_out_ref, sems.at[cols])]
     for c in range(cols):
         copies.append(pltpu.make_async_copy(blocks_ref.at[c], out_ref.at[c], sems.at[c]))
-    core, rows = core_ref[0], full_ref.shape[2]
+    core, rows = core_ref[0], full_ref.shape[3]
     found, section = products(full_ref, acts_ref, turned_ref, rows - 8)
     half = section_ref.shape[0] // 2
     section_ref[pl.ds(pl.multiple_of(core * half, half), half)] = near_section_ref[...]
@@ -310,7 +319,7 @@
     groups, rows, units = mine.shape
     chips, _, width = full.shape
     cols, keep = own_kept.shape
-    full = full.reshape(2, chips // 2, *full.shape[1:])
+    full = full.reshape(chips // 4, 2, 2, *full.shape[1:])
     whole = pl.BlockSpec(memory_space=pltpu.VMEM)
     scalar = pl.BlockSpec(memory_space=pltpu.SMEM)
     turned = pltpu.VMEM((width, groups * rows), jnp.bfloat16)
@@ -377,9 +386,9 @@
     start = lax.ppermute(start, ("section", "dp") + TENSOR, pairs)
     start = exchange(start, CHIPS)
     partial_out, mine, others = forward(core, every, dense, rows, start)
-    sent, final, scaled = cascade(exchange(partial_out, CHIPS), start)
+    sent, final, scaled = cascade(exchange(partial_out, TURNED), start)
     spread = norm(core, exchange(sent, "dp"), final, scaled)
-    grads, section_out = gradient(core, own_kept, exchange(spread, CHIPS), mine, others, blk)
+    grads, section_out = gradient(core, own_kept, exchange(spread, TURNED), mine, others, blk)
     return (section_out[None], grads[None, None])
 
 

time: 190 us -> 190 us (level)
  no operation moved by 1% of the time
where the time goes in v10:
time: 190 us; the launch traced here: 189 us
  waiting for transfers between devices  70.3 us (37%)
  blocking collectives  50.4 us (27%)
  starting transfers between devices  37.9 us (20%)
  between operations  14.2 us (7%)
  local copies, waits for them, and re-layouts  6.82 us (4%)
  Pallas kernels  6.68 us (4%)
  other arithmetic  2.92 us (2%)
    all_gather x1, waiting for transfers between devices, body(): every = lax.all_gather(acts, 'dp', axis=0, tiled=True)  64.4 us
    all_to_all x3, blocking collectives, exchange(): return lax.all_to_all(value, axes, split_axis=0, concat_axis=0, tiled=True)  50.4 us
    all_to_all x1, starting transfers between devices, exchange(): return lax.all_to_all(value, axes, split_axis=0, concat_axis=0, tiled=True)  21.2 us
    ppermute x1, starting transfers between devices, gradient(): other = lax.ppermute(full, 'core', [(0, 1), (1, 0)])  7.76 us
    ppermute x1, starting transfers between devices, body(): start = lax.ppermute(start, ('section', 'dp') + TENSOR, pairs)  6.29 us
    unnamed x11, local copies, waits for them, and re-layouts  5.7 us
  transfers between devices with their start and end apart: 5, of which 5 were waited for; matrix products, arithmetic and copies ran while one was open for 2% of the time, Pallas kernels for 1%

profile of v10, /device:TPU:1, one launch (start us, length us, event | category | flops | bytes accessed | tf_op | source)
XLA Modules:
  0.0 189.1 jit_solution(15358605808346081454)
XLA Ops:
  7.2 0.0 copy-start
  7.2 0.0 all-gather.3.cloned.1.call-start
  7.2 0.7 all-gather.3.cloned.1.call-update
  7.9 0.0 copy-start.2
  7.9 0.9 copy-done.2
  8.8 0.0 copy-start.3
  8.8 0.9 copy-done.3
  9.7 0.0 copy-start.4
  9.7 0.7 copy-done.4
  10.4 6.3 %collective-permute-start = (bf16[16,8,256]{2,1,0:T(8,128)(2,1)S(1)}, bf16[16,8,256]{2,1,0:T(8,128)(2,1)}, u32[]{:S(2)}, u32[]{:S(2)}) collective-permute-start(bf16[16,8,256]{2,1,0:T(8,128)(2,1)S(1)} %bitcast.32), channel_id=1, source_target_pairs={{0,0},{1,16},{2,32},{3,48},{4,64},{5,80},{6,96},{7,112},{8,2},{9,1... | collective-permute-start | bytes 196616 | tf_op jit(solution)/shard_map/ppermute | solution.py:386
  16.7 0.0 copy-done
  16.8 0.1 constant_dynamic-slice_fusion
  16.8 0.1 copy.9
  16.9 1.1 bitcast_convert_fusion
  18.1 0.6 collective-permute-done
  18.7 21.2 %all-to-all-start = ((bf16[16,8,256]{2,1,0:T(8,128)(2,1)}), bf16[16,8,256]{2,1,0:T(8,128)(2,1)S(1)}, u32[]{:S(2)}, u32[]{:S(2)}) async-start(bf16[16,8,256]{2,1,0:T(8,128)(2,1)} %collective-permute-done), calls=%async_computation | async-start | bytes 131072 | tf_op jit(solution)/shard_map/all_to_all | solution.py:363
  39.9 1.8 select_reduce_fusion
  41.7 0.9 copy.10
  42.7 0.1 copy.13
  42.8 3.6 %all-to-all-done.after_ref.start_ref = bf16[16,8,256]{2,1,0:T(8,128)(2,1)S(1)} async-done(((bf16[16,8,256]{2,1,0:T(8,128)(2,1)}), bf16[16,8,256]{2,1,0:T(8,128)(2,1)S(1)}, u32[]{:S(2)}, u32[]{:S(2)}) %all-to-all-start) | async-done | bytes 65568 | tf_op jit(solution)/shard_map/all_to_all | solution.py:363
  46.4 64.4 %all-gather.3.cloned.1.call-done = bf16[1,2048,1792]{2,1,0:T(8,128)(2,1)} async-done(((bf16[1,128,1792]{2,1,0:T(8,128)(2,1)}), bf16[1,2048,1792]{2,1,0:T(8,128)(2,1)}) %all-gather.3.cloned.1.call-update) | async-done | bytes 7340048 | tf_op jit(solution)/shard_map/all_gather | solution.py:376
  110.8 0.0 copy-start.1
  110.8 3.1 %copy-done.1 = bf16[1,2048,1792]{2,1,0:T(8,128)(2,1)S(1)} copy-done((bf16[1,2048,1792]{2,1,0:T(8,128)(2,1)S(1)}, bf16[1,2048,1792]{2,1,0:T(8,128)(2,1)}, u32[]{:S(2)}) %copy-start.1) | copy-done | bytes 7340056
  113.9 1.1 other_core_matmul.1
  115.1 2.6 %collective-permute-start.1 = (bf16[2,8,64,256]{3,2,1,0:T(8,128)(2,1)S(1)}, bf16[2,8,64,256]{3,2,1,0:T(8,128)(2,1)S(1)}, u32[]{:S(2)}, u32[]{:S(2)}) collective-permute-start(bf16[2,8,64,256]{3,2,1,0:T(8,128)(2,1)S(1)} %get-tuple-element.14), channel_id=1, source_target_pairs={{0,1},{1,0},{2,3},{3,2},{4,5},{5,4},{6,7},{7,6},{8,9},{9,8},{10,11... | collective-permute-start | bytes 1572872 | tf_op jit(solution)/shard_map/ppermute | solution.py:129
  117.6 1.1 own_core_matmul.1
  118.8 0.4 collective-permute-done.1.got_ref
  119.2 0.1 add_cores.1
  119.2 16.7 %all_to_all.20.parts_ref = bf16[16,64,256]{2,1,0:T(8,128)(2,1)S(1)} all-to-all(bf16[16,64,256]{2,1,0:T(8,128)(2,1)S(1)} %bitcast.30), channel_id=1, replica_groups=mesh['section'=4,'dp'=16,'x'=4,'core'=2] {'x','section'}, dimensions={0} | all-to-all | bytes 1048576 | tf_op jit(solution)/shard_map/all_to_all | solution.py:363
  135.9 0.3 cascade.1
  136.2 20.5 %all_to_all.21.got_ref = bf16[16,40,128]{2,1,0:T(8,128)(2,1)S(1)} all-to-all(bf16[16,40,128]{2,1,0:T(8,128)(2,1)S(1)} %bitcast.31), channel_id=1, replica_groups=mesh['section'=4,'dp'=16,'x'=4,'core'=2] {'dp'}, dimensions={0} | all-to-all | bytes 327680 | tf_op jit(solution)/shard_map/all_to_all | solution.py:363
  156.7 0.2 norm_gradient.1
  156.9 13.1 %all_to_all.22 = bf16[16,80,256]{2,1,0:T(8,128)(2,1)S(1)} all-to-all(bf16[16,80,256]{2,1,0:T(8,128)(2,1)S(1)} %bitcast.27), channel_id=1, replica_groups=mesh['section'=4,'dp'=16,'x'=4,'core'=2] {'x','section'}, dimensions={0} | all-to-all | bytes 1310720 | tf_op jit(solution)/shard_map/all_to_all | solution.py:363
  170.1 7.8 %collective-permute-start.2 = (bf16[4,2,2,80,256]{4,3,2,1,0:T(8,128)(2,1)S(1)}, bf16[4,2,2,80,256]{4,3,2,1,0:T(8,128)(2,1)S(1)}, u32[]{:S(2)}, u32[]{:S(2)}) collective-permute-start(bf16[4,2,2,80,256]{4,3,2,1,0:T(8,128)(2,1)S(1)} %bitcast.28), channel_id=1, source_target_pairs={{0,1},{1,0},{2,3},{3,2},{4,5},{5,4},{6,7},{7,6},{8,9},{9,8},{10,11... | collective-permute-start | bytes 1966088 | tf_op jit(solution)/shard_map/ppermute | solution.py:327
  177.8 1.2 own_core_gradient.1
  179.0 0.5 collective-permute-done.2.full_ref
  179.5 2.7 %other_core_gradient.1 = (bf16[2,7,128,128]{3,2,1,0:T(8,128)(2,1)}, bf16[128,512]{1,0:T(8,128)(2,1)}) custom-call(s32[1]{0:T(128)} %bitcast.core_ref, s32[2,7]{1,0:T(2,128)S(1)} %bitcast.34, bf16[4,2,2,80,256]{4,3,2,1,0:T(8,128)(2,1)S(1)} %collective-permute-done.2.full_ref, bf16[16,64,1792]{2,1,0:T(8,128)(2,1)S(1)} %get-tuple-element.18.acts_ref, ...), custom_call_target="tpu_custom_call" | custom-call | flops 939524096 | bytes 3670016 | tf_op jit(solution)/shard_map/other_core_gradient/pallas_call | solution.py:341
  (2 shorter events, 0.0 us)
Async XLA Ops:
  7.2 9.6 %copy-start = (s32[1,1,32,7]{2,1,3,0:T(1,128)S(1)}, s32[1,1,32,7]{2,1,3,0:T(1,128)}, u32[]{:S(2)}) copy-start(s32[1,1,32,7]{2,1,3,0:T(1,128)} %param.9) | copy-start | bytes 2692
  7.2 103.7 %all-gather.3.cloned.1.call-start = ((), (), s32[]{:S(2)}) async-start(), calls=%async_computation.4 | async-start | bytes 7798784 | tf_op jit(solution)/shard_map/all_gather | solution.py:376
  7.9 0.9 copy-start.2
  8.8 0.9 copy-start.3
  9.7 0.7 copy-start.4
  10.4 8.3 %collective-permute-start = (bf16[16,8,256]{2,1,0:T(8,128)(2,1)S(1)}, bf16[16,8,256]{2,1,0:T(8,128)(2,1)}, u32[]{:S(2)}, u32[]{:S(2)}) collective-permute-start(bf16[16,8,256]{2,1,0:T(8,128)(2,1)S(1)} %bitcast.32), channel_id=1, source_target_pairs={{0,0},{1,16},{2,32},{3,48},{4,64},{5,80},{6,96},{7,112},{8,2},{9,1... | collective-permute-start | bytes 196616 | tf_op jit(solution)/shard_map/ppermute | solution.py:386
  18.7 27.7 %all-to-all-start = ((bf16[16,8,256]{2,1,0:T(8,128)(2,1)}), bf16[16,8,256]{2,1,0:T(8,128)(2,1)S(1)}, u32[]{:S(2)}, u32[]{:S(2)}) async-start(bf16[16,8,256]{2,1,0:T(8,128)(2,1)} %collective-permute-done), calls=%async_computation | async-start | bytes 131072 | tf_op jit(solution)/shard_map/all_to_all | solution.py:363
  110.8 3.1 %copy-start.1 = (bf16[1,2048,1792]{2,1,0:T(8,128)(2,1)S(1)}, bf16[1,2048,1792]{2,1,0:T(8,128)(2,1)}, u32[]{:S(2)}) copy-start(bf16[1,2048,1792]{2,1,0:T(8,128)(2,1)} %all-gather.3.cloned.1.call-done) | copy-start | bytes 22020100
  115.1 4.1 %collective-permute-start.1 = (bf16[2,8,64,256]{3,2,1,0:T(8,128)(2,1)S(1)}, bf16[2,8,64,256]{3,2,1,0:T(8,128)(2,1)S(1)}, u32[]{:S(2)}, u32[]{:S(2)}) collective-permute-start(bf16[2,8,64,256]{3,2,1,0:T(8,128)(2,1)S(1)} %get-tuple-element.14), channel_id=1, source_target_pairs={{0,1},{1,0},{2,3},{3,2},{4,5},{5,4},{6,7},{7,6},{8,9},{9,8},{10,11... | collective-permute-start | bytes 1572872 | tf_op jit(solution)/shard_map/ppermute | solution.py:129
  170.1 9.5 %collective-permute-start.2 = (bf16[4,2,2,80,256]{4,3,2,1,0:T(8,128)(2,1)S(1)}, bf16[4,2,2,80,256]{4,3,2,1,0:T(8,128)(2,1)S(1)}, u32[]{:S(2)}, u32[]{:S(2)}) collective-permute-start(bf16[4,2,2,80,256]{4,3,2,1,0:T(8,128)(2,1)S(1)} %bitcast.28), channel_id=1, source_target_pairs={{0,1},{1,0},{2,3},{3,2},{4,5},{5,4},{6,7},{7,6},{8,9},{9,8},{10,11... | collective-permute-start | bytes 1966088 | tf_op jit(solution)/shard_map/ppermute | solution.py:327
Sparse Core Ops, SparseCore 0:
  10.1 100.7 all-gather.2
